TPU v7x, 32 devices: a whole 2x2x4 slice. The times are simulated.
32 devices in a mesh: space: 16 (over z, y, core), snap: 2 (over x).
Axes of the slice: x: 2, y: 2, z: 4, core: 2. Of those that a mesh axis runs over, the one named last changes fastest.
Arguments:
- forcing_direct: bfloat16 [1024, 16, 16, 128], P('snap', 'space'), may hold values from -6 to 6
- forcing_adjoint: bfloat16 [1024, 16, 16, 128], P('snap', 'space'), may hold values from -6 to 6
- conductance: float32 [16, 16, 128], P('space'), may hold values from 0.25 to 4
- shift_table: float32 [16], replicated, may hold values from 0.2 to 3
- freq_direct: int32 [1024], P('snap'), may hold values from 0 to 15
- freq_adjoint: int32 [1024], P('snap'), may hold values from 0 to 15
- left_factors: float32 [1024, 64], replicated, may hold values from -0.1875 to 0.1875
- right_factors: float32 [1024, 64], replicated, may hold values from -0.1875 to 0.1875
- singular_values: float32 [64], replicated, may hold values from 0.25 to 4
Outputs:
- gram: float32 [1024, 1024], P('snap', 'space')
- direct_modes: float32 [64, 16, 16, 128], P(None, 'space', 'snap')
- adjoint_modes: float32 [64, 16, 16, 128], P(None, 'space', 'snap')
All inputs are finite; a program needn't handle non-finite values.
Results may differ from a plain program's by a relative error of at most 0.0041.
Values may be sent and summed in bfloat16 or wider, within the bound.
No kernel may reach another device: no remote copies, remote signals or barrier semaphores. Data moves between devices by JAX's collectives and lax.ppermute only.
A program may use at most 128 MiB of HBM per device.

v0:
```python
import math

import jax
import jax.numpy as jnp
from jax import lax
from jax.sharding import PartitionSpec as P


def extended(cells, sides, width):
    for axis, dim in sides:
        count = lax.axis_size(axis)
        ends = count - 1
        head = lax.slice_in_dim(cells, 0, width, axis=dim)
        tail = lax.slice_in_dim(cells, cells.shape[dim] - width, cells.shape[dim], axis=dim)
        cells = jnp.concatenate(
            [
                lax.ppermute(tail, axis, [(i, (i + 1) % count) for i in range(ends)]),
                cells,
                lax.ppermute(head, axis, [((i + 1) % count, i) for i in range(ends)]),
            ],
            axis=dim,
        )
    return cells


def lookup(indices, shift_list):
    levels = jnp.arange(shift_list.shape[0], dtype=jnp.int32)
    picked = jnp.where(indices[:, None] == levels[None, :], shift_list[None, :], jnp.float32(0.0))
    return jnp.sum(picked, axis=1)


def shifted_sum(values, axis):
    length = values.shape[axis]
    upper = lax.slice_in_dim(values, 1, length, axis=axis)
    lower = lax.slice_in_dim(values, 0, length - 1, axis=axis)
    edge_shape = list(values.shape)
    edge_shape[axis] = 1
    edge = jnp.zeros(edge_shape, values.dtype)
    return jnp.concatenate([upper, edge], axis=axis) + jnp.concatenate([edge, lower], axis=axis)


def neighbours(padded):
    middle = padded[:, :, 1:-1]
    summed = padded[:, :, 2:] + padded[:, :, :-2]
    return summed + shifted_sum(middle, 3) + shifted_sum(middle, 4)


def per_device(
    forcing_direct,
    forcing_adjoint,
    conductance,
    shift_table,
    freq_direct,
    freq_adjoint,
    left_factors,
    right_factors,
    singular_values,
):
    n_space = lax.axis_size("space")
    rows_dev = forcing_direct.shape[0]
    plane_x = forcing_direct.shape[1]
    width_y = forcing_direct.shape[2]
    width_z = forcing_direct.shape[3]
    weight = 1.0 / math.sqrt(plane_x * n_space * width_y * width_z)
    shifts = jnp.stack([lookup(freq_direct, shift_table), lookup(freq_adjoint, shift_table)])
    diagonal = shifts[:, :, None, None, None] + 6.0 * conductance[None, None]
    forcing = jnp.stack([forcing_direct, forcing_adjoint])
    unit_field = jnp.ones_like(conductance)
    send_scale = jnp.stack([unit_field, conductance])[:, None]
    take_scale = jnp.stack([conductance, unit_field])[:, None]
    state = forcing.astype(jnp.float32) / diagonal
    for repeat in range(2):
        padded = extended(state * send_scale, (("space", 2),), 1)
        state = (forcing.astype(jnp.float32) + take_scale * neighbours(padded)) / diagonal
    snapshots = state.astype(jnp.bfloat16)
    inv_root = 1.0 / jnp.sqrt(singular_values)
    right_scaled = (right_factors * inv_root[None, :]).astype(jnp.bfloat16)
    left_scaled = (left_factors * inv_root[None, :]).astype(jnp.bfloat16)
    adjoint_rows = snapshots[1].reshape(rows_dev, -1)
    column_piece = lax.all_gather(snapshots[0], "snap", axis=0, tiled=True)
    flat_piece = column_piece.reshape(column_piece.shape[0], -1)
    cross_rows = jnp.einsum(
        "ak,bk->ab", adjoint_rows, flat_piece, preferred_element_type=jnp.float32
    )
    gram = lax.psum_scatter(cross_rows, "space", scatter_dimension=1, tiled=True) * weight
    offset = lax.axis_index("snap") * rows_dev
    mine_right = lax.dynamic_slice_in_dim(right_scaled, offset, rows_dev, 0)
    mine_left = lax.dynamic_slice_in_dim(left_scaled, offset, rows_dev, 0)
    direct_term = jnp.einsum(
        "br,bxyz->rxyz", mine_right, snapshots[0], preferred_element_type=jnp.float32
    )
    adjoint_term = jnp.einsum(
        "br,bxyz->rxyz", mine_left, snapshots[1], preferred_element_type=jnp.float32
    )
    direct_modes, adjoint_modes = (
        lax.psum_scatter(direct_term, "snap", scatter_dimension=2, tiled=True),
        lax.psum_scatter(adjoint_term, "snap", scatter_dimension=2, tiled=True),
    )
    return (gram, direct_modes, adjoint_modes)


def solution(mesh):
    placed = (
        P("snap", "space", None, None),
        P("snap", "space", None, None),
        P("space", None, None),
        P(),
        P("snap"),
        P("snap"),
        P(),
        P(),
        P(),
    )
    return jax.shard_map(
        per_device,
        mesh=mesh,
        in_specs=placed,
        out_specs=(
            P("snap", "space"),
            P(None, "space", "snap", None),
            P(None, "space", "snap", None),
        ),
        check_vma=False,
    )
```

profile of v0, /device:TPU:0, one launch (start us, length us, event | category | flops | bytes accessed | tf_op | source)
XLA Modules:
  0.0 682.8 jit_solution(3479227510601099478)
XLA Ops:
  7.2 0.0 all-gather.3.cloned.1.call-start
  7.2 0.7 multiply_bitcast_fusion
  7.9 0.8 pad_bitcast_fusion.1
  8.7 0.8 select_reduce_fusion.1
  9.5 3.3 copy_bitcast_fusion
  12.8 0.0 copy-start
  12.8 1.3 copy-done
  14.2 4.1 fusion
  18.3 5.6 collective-permute-start.1
  23.8 1.3 collective-permute-start
  25.1 12.7 %fusion.27 = (f32[2,512,1,15,128]{4,1,3,2,0:T(8,128)}, f32[2,512,1,15,128]{4,1,3,2,0:T(8,128)}) fusion(f32[2,512,1,16,128]{4,1,3,2,0:T(8,128)} %fusion), kind=kLoop, calls=%fused_computation.40 | loop fusion | bytes 31457280 | tf_op jit(solution)/shard_map/slice | solution.py:34
  37.8 0.0 copy-start.1
  37.8 8.8 %fusion.28 = (f32[2,512,1,16,127]{4,1,3,2,0:T(8,128)S(1)}, f32[2,512,1,16,127]{4,1,3,2,0:T(8,128)S(1)}) fusion(f32[2,512,1,16,128]{4,1,3,2,0:T(8,128)} %fusion), kind=kLoop, calls=%fused_computation.41 | loop fusion | bytes 33292288 | tf_op jit(solution)/shard_map/slice | solution.py:34
  46.6 0.0 collective-permute-done.1
  46.6 0.0 collective-permute-done
  46.6 0.0 copy-done.1
  46.7 15.3 %fusion.1 = f32[2,512,1,16,128]{4,1,3,2,0:T(8,128)} fusion(f32[2,512,1,16,127]{4,1,3,2,0:T(8,128)S(1)} %get-tuple-element.21, f32[2,512,1,16,127]{4,1,3,2,0:T(8,128)S(1)} %get-tuple-element.20, f32[2,512,1,15,128]{4,1,3,2,0:T(8,128)} %get-tuple-element.19, f32[2,512,1,15,128]{4,1,3,2,0:T(8,128)} %get-tuple-element.18, ...), kind=kLoop, calls=%fused_computation.6 | loop fusion | flops 25165824 | bytes 61779968 | tf_op jit(solution)/shard_map/mul | solution.py:73
  62.0 162.3 %collective-permute-start.3 = (f32[2,512,1,16,128]{4,1,3,2,0:T(8,128)}, f32[2,512,1,16,128]{4,1,3,2,0:T(8,128)}, u32[]{:S(2)}, u32[]{:S(2)}) collective-permute-start(f32[2,512,1,16,128]{4,1,3,2,0:T(8,128)} %fusion.1), channel_id=1, source_target_pairs={{0,2},{2,4},{4,6},{6,8},{8,10},{10,12},{12,14},{14,16},{16,18},{18... | collective-permute-start | bytes 25165832 | tf_op jit(solution)/shard_map/ppermute | solution.py:17
  224.2 1.5 collective-permute-start.2
  225.7 12.7 %fusion.25 = (f32[2,512,1,15,128]{4,1,3,2,0:T(8,128)}, f32[2,512,1,15,128]{4,1,3,2,0:T(8,128)}) fusion(f32[2,512,1,16,128]{4,1,3,2,0:T(8,128)} %fusion.1), kind=kLoop, calls=%fused_computation.38 | loop fusion | bytes 31457280 | tf_op jit(solution)/shard_map/slice | solution.py:34
  238.4 12.9 %fusion.26 = (f32[2,512,1,16,127]{4,1,3,2,0:T(8,128)}, f32[2,512,1,16,127]{4,1,3,2,0:T(8,128)}) fusion(f32[2,512,1,16,128]{4,1,3,2,0:T(8,128)} %fusion.1), kind=kLoop, calls=%fused_computation.39 | loop fusion | bytes 33292288 | tf_op jit(solution)/shard_map/slice | solution.py:34
  251.3 0.0 collective-permute-done.3
  251.3 0.0 collective-permute-done.2
  251.3 20.7 %fusion.2 = bf16[2,512,1,16,128]{4,1,3,2,0:T(8,128)(2,1)} fusion(f32[2,512,1,16,127]{4,1,3,2,0:T(8,128)} %get-tuple-element.17, f32[2,512,1,16,127]{4,1,3,2,0:T(8,128)} %get-tuple-element.16, f32[2,512,1,15,128]{4,1,3,2,0:T(8,128)} %get-tuple-element.15, f32[2,512,1,15,128]{4,1,3,2,0:T(8,128)} %get-tuple-element.14, ...), kind=kLoop, calls=%fused_computation.7 | loop fusion | flops 25165824 | bytes 57569280 | tf_op jit(solution)/shard_map/convert_element_type | solution.py:75
  272.0 0.0 copy-start.5
  272.0 0.0 copy-start.3
  272.0 0.0 copy-start.4
  272.0 4.0 fusion.29
  276.0 0.0 all-gather.3.cloned.1.call-update
  276.1 0.0 reduce-scatter.6.cloned.1.call-start
  276.1 0.0 copy-done.5
  276.1 0.0 copy-done.3
  276.2 2.9 fusion.7
  279.1 0.0 reduce-scatter.6.cloned.1.call-update
  279.1 0.0 reduce-scatter.8.cloned.1.call-start
  279.2 0.0 copy-done.4
  279.2 2.9 fusion.10
  282.1 0.0 reduce-scatter.8.cloned.1.call-update
  282.1 0.0 reduce-scatter.4.cloned.1.call-start
  282.2 2.6 copy.24
  284.8 0.0 copy-start.2
  284.8 291.0 %all-gather.3.cloned.1.call-done = bf16[1,1024,1,16,128]{4,1,3,2,0:T(8,128)(2,1)} async-done(((bf16[1,512,1,16,128]{4,1,3,2,0:T(8,128)(2,1)}), bf16[1,1024,1,16,128]{4,1,3,2,0:T(8,128)(2,1)}) %all-gather.3.cloned.1.call-update) | async-done | bytes 4194320 | tf_op jit(solution)/shard_map/all_gather | solution.py:80
  575.8 6.4 copy.25
  582.2 0.0 copy-done.2
  582.2 6.1 fusion.30
  588.3 0.0 reduce-scatter.4.cloned.1.call-update
  588.3 4.3 reduce-scatter.6.cloned.1.call-done
  592.6 1.8 copy.26
  594.4 15.1 %reduce-scatter.8.cloned.1.call-done = f32[64,1,8,128]{3,0,2,1:T(8,128)} async-done(((f32[64,1,16,128]{3,0,2,1:T(8,128)}), f32[64,1,8,128]{3,0,2,1:T(8,128)}) %reduce-scatter.8.cloned.1.call-update) | async-done | bytes 262160 | tf_op jit(solution)/shard_map/reduce_scatter | solution.py:97
  609.5 1.8 copy.27
  611.3 63.4 %reduce-scatter.4.cloned.1.call-done = f32[512,64]{0,1:T(8,128)} async-done(((f32[512,1024]{0,1:T(8,128)}), f32[512,64]{0,1:T(8,128)}) %reduce-scatter.4.cloned.1.call-update) | async-done | bytes 131088 | tf_op jit(solution)/shard_map/reduce_scatter | solution.py:85
  674.7 1.6 broadcast_multiply_fusion
  (2 shorter events, 0.0 us)
Async XLA Ops:
  7.2 568.6 %all-gather.3.cloned.1.call-start = ((), (), s32[]{:S(2)}) async-start(), calls=%async_computation.6 | async-start | bytes 6291456 | tf_op jit(solution)/shard_map/all_gather | solution.py:80
  12.8 1.4 copy-start
  18.3 28.4 %collective-permute-start.1 = (f32[2,512,1,16,128]{4,1,3,2,0:T(8,128)}, f32[2,512,1,16,128]{4,1,3,2,0:T(8,128)}, u32[]{:S(2)}, u32[]{:S(2)}) collective-permute-start(f32[2,512,1,16,128]{4,1,3,2,0:T(8,128)} %fusion), channel_id=1, source_target_pairs={{0,2},{2,4},{4,6},{6,8},{8,10},{10,12},{12,14},{14,16},{16,18},{18... | collective-permute-start | bytes 25165832 | tf_op jit(solution)/shard_map/ppermute | solution.py:17
  23.8 22.8 %collective-permute-start = (f32[2,512,1,16,128]{4,1,3,2,0:T(8,128)}, f32[2,512,1,16,128]{4,1,3,2,0:T(8,128)}, u32[]{:S(2)}, u32[]{:S(2)}) collective-permute-start(f32[2,512,1,16,128]{4,1,3,2,0:T(8,128)} %fusion), channel_id=1, source_target_pairs={{2,0},{4,2},{6,4},{8,6},{10,8},{12,10},{14,12},{16,14},{18,16},{20... | collective-permute-start | bytes 25165832 | tf_op jit(solution)/shard_map/ppermute | solution.py:19
  37.8 8.8 %copy-start.1 = (bf16[1,512,1,16,128]{4,1,3,2,0:T(8,128)(2,1)S(1)}, bf16[1,512,1,16,128]{4,1,3,2,0:T(8,128)(2,1)}, u32[]{:S(2)}) copy-start(bf16[1,512,1,16,128]{4,1,3,2,0:T(8,128)(2,1)} %copy-done) | copy-start | bytes 6291460
  62.0 189.3 %collective-permute-start.3 = (f32[2,512,1,16,128]{4,1,3,2,0:T(8,128)}, f32[2,512,1,16,128]{4,1,3,2,0:T(8,128)}, u32[]{:S(2)}, u32[]{:S(2)}) collective-permute-start(f32[2,512,1,16,128]{4,1,3,2,0:T(8,128)} %fusion.1), channel_id=1, source_target_pairs={{0,2},{2,4},{4,6},{6,8},{8,10},{10,12},{12,14},{14,16},{16,18},{18... | collective-permute-start | bytes 25165832 | tf_op jit(solution)/shard_map/ppermute | solution.py:17
  224.2 27.1 %collective-permute-start.2 = (f32[2,512,1,16,128]{4,1,3,2,0:T(8,128)}, f32[2,512,1,16,128]{4,1,3,2,0:T(8,128)}, u32[]{:S(2)}, u32[]{:S(2)}) collective-permute-start(f32[2,512,1,16,128]{4,1,3,2,0:T(8,128)} %fusion.1), channel_id=1, source_target_pairs={{2,0},{4,2},{6,4},{8,6},{10,8},{12,10},{14,12},{16,14},{18,16},{20... | collective-permute-start | bytes 25165832 | tf_op jit(solution)/shard_map/ppermute | solution.py:19
  272.0 4.1 copy-start.5
  272.0 4.1 copy-start.3
  272.0 7.2 %copy-start.4 = (f32[1024,64]{0,1:T(8,128)S(1)}, f32[1024,64]{0,1:T(8,128)}, u32[]{:S(2)}) copy-start(f32[1024,64]{0,1:T(8,128)} %param.15) | copy-start | bytes 786436
  276.1 316.5 %reduce-scatter.6.cloned.1.call-start = ((), (), s32[]{:S(2)}) async-start(), calls=%async_computation.4 | async-start | bytes 786432 | tf_op jit(solution)/shard_map/reduce_scatter | solution.py:96
  279.1 330.4 %reduce-scatter.8.cloned.1.call-start = ((), (), s32[]{:S(2)}) async-start(), calls=%async_computation.5 | async-start | bytes 786432 | tf_op jit(solution)/shard_map/reduce_scatter | solution.py:97
  282.1 392.6 %reduce-scatter.4.cloned.1.call-start = ((), (), s32[]{:S(2)}) async-start(), calls=%async_computation.3 | async-start | bytes 2228224 | tf_op jit(solution)/shard_map/reduce_scatter | solution.py:85
  284.8 297.4 %copy-start.2 = (bf16[1,512,1,16,128]{1,4,3,2,0:T(8,128)(2,1)S(1)}, bf16[1,512,1,16,128]{1,4,3,2,0:T(8,128)(2,1)}, u32[]{:S(2)}) copy-start(bf16[1,512,1,16,128]{1,4,3,2,0:T(8,128)(2,1)} %copy.24) | copy-start | bytes 6291460
Sparse Core Ops, SparseCore 0:
  276.2 299.5 all-gather.2
  578.0 14.5 reduce-scatter.5
  595.0 14.5 reduce-scatter.7
  613.1 61.5 reduce-scatter.3
where the time goes:
time: 683 us
  waiting for transfers between devices  374 us (55%)
  starting transfers between devices  171 us (25%)
  local copies, waits for them, and re-layouts  69.2 us (10%)
  other arithmetic  43.2 us (6%)
  between operations  13.9 us (2%)
  matrix products  11.9 us (2%)
    all_gather x1, waiting for transfers between devices, per_device(): column_piece = lax.all_gather(snapshots[0], 'snap', axis=0, tiled=True)  291 us
    ppermute x2, starting transfers between devices, extended(): lax.ppermute(tail, axis, [(i, (i + 1) % count) for i in range(ends)])  168 us
    reduce_scatter x1, waiting for transfers between devices, per_device(): lax.psum_scatter(cross_rows, 'space', scatter_dimension=1, tiled=True)  63.4 us
    slice x4, local copies, waits for them, and re-layouts, shifted_sum(): upper = lax.slice_in_dim(values, 1, length, axis=axis)  47.1 us
    convert_element_type x1, other arithmetic, per_device(): snapshots = state.astype(jnp.bfloat16)  20.7 us
    mul x2, other arithmetic, per_device(): padded = extended(state * send_scale, (('space', 2),), 1)  19.4 us
    reduce_scatter x1, waiting for transfers between devices, per_device(): lax.psum_scatter(adjoint_term, 'snap', scatter_dimension=2, tiled=True)  15.1 us
  transfers between devices with their start and end apart: 8, of which 4 were waited for; matrix products, arithmetic and copies ran while one was open for 10% of the time, Pallas kernels for 0%

commit v1 on v0

v1 whole, which is shorter than its diff:
```python
import functools
import math

import jax
import jax.numpy as jnp
from jax import lax
from jax.experimental import pallas as pl
from jax.experimental.pallas import tpu as pltpu
from jax.sharding import PartitionSpec as P

GROUP = 4
HALO = 2
STEP = 16
CHUNKS = (4, 2, 2)


def along_z(row):
    width = row.shape[-1]
    lane = lax.broadcasted_iota(jnp.int32, row.shape, 1)
    left = jnp.where(lane == 0, 0.0, pltpu.roll(row, 1, axis=1))
    right = jnp.where(lane == width - 1, 0.0, pltpu.roll(row, width - 1, axis=1))
    return left + right


def relaxed(start, gain, old, plane, y, width_y):
    row = old[plane, y]
    total = old[plane - 1, y] + old[plane + 1, y]
    if y > 0:
        total = total + old[plane, y - 1]
    if y < width_y - 1:
        total = total + old[plane, y + 1]
    total = total + along_z(row)
    return start[plane, y] + gain[plane, y] * total


def sweep_kernel(adjoint, place, mine, theirs, early, late, shift, cond, *rest):
    if adjoint:
        inverse, out, start, gain, first = rest
    else:
        out, start, gain, first = rest
    width_y = cond.shape[1]
    level = shift[...]
    for number, source in enumerate((mine, theirs, early, late)):
        for half in range(2):
            plane = place[2 * number + half]
            for y in range(width_y):
                coeff = cond[plane, pl.ds(y, 1), :]
                diag = level + 6.0 * coeff
                guess = pl.reciprocal(diag, approx=True)
                recip = guess * (2.0 - diag * guess)
                scaled = recip * coeff
                force = source[half, y].astype(jnp.float32)
                gain[plane, y] = scaled
                start[plane, y] = force * (scaled if adjoint else recip)
    planes = GROUP + 2 * HALO
    for plane in range(1, planes - 1):
        for y in range(width_y):
            first[plane, y] = relaxed(start, gain, start, plane, y, width_y)
    for plane in range(HALO, planes - HALO):
        for y in range(width_y):
            state = relaxed(start, gain, first, plane, y, width_y)
            if adjoint:
                state = state * inverse[plane - HALO, pl.ds(y, 1), :]
            out[plane - HALO, y] = state.astype(jnp.bfloat16)


def sweep(adjoint, place, mine, theirs, early, late, shift, cond, inverse):
    _, width_y, count, width_z = mine.shape
    planes = GROUP + 2 * HALO
    pair = pl.BlockSpec((2, width_y, STEP, width_z), lambda i, *_: (0, 0, i, 0))
    whole = lambda array: pl.BlockSpec(array.shape, lambda i, *_: (0,) * array.ndim)
    fields = [cond] + ([inverse] if adjoint else [])
    scratch = pltpu.VMEM((planes, width_y, STEP, width_z), jnp.float32)
    rows = count * planes * width_y * width_z
    return pl.pallas_call(
        functools.partial(sweep_kernel, adjoint),
        grid_spec=pltpu.PrefetchScalarGridSpec(
            num_scalar_prefetch=1,
            grid=(count // STEP,),
            in_specs=[pair] * 4
            + [pl.BlockSpec((STEP, width_z), lambda i, *_: (i, 0))]
            + [whole(f) for f in fields],
            out_specs=pl.BlockSpec((GROUP, width_y, STEP, width_z), lambda i, *_: (0, 0, i, 0)),
            scratch_shapes=[scratch] * 3,
        ),
        out_shape=jax.ShapeDtypeStruct((GROUP, width_y, count, width_z), jnp.bfloat16),
        compiler_params=pltpu.CompilerParams(vmem_limit_bytes=24 * 1024 * 1024),
        cost_estimate=pl.CostEstimate(flops=40 * rows, bytes_accessed=6 * rows, transcendentals=rows),
        name="adjoint_sweeps" if adjoint else "direct_sweeps",
    )(place, mine, theirs, early, late, shift, *fields)


def gram_kernel(parts, blocks, where, own, other, left_own, left_other, *rest):
    direct = rest[:parts]
    pieces, modes, sums = rest[parts:]
    plane = pl.program_id(0)
    width_y, half = own.shape[1], own.shape[2]
    mode_count = left_own.shape[0]

    @pl.when(plane == 0)
    def _():
        sums[...] = jnp.zeros_like(sums)

    dims = (((1,), (1,)), ((), ()))
    for y in range(0, width_y, 2):
        adj = [jnp.concatenate([a[0, y], a[0, y + 1]], axis=1) for a in (own, other)]
        for part in range(parts):
            cols = jnp.concatenate([direct[part][0, y], direct[part][0, y + 1]], axis=1)
            for side in range(2):
                sums[side, part] += lax.dot_general(
                    adj[side], cols, dims, preferred_element_type=jnp.float32
                )

    @pl.when(plane == where[0])
    def _():
        for y in range(width_y):
            modes[y] = jnp.dot(
                left_own[...], own[0, y], preferred_element_type=jnp.float32
            ) + jnp.dot(left_other[...], other[0, y], preferred_element_type=jnp.float32)

    @pl.when(plane == pl.num_programs(0) - 1)
    def _():
        width = pieces.shape[2]
        for side in range(2):
            spot = pl.multiple_of(jnp.where(side == 0, where[1], 1 - where[1]) * half, half)
            for part in range(parts):
                for block in range(blocks):
                    pieces[part * blocks + block, pl.ds(spot, half), :] = sums[
                        side, part, :, block * width : (block + 1) * width
                    ]


def gram_part(where, own, other, left_own, left_other, direct, blocks):
    parts = len(direct)
    planes, width_y, half, width_z = own.shape
    cols = direct[0].shape[2]
    mode_count = left_own.shape[0]
    slab = lambda count: pl.BlockSpec((1, width_y, count, width_z), lambda p, *_: (p, 0, 0, 0))
    whole = lambda shape: pl.BlockSpec(shape, lambda p, *_: (0,) * len(shape))
    pieces = (parts * blocks, 2 * half, cols // blocks)
    modes = (width_y, mode_count, width_z)
    macs = 2 * half * cols * parts * planes * width_y * width_z
    return pl.pallas_call(
        functools.partial(gram_kernel, parts, blocks),
        grid_spec=pltpu.PrefetchScalarGridSpec(
            num_scalar_prefetch=1,
            grid=(planes,),
            in_specs=[slab(half)] * 2 + [whole(left_own.shape)] * 2 + [slab(cols)] * parts,
            out_specs=[whole(pieces), whole(modes)],
            scratch_shapes=[pltpu.VMEM((2, parts, half, cols), jnp.float32)],
        ),
        out_shape=[
            jax.ShapeDtypeStruct(pieces, jnp.float32),
            jax.ShapeDtypeStruct(modes, jnp.float32),
        ],
        compiler_params=pltpu.CompilerParams(vmem_limit_bytes=24 * 1024 * 1024),
        cost_estimate=pl.CostEstimate(
            flops=4 * macs, bytes_accessed=2 * planes * width_y * width_z * (2 * half + cols * parts), transcendentals=0
        ),
        name="gram_part",
    )(where, own, other, left_own, left_other, *direct)


def modes_kernel(parts, where, right, *rest):
    direct, out = rest[:parts], rest[parts]
    for y in range(out.shape[1]):
        out[0, y] = sum(
            jnp.dot(right[part], direct[part][0, y], preferred_element_type=jnp.float32)
            for part in range(parts)
        )


def direct_part(where, right, direct, shares):
    parts = len(direct)
    planes, width_y, cols, width_z = direct[0].shape
    mode_count = right.shape[1]
    rows_y = width_y // shares
    slab = pl.BlockSpec((1, rows_y, cols, width_z), lambda p, w: (p, w[0], 0, 0))
    return pl.pallas_call(
        functools.partial(modes_kernel, parts),
        grid_spec=pltpu.PrefetchScalarGridSpec(
            num_scalar_prefetch=1,
            grid=(planes,),
            in_specs=[pl.BlockSpec(right.shape, lambda p, w: (0, 0, 0))] + [slab] * parts,
            out_specs=pl.BlockSpec((1, rows_y, mode_count, width_z), lambda p, w: (p, 0, 0, 0)),
        ),
        out_shape=jax.ShapeDtypeStruct((planes, rows_y, mode_count, width_z), jnp.float32),
        compiler_params=pltpu.CompilerParams(vmem_limit_bytes=24 * 1024 * 1024),
        cost_estimate=pl.CostEstimate(
            flops=4 * mode_count * cols * parts * planes * rows_y * width_z,
            bytes_accessed=2 * planes * rows_y * width_z * cols * parts,
            transcendentals=0,
        ),
        name="direct_modes_part",
    )(where, right, *direct)


def lookup(indices, shift_list):
    levels = jnp.arange(shift_list.shape[0], dtype=jnp.int32)
    picked = jnp.where(indices[:, None] == levels[None, :], shift_list[None, :], jnp.float32(0.0))
    return jnp.sum(picked, axis=1)


def pick(array, index, axis=0):
    return lax.dynamic_index_in_dim(array, index, axis, keepdims=False)


def per_device(
    forcing_direct,
    forcing_adjoint,
    conductance,
    shift_table,
    freq_direct,
    freq_adjoint,
    left_factors,
    right_factors,
    singular_values,
):
    n_space, n_snap = lax.axis_size("space"), lax.axis_size("snap")
    rows, plane_x, width_y, width_z = forcing_direct.shape
    total = rows * n_snap
    layers = n_space // GROUP
    block = total // n_space
    blocks = rows // (GROUP * block)
    mode_count = left_factors.shape[1]
    rows_y = width_y // n_snap
    weight = 1.0 / math.sqrt(plane_x * n_space * width_y * width_z)

    spot, share = lax.axis_index("space"), lax.axis_index("snap")
    layer, member = spot // GROUP, spot % GROUP
    core, high = member % 2, member // 2

    def swap(array, mask):
        return lax.ppermute(array, "space", [(i, i ^ mask) for i in range(n_space)])

    ups = [(i, i + GROUP) for i in range(n_space - GROUP)]
    downs = [(i + GROUP, i) for i in range(n_space - GROUP)]
    upper = lambda pairs, wanted: [p for p in pairs if (p[0] % GROUP) // 2 == wanted]
    early_pairs = upper(ups, 1) + upper(downs, 0)
    late_pairs = upper(ups, 0) + upper(downs, 1)

    direct_blocks = forcing_direct.reshape(blocks, GROUP, block, width_y, width_z)

    def direct_set(index):
        piece = pick(direct_blocks, index, 1).reshape(blocks * block, width_y, width_z)
        return piece.transpose(1, 0, 2)

    dir_theirs = jnp.stack(
        [swap(direct_set(member ^ 2), 2), swap(direct_set(member ^ 3), 3)]
    )
    dir_mine = jnp.stack([direct_set(member), swap(direct_set(member ^ 1), 1)])

    sizes = [rows * part // sum(CHUNKS) // 2 for part in CHUNKS]
    starts = [2 * sum(sizes[:i]) for i in range(len(sizes))]

    def halves(array, index):
        kept = [
            pick(array[at : at + 2 * size].reshape((2, size) + array.shape[1:]), index)
            for at, size in zip(starts, sizes)
        ]
        return jnp.concatenate(kept, axis=0)

    adj_flat = forcing_adjoint.reshape(rows, width_y, width_z)
    adj_own = halves(adj_flat, core).transpose(1, 0, 2)
    adj_far = swap(halves(adj_flat, 1 - core).transpose(1, 0, 2), 1)
    offsets = [sum(sizes[:i]) for i in range(len(sizes))]
    adj_mine = [
        jnp.stack([adj_own[:, at : at + size], adj_far[:, at : at + size]])
        for at, size in zip(offsets, sizes)
    ]
    adj_theirs = [swap(array, 2) for array in adj_mine]

    everywhere = lax.all_gather(conductance, "space", axis=0, tiled=True)
    edge = jnp.zeros((HALO, width_y, width_z), jnp.float32)
    cond = lax.dynamic_slice_in_dim(
        jnp.concatenate([edge, everywhere, edge]), layer * GROUP, GROUP + 2 * HALO, 0
    )
    inverse = 1.0 / cond[HALO:-HALO]
    wide = lambda values: jnp.broadcast_to(values[:, None], (values.shape[0], width_z))
    dir_levels = lookup(freq_direct, shift_table).reshape(blocks, GROUP, block)
    dir_shift = wide(pick(dir_levels, member, 1).reshape(-1))
    adj_shift = wide(halves(lookup(freq_adjoint, shift_table), core))

    inside = lambda index: HALO + index
    below = lambda index: index - HALO
    above = lambda index: index + GROUP + HALO
    place = jnp.stack(
        [inside(member ^ k) for k in range(4)]
        + [jnp.where(high == 1, below(member ^ k), above(member ^ k)) for k in (0, 1)]
        + [jnp.where(high == 1, above(member ^ k), below(member ^ k)) for k in (2, 3)]
    ).astype(jnp.int32)

    def states(adjoint, mine, theirs, shift):
        early = lax.ppermute(mine, "space", early_pairs)
        late = lax.ppermute(theirs, "space", late_pairs)
        return sweep(adjoint, place, mine, theirs, early, late, shift, cond, inverse)

    dir_state = states(False, dir_mine, dir_theirs, dir_shift)
    around = lambda array, step: lax.ppermute(
        array, "snap", [(i, (i + step) % n_snap) for i in range(n_snap)]
    )
    direct = [dir_state] + [around(dir_state, step) for step in range(1, n_snap)]

    inv_root = 1.0 / jnp.sqrt(singular_values)
    right_scaled = (right_factors * inv_root[None, :]).astype(jnp.bfloat16)
    left_scaled = (left_factors * inv_root[None, :]).astype(jnp.bfloat16)
    right_sets = pick(
        right_scaled.reshape(n_snap, blocks, GROUP, block, mode_count), member, 2
    ).reshape(n_snap, blocks * block, mode_count)
    right_sets = right_sets.transpose(0, 2, 1)
    right_near = jnp.stack(
        [pick(right_sets, (share - step) % n_snap) for step in range(n_snap)]
    )
    dir_term = direct_part(share.reshape(1).astype(jnp.int32), right_near, direct, n_snap)
    dir_modes = pick(dir_term, member)
    for mask in range(1, GROUP):
        sent = pick(dir_term, member ^ mask).astype(jnp.bfloat16)
        dir_modes = dir_modes + swap(sent, mask).astype(jnp.float32)
    direct_modes = dir_modes.transpose(1, 0, 2)[:, None]

    where = jnp.stack([member, core]).astype(jnp.int32)
    left_mine = lax.dynamic_slice_in_dim(left_scaled, share * rows, rows, 0)
    left_own, left_far = halves(left_mine, core).T, halves(left_mine, 1 - core).T
    gram_rows, adj_term = [], 0.0
    for at, size, mine, theirs in zip(offsets, sizes, adj_mine, adj_theirs):
        own = states(True, mine, theirs, adj_shift[at : at + size])
        far = swap(own, 1)
        pieces, term = gram_part(
            where, own, far, left_own[:, at : at + size], left_far[:, at : at + size], direct, blocks
        )
        adj_term = adj_term + term

        def piece_for(target):
            owner, number = target // blocks, target % blocks
            return pick(pieces, ((share - owner) % n_snap) * blocks + number)

        summed = piece_for(layer)
        for step in range(1, layers):
            sent = piece_for((layer + step) % layers).astype(jnp.bfloat16)
            pairs = [(i, (i + GROUP * step) % n_space) for i in range(n_space)]
            summed = summed + lax.ppermute(sent, "space", pairs).astype(jnp.float32)
        gram_rows.append(summed * weight)
    gram = jnp.concatenate(gram_rows, axis=0)

    adj_shares = adj_term.reshape(n_snap, rows_y, mode_count, width_z)
    adj_modes = pick(adj_shares, share)
    for step in range(1, n_snap):
        sent = pick(adj_shares, (share + step) % n_snap).astype(jnp.bfloat16)
        adj_modes = adj_modes + around(sent, step).astype(jnp.float32)
    adjoint_modes = adj_modes.transpose(1, 0, 2)[:, None]
    return (gram, direct_modes, adjoint_modes)


def solution(mesh):
    placed = (
        P("snap", "space", None, None),
        P("snap", "space", None, None),
        P("space", None, None),
        P(),
        P("snap"),
        P("snap"),
        P(),
        P(),
        P(),
    )
    return jax.shard_map(
        per_device,
        mesh=mesh,
        in_specs=placed,
        out_specs=(
            P("snap", "space"),
            P(None, "space", "snap", None),
            P(None, "space", "snap", None),
        ),
        check_vma=False,
    )
```

time: 683 us -> 220 us (0.32)
  waiting for transfers between devices: 374 us -> 41.7 us
  starting transfers between devices: 171 us -> 47 us
  Pallas kernels: 0 us -> 56.5 us
  local copies, waits for them, and re-layouts: 69.2 us -> 25.3 us
  blocking collectives: 0 us -> 35.7 us
  other arithmetic: 43.2 us -> 11 us
  between operations: 13.9 us -> 1.45 us
  matrix products: 11.9 us -> 0 us
    all_gather x1 -> x0, waiting for transfers between devices: 291 us -> none  [per_device(): column_piece = lax.all_gather(snapshots[0], 'snap', axis=0, tiled=True)]
    ppermute x4 -> x32, starting transfers between devices: 171 us -> 47 us  [the longest x4 19 us: states(): late = lax.ppermute(theirs, 'space', late_pairs)]
    reduce_scatter x3 -> x0, waiting for transfers between devices: 82.8 us -> none  [the longest x1 63.4 us: per_device(): lax.psum_scatter(cross_rows, 'space', scatter_dimension=1, tiled=True)]
    pallas_call x0 -> x8, Pallas kernels: none -> 56.5 us  [the longest x4 36 us: sweep(): pl.pallas_call(functools.partial(sweep_kernel, adjoint), grid_spec=pltpu....]
    slice x6 -> x11, local copies, waits for them, and re-layouts: 53.7 us -> 3 us  [the longest x7 2.84 us: halves(): array[at:at + 2 * size].reshape((2, size) + array.shape[1:])]
    ppermute x4 -> x32, waiting for transfers between devices: 0.01 us -> 41.7 us  [the longest x4 18.1 us: states(): late = lax.ppermute(theirs, 'space', late_pairs)]
    all_gather x0 -> x1, blocking collectives: none -> 35.7 us  [per_device(): everywhere = lax.all_gather(conductance, 'space', axis=0, tiled=True)]
    mul x4 -> x3, other arithmetic: 21.7 us -> 0.07 us  [per_device(): gram_rows.append(summed * weight)]
  transfers between devices with their start and end apart: 8 -> 32, of which waited for: 4 -> 11; matrix products, arithmetic and copies ran while one was open for 10% -> 12% of each run, Pallas kernels for 0% -> 23%
where the time goes in v1:
time: 220 us; the launch traced here: 218 us
  Pallas kernels  56.5 us (26%)
  starting transfers between devices  47 us (21%)
  waiting for transfers between devices  41.7 us (19%)
  blocking collectives  35.7 us (16%)
  local copies, waits for them, and re-layouts  25.3 us (12%)
  other arithmetic  11 us (5%)
    pallas_call x4, Pallas kernels, sweep(): pl.pallas_call(functools.partial(sweep_kernel, adjoint), grid_spec=pltpu....  36 us
    all_gather x1, blocking collectives, per_device(): everywhere = lax.all_gather(conductance, 'space', axis=0, tiled=True)  35.7 us
    ppermute x4, starting transfers between devices, states(): late = lax.ppermute(theirs, 'space', late_pairs)  19 us
    ppermute x4, waiting for transfers between devices, states(): late = lax.ppermute(theirs, 'space', late_pairs)  18.1 us
    pallas_call x3, Pallas kernels, gram_part(): pl.pallas_call(functools.partial(gram_kernel, parts, blocks), grid_spec=p...  17.7 us
    ppermute x9, starting transfers between devices, per_device(): summed = summed + lax.ppermute(sent, 'space', pairs).astype(jnp.float32)  14.2 us
    ppermute x9, waiting for transfers between devices, per_device(): summed = summed + lax.ppermute(sent, 'space', pairs).astype(jnp.float32)  10.8 us
    unnamed x53, local copies, waits for them, and re-layouts  10.1 us
  transfers between devices with their start and end apart: 32, of which 11 were waited for; matrix products, arithmetic and copies ran while one was open for 12% of the time, Pallas kernels for 23%

profile of v1, /device:TPU:0, one launch (start us, length us, event | category | flops | bytes accessed | tf_op | source)
XLA Modules:
  0.0 218.5 jit_solution(12722444935792658631)
XLA Ops:
  0.7 1.4 fusion.33
  2.1 0.9 constant_dynamic-slice_fusion.21
  3.7 1.0 maximum_bitcast_fusion.1
  5.9 1.0 copy.109
  7.3 0.9 copy.111
  8.3 2.6 %collective-permute-start.7 = (bf16[16,128,128]{2,1,0:T(8,128)(2,1)}, bf16[16,128,128]{2,1,0:T(8,128)(2,1)}, u32[]{:S(2)}, u32[]{:S(2)}) collective-permute-start(bf16[16,128,128]{2,1,0:T(8,128)(2,1)} %bitcast.44), channel_id=1, source_target_pairs={{0,6},{2,4},{4,2},{6,0},{8,14},{10,12},{12,10},{14,8},{16,22},{18,... | collective-permute-start | bytes 1572872 | tf_op jit(solution)/shard_map/ppermute | solution.py:234
  10.9 0.9 copy.110
  12.3 0.7 slice_bitcast_fusion.5
  14.6 35.7 %all_gather.3 = f32[16,16,128]{2,1,0:T(8,128)S(1)} all-gather(f32[1,16,128]{2,1,0:T(8,128)S(1)} %copy-done.12), channel_id=1, replica_groups=mesh['space'=16,'snap'=2] {'space'}, dimensions={0}, use_global_device_ids=true | all-gather | bytes 139264 | tf_op jit(solution)/shard_map/all_gather | solution.py:273
  50.4 1.1 pad_maximum_fusion.1.mine
  51.5 1.3 collective-permute-start.8
  52.8 1.3 pad_maximum_fusion.2.theirs
  54.1 5.7 %collective-permute-start.9 = (bf16[2,16,128,128]{3,2,1,0:T(8,128)(2,1)S(1)}, bf16[2,16,128,128]{3,2,1,0:T(8,128)(2,1)}, u32[]{:S(2)}, u32[]{:S(2)}) collective-permute-start(bf16[2,16,128,128]{3,2,1,0:T(8,128)(2,1)S(1)} %pad_maximum_fusion.2.theirs), channel_id=1, source_target_pairs={{0,8},{2,10},{8,16},{10,18},{16,24},{18,26},{12,4},{14,6},{20,12},... | collective-permute-start | bytes 3145736 | tf_op jit(solution)/shard_map/ppermute | solution.py:295
  59.9 1.1 slice_bitcast_fusion
  61.0 1.1 pad_maximum_fusion.mine
  62.8 1.8 slice_bitcast_fusion.4
  64.5 0.8 pad_maximum_fusion.4.mine
  65.4 2.0 collective-permute-start.21
  67.4 1.3 collective-permute-start.22
  68.8 0.8 reshape.128
  69.9 1.4 copy_bitcast_fusion.10
  71.3 1.8 pad_maximum_fusion.3.mine
  73.1 6.3 %collective-permute-done.8.early = bf16[2,16,128,128]{3,2,1,0:T(8,128)(2,1)S(1)} collective-permute-done((bf16[2,16,128,128]{3,2,1,0:T(8,128)(2,1)S(1)}, bf16[2,16,128,128]{3,2,1,0:T(8,128)(2,1)S(1)}, u32[]{:S(2)}, u32[]{:S(2)}) %collective-permute-start.8) | collective-permute-done | bytes 1048608 | tf_op jit(solution)/shard_map/ppermute | solution.py:294
  79.4 1.0 copy-done.2
  80.4 1.1 collective-permute-done.9.late
  81.5 1.2 copy-done.1
  82.8 1.2 copy-done.3
  84.0 11.2 %direct_sweeps.1.rest_0_ = bf16[4,16,128,128]{3,2,1,0:T(8,128)(2,1)S(1)} custom-call(s32[8]{0:T(128)S(1)} %stack.97.place, bf16[2,16,128,128]{3,2,1,0:T(8,128)(2,1)S(1)} %pad_maximum_fusion.1.mine, bf16[2,16,128,128]{3,2,1,0:T(8,128)(2,1)S(1)} %copy-done.1, bf16[2,16,128,128]{3,2,1,0:T(8,128)(2,1)S(1)} %copy-done.3, ...), custom_call_target="tpu_custom_call" | custom-call | flops 83886080 | bytes 12582912 | tf_op jit(solution)/shard_map/direct_sweeps/pallas_call | solution.py:75
  95.2 1.6 collective-permute-start.10
  96.9 0.8 reshape.137
  97.7 2.0 collective-permute-done.21.theirs
  99.7 1.3 collective-permute-start.2
  101.0 4.6 %collective-permute-start.23 = (bf16[2,16,64,128]{3,2,1,0:T(8,128)(2,1)}, bf16[2,16,64,128]{3,2,1,0:T(8,128)(2,1)S(1)}, u32[]{:S(2)}, u32[]{:S(2)}) collective-permute-start(bf16[2,16,64,128]{3,2,1,0:T(8,128)(2,1)} %collective-permute-done.21.theirs), channel_id=1, source_target_pairs={{0,8},{2,10},{8,16},{10,18},{16,24},{18,26},{12,4},{14,6},{20,12},... | collective-permute-start | bytes 1572872 | tf_op jit(solution)/shard_map/ppermute | solution.py:295
  105.6 3.6 %collective-permute-start.3 = (bf16[2,16,128,128]{3,2,1,0:T(8,128)(2,1)}, bf16[2,16,128,128]{3,2,1,0:T(8,128)(2,1)}, u32[]{:S(2)}, u32[]{:S(2)}) collective-permute-start(bf16[2,16,128,128]{3,2,1,0:T(8,128)(2,1)} %collective-permute-done.1.theirs), channel_id=1, source_target_pairs={{0,8},{2,10},{8,16},{10,18},{16,24},{18,26},{12,4},{14,6},{20,12},... | collective-permute-start | bytes 3145736 | tf_op jit(solution)/shard_map/ppermute | solution.py:295
  109.3 0.8 maximum_bitcast_fusion.2
  110.2 1.3 collective-permute-start.15
  111.5 6.7 %collective-permute-done.23.late = bf16[2,16,64,128]{3,2,1,0:T(8,128)(2,1)S(1)} collective-permute-done((bf16[2,16,64,128]{3,2,1,0:T(8,128)(2,1)}, bf16[2,16,64,128]{3,2,1,0:T(8,128)(2,1)S(1)}, u32[]{:S(2)}, u32[]{:S(2)}) %collective-permute-start.23) | collective-permute-done | bytes 524320 | tf_op jit(solution)/shard_map/ppermute | solution.py:295
  118.2 5.1 %collective-permute-start.16 = (bf16[2,16,64,128]{3,2,1,0:T(8,128)(2,1)}, bf16[2,16,64,128]{3,2,1,0:T(8,128)(2,1)}, u32[]{:S(2)}, u32[]{:S(2)}) collective-permute-start(bf16[2,16,64,128]{3,2,1,0:T(8,128)(2,1)} %collective-permute-done.14.theirs), channel_id=1, source_target_pairs={{0,8},{2,10},{8,16},{10,18},{16,24},{18,26},{12,4},{14,6},{20,12},... | collective-permute-start | bytes 1572872 | tf_op jit(solution)/shard_map/ppermute | solution.py:295
  123.5 1.4 maximum_bitcast_fusion.3
  125.0 1.0 copy-done.5
  126.1 6.2 %adjoint_sweeps.5.own = bf16[4,16,64,128]{3,2,1,0:T(8,128)(2,1)S(1)} custom-call(s32[8]{0:T(128)S(1)} %stack.97.place, bf16[2,16,64,128]{3,2,1,0:T(8,128)(2,1)} %pad_maximum_fusion.4.mine, bf16[2,16,64,128]{3,2,1,0:T(8,128)(2,1)} %collective-permute-done.21.theirs, bf16[2,16,64,128]{3,2,1,0:T(8,128)(2,1)} %collective-permute-done.22.early, ...), custom_call_target="tpu_custom_call" | custom-call | flops 41943040 | bytes 6291456 | tf_op jit(solution)/shard_map/adjoint_sweeps/pallas_call | solution.py:75
  132.3 3.7 %collective-permute-done.15.early = bf16[2,16,64,128]{3,2,1,0:T(8,128)(2,1)} collective-permute-done((bf16[2,16,64,128]{3,2,1,0:T(8,128)(2,1)}, bf16[2,16,64,128]{3,2,1,0:T(8,128)(2,1)}, u32[]{:S(2)}, u32[]{:S(2)}) %collective-permute-start.15) | collective-permute-done | bytes 524320 | tf_op jit(solution)/shard_map/ppermute | solution.py:294
  136.0 1.1 dynamic-slice_reduce_fusion
  137.1 0.9 reshape.145
  138.1 10.3 %collective-permute-done.16.late = bf16[2,16,64,128]{3,2,1,0:T(8,128)(2,1)} collective-permute-done((bf16[2,16,64,128]{3,2,1,0:T(8,128)(2,1)}, bf16[2,16,64,128]{3,2,1,0:T(8,128)(2,1)}, u32[]{:S(2)}, u32[]{:S(2)}) %collective-permute-start.16) | collective-permute-done | bytes 524320 | tf_op jit(solution)/shard_map/ppermute | solution.py:295
  148.5 7.0 %adjoint_sweeps.4.own = bf16[4,16,64,128]{3,2,1,0:T(8,128)(2,1)} custom-call(s32[8]{0:T(128)S(1)} %stack.97.place, bf16[2,16,64,128]{3,2,1,0:T(8,128)(2,1)} %pad_maximum_fusion.3.mine, bf16[2,16,64,128]{3,2,1,0:T(8,128)(2,1)} %collective-permute-done.14.theirs, bf16[2,16,64,128]{3,2,1,0:T(8,128)(2,1)} %collective-permute-done.15.early, ...), custom_call_target="tpu_custom_call" | custom-call | flops 41943040 | bytes 6291456 | tf_op jit(solution)/shard_map/adjoint_sweeps/pallas_call | solution.py:75
  155.6 11.6 %adjoint_sweeps.3.own = bf16[4,16,128,128]{3,2,1,0:T(8,128)(2,1)} custom-call(s32[8]{0:T(128)S(1)} %stack.97.place, bf16[2,16,128,128]{3,2,1,0:T(8,128)(2,1)} %pad_maximum_fusion.mine, bf16[2,16,128,128]{3,2,1,0:T(8,128)(2,1)} %collective-permute-done.1.theirs, bf16[2,16,128,128]{3,2,1,0:T(8,128)(2,1)} %collective-permute-done.2.early, ...), custom_call_target="tpu_custom_call" | custom-call | flops 83886080 | bytes 12582912 | tf_op jit(solution)/shard_map/adjoint_sweeps/pallas_call | solution.py:75
  168.0 5.8 %gram_part.5 = (f32[4,128,64]{2,1,0:T(8,128)S(1)}, f32[16,64,128]{2,1,0:T(8,128)S(1)}) custom-call(s32[2]{0:T(128)S(1)} %pad_add_fusion.where, bf16[4,16,64,128]{3,2,1,0:T(8,128)(2,1)S(1)} %adjoint_sweeps.5.own, bf16[4,16,64,128]{3,2,1,0:T(8,128)(2,1)} %collective-permute-done.24.other, bf16[64,64]{1,0:T(8,128)(2,1)S(1)} %get-tuple-element.64.left_own, ...), custom_call_target="tpu_custom_call" | custom-call | flops 1073741824 | bytes 6291456 | tf_op jit(solution)/shard_map/gram_part/pallas_call | solution.py:143
  173.8 4.7 %collective-permute-start.27 = (bf16[128,64]{1,0:T(8,128)(2,1)S(1)}, bf16[128,64]{1,0:T(8,128)(2,1)S(1)}, u32[]{:S(2)}, u32[]{:S(2)}) collective-permute-start(bf16[128,64]{1,0:T(8,128)(2,1)S(1)} %get-tuple-element.55), channel_id=1, source_target_pairs={{0,24},{2,26},{4,28},{6,30},{8,0},{10,2},{12,4},{14,6},{16,8},{18,... | collective-permute-start | bytes 49160 | tf_op jit(solution)/shard_map/ppermute | solution.py:341
  178.5 1.0 collective-permute-start.25
  179.6 5.9 %gram_part.4 = (f32[4,128,64]{2,1,0:T(8,128)S(1)}, f32[16,64,128]{2,1,0:T(8,128)S(1)}) custom-call(s32[2]{0:T(128)S(1)} %pad_add_fusion.where, bf16[4,16,64,128]{3,2,1,0:T(8,128)(2,1)} %adjoint_sweeps.4.own, bf16[4,16,64,128]{3,2,1,0:T(8,128)(2,1)} %collective-permute-done.17.other, bf16[64,64]{1,0:T(8,128)(2,1)S(1)} %get-tuple-element.63.left_own, ...), custom_call_target="tpu_custom_call" | custom-call | flops 1073741824 | bytes 6291456 | tf_op jit(solution)/shard_map/gram_part/pallas_call | solution.py:143
  185.5 2.9 %collective-permute-start.20 = (bf16[128,64]{1,0:T(8,128)(2,1)S(1)}, bf16[128,64]{1,0:T(8,128)(2,1)S(1)}, u32[]{:S(2)}, u32[]{:S(2)}) collective-permute-start(bf16[128,64]{1,0:T(8,128)(2,1)S(1)} %get-tuple-element.52), channel_id=1, source_target_pairs={{0,24},{2,26},{4,28},{6,30},{8,0},{10,2},{12,4},{14,6},{16,8},{18,... | collective-permute-start | bytes 49160 | tf_op jit(solution)/shard_map/ppermute | solution.py:341
  188.4 2.7 %direct_modes_part.1 = f32[4,8,64,128]{3,2,1,0:T(8,128)S(1)} custom-call(s32[1]{0:T(128)} %bitcast.64.where, bf16[2,64,128]{2,1,0:T(8,128)(2,1)S(1)} %pad_maximum_fusion.6.right, bf16[4,16,128,128]{3,2,1,0:T(8,128)(2,1)S(1)} %direct_sweeps.1.rest_0_, bf16[4,16,128,128]{3,2,1,0:T(8,128)(2,1)} %collective-permute-done.10.rest_1_), custom_call_target="tpu_custom_call" | custom-call | flops 268435456 | bytes 2097152 | tf_op jit(solution)/shard_map/direct_modes_part/pallas_call | solution.py:179
  191.2 1.2 collective-permute-start.19
  192.9 3.3 %collective-permute-done.19 = bf16[128,64]{1,0:T(8,128)(2,1)S(1)} collective-permute-done((bf16[128,64]{1,0:T(8,128)(2,1)S(1)}, bf16[128,64]{1,0:T(8,128)(2,1)S(1)}, u32[]{:S(2)}, u32[]{:S(2)}) %collective-permute-start.19) | collective-permute-done | bytes 16416 | tf_op jit(solution)/shard_map/ppermute | solution.py:341
  196.2 1.9 collective-permute-done.18
  198.1 0.8 collective-permute-done.29
  199.0 0.9 copy.95
  199.8 6.1 %gram_part.3 = (f32[4,256,64]{2,1,0:T(8,128)S(1)}, f32[16,64,128]{2,1,0:T(8,128)S(1)}) custom-call(s32[2]{0:T(128)S(1)} %pad_add_fusion.where, bf16[4,16,128,128]{3,2,1,0:T(8,128)(2,1)} %adjoint_sweeps.3.own, bf16[4,16,128,128]{3,2,1,0:T(8,128)(2,1)} %collective-permute-done.4.other, bf16[64,128]{1,0:T(8,128)(2,1)S(1)} %slice.137.left_own, ...), custom_call_target="tpu_custom_call" | custom-call | flops 2147483648 | bytes 8388608 | tf_op jit(solution)/shard_map/gram_part/pallas_call | solution.py:143
  206.0 3.8 %collective-permute-start.13 = (bf16[256,64]{1,0:T(8,128)(2,1)S(1)}, bf16[256,64]{1,0:T(8,128)(2,1)S(1)}, u32[]{:S(2)}, u32[]{:S(2)}) collective-permute-start(bf16[256,64]{1,0:T(8,128)(2,1)S(1)} %get-tuple-element.45), channel_id=1, source_target_pairs={{0,24},{2,26},{4,28},{6,30},{8,0},{10,2},{12,4},{14,6},{16,8},{18,... | collective-permute-start | bytes 98312 | tf_op jit(solution)/shard_map/ppermute | solution.py:341
  211.3 0.9 collective-permute-done.13
  212.2 4.6 %collective-permute-done.12 = bf16[256,64]{1,0:T(8,128)(2,1)S(1)} collective-permute-done((bf16[256,64]{1,0:T(8,128)(2,1)S(1)}, bf16[256,64]{1,0:T(8,128)(2,1)S(1)}, u32[]{:S(2)}, u32[]{:S(2)}) %collective-permute-start.12) | collective-permute-done | bytes 32800 | tf_op jit(solution)/shard_map/ppermute | solution.py:341
  216.9 0.8 copy.94
  217.6 0.9 fusion
  (135 shorter events, 9.3 us)
Async XLA Ops:
  2.1 1.3 slice-start
  3.6 2.0 copy-start.6
  4.8 55.1 %collective-permute-start = (bf16[16,256,128]{2,1,0:T(8,128)(2,1)}, bf16[16,256,128]{2,1,0:T(8,128)(2,1)}, u32[]{:S(2)}, u32[]{:S(2)}) collective-permute-start(bf16[16,256,128]{2,1,0:T(8,128)(2,1)} %maximum_bitcast_fusion.1), channel_id=1, source_target_pairs={{0,2},{2,0},{4,6},{6,4},{8,10},{10,8},{12,14},{14,12},{16,18},{18,... | collective-permute-start | bytes 3145736 | tf_op jit(solution)/shard_map/ppermute | solution.py:234
  5.9 6.0 %copy-start.8 = (bf16[1,64,16,128]{3,2,1,0:T(8,128)(2,1)S(1)}, bf16[1,64,16,128]{3,2,1,0:T(8,128)(2,1)}, u32[]{:S(2)}) copy-start(bf16[1,64,16,128]{3,2,1,0:T(8,128)(2,1)} %get-tuple-element.49) | copy-start | bytes 786436
  6.9 43.5 %collective-permute-start.5 = (bf16[16,128,128]{2,1,0:T(8,128)(2,1)}, bf16[16,128,128]{2,1,0:T(8,128)(2,1)}, u32[]{:S(2)}, u32[]{:S(2)}) collective-permute-start(bf16[16,128,128]{2,1,0:T(8,128)(2,1)} %bitcast.38), channel_id=1, source_target_pairs={{0,2},{2,0},{4,6},{6,4},{8,10},{10,8},{12,14},{14,12},{16,18},{18,... | collective-permute-start | bytes 1572872 | tf_op jit(solution)/shard_map/ppermute | solution.py:234
  8.3 44.5 %collective-permute-start.7 = (bf16[16,128,128]{2,1,0:T(8,128)(2,1)}, bf16[16,128,128]{2,1,0:T(8,128)(2,1)}, u32[]{:S(2)}, u32[]{:S(2)}) collective-permute-start(bf16[16,128,128]{2,1,0:T(8,128)(2,1)} %bitcast.44), channel_id=1, source_target_pairs={{0,6},{2,4},{4,2},{6,0},{8,14},{10,12},{12,10},{14,8},{16,22},{18,... | collective-permute-start | bytes 1572872 | tf_op jit(solution)/shard_map/ppermute | solution.py:234
  11.8 41.0 %collective-permute-start.6 = (bf16[16,128,128]{2,1,0:T(8,128)(2,1)}, bf16[16,128,128]{2,1,0:T(8,128)(2,1)}, u32[]{:S(2)}, u32[]{:S(2)}) collective-permute-start(bf16[16,128,128]{2,1,0:T(8,128)(2,1)} %bitcast.41), channel_id=1, source_target_pairs={{0,4},{2,6},{4,0},{6,2},{8,12},{10,14},{12,8},{14,10},{16,20},{18,... | collective-permute-start | bytes 1572872 | tf_op jit(solution)/shard_map/ppermute | solution.py:234
  12.0 1.0 copy-start.17
  12.0 1.0 copy-start.13
  12.0 1.0 copy-start.14
  12.0 1.0 copy-start.15
  12.2 1.0 copy-start.11
  12.2 2.4 %copy-start.12 = (f32[1,16,128]{2,1,0:T(8,128)S(1)}, f32[1,16,128]{2,1,0:T(8,128)}, u32[]{:S(2)}) copy-start(f32[1,16,128]{2,1,0:T(8,128)} %param.11) | copy-start | bytes 24580
  51.5 27.9 %collective-permute-start.8 = (bf16[2,16,128,128]{3,2,1,0:T(8,128)(2,1)S(1)}, bf16[2,16,128,128]{3,2,1,0:T(8,128)(2,1)S(1)}, u32[]{:S(2)}, u32[]{:S(2)}) collective-permute-start(bf16[2,16,128,128]{3,2,1,0:T(8,128)(2,1)S(1)} %pad_maximum_fusion.1.mine), channel_id=1, source_target_pairs={{4,12},{6,14},{12,20},{14,22},{20,28},{22,30},{8,0},{10,2},{16,8},... | collective-permute-start | bytes 3145736 | tf_op jit(solution)/shard_map/ppermute | solution.py:294
  54.1 10.4 %copy-start = (bf16[2,16,128,128]{3,2,1,0:T(8,128)(2,1)}, bf16[2,16,128,128]{3,2,1,0:T(8,128)(2,1)S(1)}, u32[]{:S(2)}) copy-start(bf16[2,16,128,128]{3,2,1,0:T(8,128)(2,1)S(1)} %pad_maximum_fusion.2.theirs) | copy-start | bytes 3145732
  54.1 10.4 %copy-start.7 = (bf16[1,16,64,128]{3,2,1,0:T(8,128)(2,1)S(1)}, bf16[1,16,64,128]{3,2,1,0:T(8,128)(2,1)}, u32[]{:S(2)}) copy-start(bf16[1,16,64,128]{3,2,1,0:T(8,128)(2,1)} %get-tuple-element.39) | copy-start | bytes 786436
  54.1 27.3 %collective-permute-start.9 = (bf16[2,16,128,128]{3,2,1,0:T(8,128)(2,1)S(1)}, bf16[2,16,128,128]{3,2,1,0:T(8,128)(2,1)}, u32[]{:S(2)}, u32[]{:S(2)}) collective-permute-start(bf16[2,16,128,128]{3,2,1,0:T(8,128)(2,1)S(1)} %pad_maximum_fusion.2.theirs), channel_id=1, source_target_pairs={{0,8},{2,10},{8,16},{10,18},{16,24},{18,26},{12,4},{14,6},{20,12},... | collective-permute-start | bytes 3145736 | tf_op jit(solution)/shard_map/ppermute | solution.py:295
  62.1 43.5 %collective-permute-start.1 = (bf16[2,16,128,128]{3,2,1,0:T(8,128)(2,1)}, bf16[2,16,128,128]{3,2,1,0:T(8,128)(2,1)}, u32[]{:S(2)}, u32[]{:S(2)}) collective-permute-start(bf16[2,16,128,128]{3,2,1,0:T(8,128)(2,1)} %pad_maximum_fusion.mine), channel_id=1, source_target_pairs={{0,4},{2,6},{4,0},{6,2},{8,12},{10,14},{12,8},{14,10},{16,20},{18,... | collective-permute-start | bytes 3145736 | tf_op jit(solution)/shard_map/ppermute | solution.py:234
  65.4 34.3 %collective-permute-start.21 = (bf16[2,16,64,128]{3,2,1,0:T(8,128)(2,1)}, bf16[2,16,64,128]{3,2,1,0:T(8,128)(2,1)}, u32[]{:S(2)}, u32[]{:S(2)}) collective-permute-start(bf16[2,16,64,128]{3,2,1,0:T(8,128)(2,1)} %pad_maximum_fusion.4.mine), channel_id=1, source_target_pairs={{0,4},{2,6},{4,0},{6,2},{8,12},{10,14},{12,8},{14,10},{16,20},{18,... | collective-permute-start | bytes 1572872 | tf_op jit(solution)/shard_map/ppermute | solution.py:234
  67.4 33.6 %collective-permute-start.22 = (bf16[2,16,64,128]{3,2,1,0:T(8,128)(2,1)}, bf16[2,16,64,128]{3,2,1,0:T(8,128)(2,1)}, u32[]{:S(2)}, u32[]{:S(2)}) collective-permute-start(bf16[2,16,64,128]{3,2,1,0:T(8,128)(2,1)} %pad_maximum_fusion.4.mine), channel_id=1, source_target_pairs={{4,12},{6,14},{12,20},{14,22},{20,28},{22,30},{8,0},{10,2},{16,8},... | collective-permute-start | bytes 1572872 | tf_op jit(solution)/shard_map/ppermute | solution.py:294
  79.4 1.0 copy-start.2
  80.4 29.8 %collective-permute-start.14 = (bf16[2,16,64,128]{3,2,1,0:T(8,128)(2,1)}, bf16[2,16,64,128]{3,2,1,0:T(8,128)(2,1)}, u32[]{:S(2)}, u32[]{:S(2)}) collective-permute-start(bf16[2,16,64,128]{3,2,1,0:T(8,128)(2,1)} %pad_maximum_fusion.3.mine), channel_id=1, source_target_pairs={{0,4},{2,6},{4,0},{6,2},{8,12},{10,14},{12,8},{14,10},{16,20},{18,... | collective-permute-start | bytes 1572872 | tf_op jit(solution)/shard_map/ppermute | solution.py:234
  81.5 1.2 copy-start.1
  82.8 1.2 copy-start.3
  84.0 25.2 %copy-start.16 = (f32[128]{0:T(128)S(1)}, f32[128]{0:T(128)}, u32[]{:S(2)}) copy-start(f32[128]{0:T(128)} %get-tuple-element.71) | copy-start | bytes 1540
  84.0 26.1 %copy-start.9 = (f32[1024,64]{0,1:T(8,128)S(1)}, f32[1024,64]{0,1:T(8,128)}, u32[]{:S(2)}) copy-start(f32[1024,64]{0,1:T(8,128)} %param.16) | copy-start | bytes 786436
  95.2 72.8 %collective-permute-start.10 = (bf16[4,16,128,128]{3,2,1,0:T(8,128)(2,1)S(1)}, bf16[4,16,128,128]{3,2,1,0:T(8,128)(2,1)}, u32[]{:S(2)}, u32[]{:S(2)}) collective-permute-start(bf16[4,16,128,128]{3,2,1,0:T(8,128)(2,1)S(1)} %direct_sweeps.1.rest_0_), channel_id=1, source_target_pairs={{0,1},{1,0},{2,3},{3,2},{4,5},{5,4},{6,7},{7,6},{8,9},{9,8},{10,11... | collective-permute-start | bytes 6291464 | tf_op jit(solution)/shard_map/ppermute | solution.py:299
  99.7 55.8 %collective-permute-start.2 = (bf16[2,16,128,128]{3,2,1,0:T(8,128)(2,1)}, bf16[2,16,128,128]{3,2,1,0:T(8,128)(2,1)}, u32[]{:S(2)}, u32[]{:S(2)}) collective-permute-start(bf16[2,16,128,128]{3,2,1,0:T(8,128)(2,1)} %pad_maximum_fusion.mine), channel_id=1, source_target_pairs={{4,12},{6,14},{12,20},{14,22},{20,28},{22,30},{8,0},{10,2},{16,8},... | collective-permute-start | bytes 3145736 | tf_op jit(solution)/shard_map/ppermute | solution.py:294
  101.0 17.2 %collective-permute-start.23 = (bf16[2,16,64,128]{3,2,1,0:T(8,128)(2,1)}, bf16[2,16,64,128]{3,2,1,0:T(8,128)(2,1)S(1)}, u32[]{:S(2)}, u32[]{:S(2)}) collective-permute-start(bf16[2,16,64,128]{3,2,1,0:T(8,128)(2,1)} %collective-permute-done.21.theirs), channel_id=1, source_target_pairs={{0,8},{2,10},{8,16},{10,18},{16,24},{18,26},{12,4},{14,6},{20,12},... | collective-permute-start | bytes 1572872 | tf_op jit(solution)/shard_map/ppermute | solution.py:295
  105.6 49.9 %collective-permute-start.3 = (bf16[2,16,128,128]{3,2,1,0:T(8,128)(2,1)}, bf16[2,16,128,128]{3,2,1,0:T(8,128)(2,1)}, u32[]{:S(2)}, u32[]{:S(2)}) collective-permute-start(bf16[2,16,128,128]{3,2,1,0:T(8,128)(2,1)} %collective-permute-done.1.theirs), channel_id=1, source_target_pairs={{0,8},{2,10},{8,16},{10,18},{16,24},{18,26},{12,4},{14,6},{20,12},... | collective-permute-start | bytes 3145736 | tf_op jit(solution)/shard_map/ppermute | solution.py:295
  110.2 25.8 %collective-permute-start.15 = (bf16[2,16,64,128]{3,2,1,0:T(8,128)(2,1)}, bf16[2,16,64,128]{3,2,1,0:T(8,128)(2,1)}, u32[]{:S(2)}, u32[]{:S(2)}) collective-permute-start(bf16[2,16,64,128]{3,2,1,0:T(8,128)(2,1)} %pad_maximum_fusion.3.mine), channel_id=1, source_target_pairs={{4,12},{6,14},{12,20},{14,22},{20,28},{22,30},{8,0},{10,2},{16,8},... | collective-permute-start | bytes 1572872 | tf_op jit(solution)/shard_map/ppermute | solution.py:294
  118.2 6.7 %copy-start.4 = (bf16[2,16,64,128]{3,2,1,0:T(8,128)(2,1)}, bf16[2,16,64,128]{3,2,1,0:T(8,128)(2,1)S(1)}, u32[]{:S(2)}) copy-start(bf16[2,16,64,128]{3,2,1,0:T(8,128)(2,1)S(1)} %collective-permute-done.23.late) | copy-start | bytes 1572868
  118.2 30.2 %collective-permute-start.16 = (bf16[2,16,64,128]{3,2,1,0:T(8,128)(2,1)}, bf16[2,16,64,128]{3,2,1,0:T(8,128)(2,1)}, u32[]{:S(2)}, u32[]{:S(2)}) collective-permute-start(bf16[2,16,64,128]{3,2,1,0:T(8,128)(2,1)} %collective-permute-done.14.theirs), channel_id=1, source_target_pairs={{0,8},{2,10},{8,16},{10,18},{16,24},{18,26},{12,4},{14,6},{20,12},... | collective-permute-start | bytes 1572872 | tf_op jit(solution)/shard_map/ppermute | solution.py:295
  125.0 1.0 copy-start.5
  136.0 32.0 %collective-permute-start.24 = (bf16[4,16,64,128]{3,2,1,0:T(8,128)(2,1)S(1)}, bf16[4,16,64,128]{3,2,1,0:T(8,128)(2,1)}, u32[]{:S(2)}, u32[]{:S(2)}) collective-permute-start(bf16[4,16,64,128]{3,2,1,0:T(8,128)(2,1)S(1)} %adjoint_sweeps.5.own), channel_id=1, source_target_pairs={{0,2},{2,0},{4,6},{6,4},{8,10},{10,8},{12,14},{14,12},{16,18},{18,... | collective-permute-start | bytes 3145736 | tf_op jit(solution)/shard_map/ppermute | solution.py:234
  155.4 24.1 %collective-permute-start.17 = (bf16[4,16,64,128]{3,2,1,0:T(8,128)(2,1)}, bf16[4,16,64,128]{3,2,1,0:T(8,128)(2,1)}, u32[]{:S(2)}, u32[]{:S(2)}) collective-permute-start(bf16[4,16,64,128]{3,2,1,0:T(8,128)(2,1)} %adjoint_sweeps.4.own), channel_id=1, source_target_pairs={{0,2},{2,0},{4,6},{6,4},{8,10},{10,8},{12,14},{14,12},{16,18},{18,... | collective-permute-start | bytes 3145736 | tf_op jit(solution)/shard_map/ppermute | solution.py:234
  155.5 12.2 %copy-start.10 = (bf16[64,256]{1,0:T(8,128)(2,1)S(1)}, bf16[64,256]{1,0:T(8,128)(2,1)}, u32[]{:S(2)}) copy-start(bf16[64,256]{1,0:T(8,128)(2,1)} %maximum_bitcast_fusion.3) | copy-start | bytes 98308
  167.2 32.7 %collective-permute-start.4 = (bf16[4,16,128,128]{3,2,1,0:T(8,128)(2,1)}, bf16[4,16,128,128]{3,2,1,0:T(8,128)(2,1)}, u32[]{:S(2)}, u32[]{:S(2)}) collective-permute-start(bf16[4,16,128,128]{3,2,1,0:T(8,128)(2,1)} %adjoint_sweeps.3.own), channel_id=1, source_target_pairs={{0,2},{2,0},{4,6},{6,4},{8,10},{10,8},{12,14},{14,12},{16,18},{18,... | collective-permute-start | bytes 6291464 | tf_op jit(solution)/shard_map/ppermute | solution.py:234
  173.8 17.4 %collective-permute-start.27 = (bf16[128,64]{1,0:T(8,128)(2,1)S(1)}, bf16[128,64]{1,0:T(8,128)(2,1)S(1)}, u32[]{:S(2)}, u32[]{:S(2)}) collective-permute-start(bf16[128,64]{1,0:T(8,128)(2,1)S(1)} %get-tuple-element.55), channel_id=1, source_target_pairs={{0,24},{2,26},{4,28},{6,30},{8,0},{10,2},{12,4},{14,6},{16,8},{18,... | collective-permute-start | bytes 49160 | tf_op jit(solution)/shard_map/ppermute | solution.py:341
  178.5 13.9 %collective-permute-start.26 = (bf16[128,64]{1,0:T(8,128)(2,1)S(1)}, bf16[128,64]{1,0:T(8,128)(2,1)S(1)}, u32[]{:S(2)}, u32[]{:S(2)}) collective-permute-start(bf16[128,64]{1,0:T(8,128)(2,1)S(1)} %get-tuple-element.56), channel_id=1, source_target_pairs={{0,16},{2,18},{4,20},{6,22},{8,24},{10,26},{12,28},{14,30},{16,0},... | collective-permute-start | bytes 49160 | tf_op jit(solution)/shard_map/ppermute | solution.py:341
  178.5 13.9 %collective-permute-start.25 = (bf16[128,64]{1,0:T(8,128)(2,1)S(1)}, bf16[128,64]{1,0:T(8,128)(2,1)S(1)}, u32[]{:S(2)}, u32[]{:S(2)}) collective-permute-start(bf16[128,64]{1,0:T(8,128)(2,1)S(1)} %get-tuple-element.54), channel_id=1, source_target_pairs={{0,8},{2,10},{4,12},{6,14},{8,16},{10,18},{12,20},{14,22},{16,24},... | collective-permute-start | bytes 49160 | tf_op jit(solution)/shard_map/ppermute | solution.py:341
  185.5 7.0 %collective-permute-start.20 = (bf16[128,64]{1,0:T(8,128)(2,1)S(1)}, bf16[128,64]{1,0:T(8,128)(2,1)S(1)}, u32[]{:S(2)}, u32[]{:S(2)}) collective-permute-start(bf16[128,64]{1,0:T(8,128)(2,1)S(1)} %get-tuple-element.52), channel_id=1, source_target_pairs={{0,24},{2,26},{4,28},{6,30},{8,0},{10,2},{12,4},{14,6},{16,8},{18,... | collective-permute-start | bytes 49160 | tf_op jit(solution)/shard_map/ppermute | solution.py:341
  191.2 5.0 %collective-permute-start.19 = (bf16[128,64]{1,0:T(8,128)(2,1)S(1)}, bf16[128,64]{1,0:T(8,128)(2,1)S(1)}, u32[]{:S(2)}, u32[]{:S(2)}) collective-permute-start(bf16[128,64]{1,0:T(8,128)(2,1)S(1)} %get-tuple-element.53), channel_id=1, source_target_pairs={{0,16},{2,18},{4,20},{6,22},{8,24},{10,26},{12,28},{14,30},{16,0},... | collective-permute-start | bytes 49160 | tf_op jit(solution)/shard_map/ppermute | solution.py:341
  192.4 5.7 %collective-permute-start.18 = (bf16[128,64]{1,0:T(8,128)(2,1)S(1)}, bf16[128,64]{1,0:T(8,128)(2,1)S(1)}, u32[]{:S(2)}, u32[]{:S(2)}) collective-permute-start(bf16[128,64]{1,0:T(8,128)(2,1)S(1)} %get-tuple-element.51), channel_id=1, source_target_pairs={{0,8},{2,10},{4,12},{6,14},{8,16},{10,18},{12,20},{14,22},{16,24},... | collective-permute-start | bytes 49160 | tf_op jit(solution)/shard_map/ppermute | solution.py:341
  192.4 5.7 %collective-permute-start.30 = (bf16[8,64,128]{2,1,0:T(8,128)(2,1)S(1)}, bf16[8,64,128]{2,1,0:T(8,128)(2,1)S(1)}, u32[]{:S(2)}, u32[]{:S(2)}) collective-permute-start(bf16[8,64,128]{2,1,0:T(8,128)(2,1)S(1)} %get-tuple-element.36), channel_id=1, source_target_pairs={{0,6},{2,4},{4,2},{6,0},{8,14},{10,12},{12,10},{14,8},{16,22},{18,... | collective-permute-start | bytes 393224 | tf_op jit(solution)/shard_map/ppermute | solution.py:234
  192.5 6.4 %collective-permute-start.29 = (bf16[8,64,128]{2,1,0:T(8,128)(2,1)S(1)}, bf16[8,64,128]{2,1,0:T(8,128)(2,1)S(1)}, u32[]{:S(2)}, u32[]{:S(2)}) collective-permute-start(bf16[8,64,128]{2,1,0:T(8,128)(2,1)S(1)} %get-tuple-element.37), channel_id=1, source_target_pairs={{0,4},{2,6},{4,0},{6,2},{8,12},{10,14},{12,8},{14,10},{16,20},{18,... | collective-permute-start | bytes 393224 | tf_op jit(solution)/shard_map/ppermute | solution.py:234
  196.2 2.7 %collective-permute-start.28 = (bf16[8,64,128]{2,1,0:T(8,128)(2,1)S(1)}, bf16[8,64,128]{2,1,0:T(8,128)(2,1)S(1)}, u32[]{:S(2)}, u32[]{:S(2)}) collective-permute-start(bf16[8,64,128]{2,1,0:T(8,128)(2,1)S(1)} %get-tuple-element.35), channel_id=1, source_target_pairs={{0,2},{2,0},{4,6},{6,4},{8,10},{10,8},{12,14},{14,12},{16,18},{18,... | collective-permute-start | bytes 393224 | tf_op jit(solution)/shard_map/ppermute | solution.py:234
  206.0 6.2 %collective-permute-start.13 = (bf16[256,64]{1,0:T(8,128)(2,1)S(1)}, bf16[256,64]{1,0:T(8,128)(2,1)S(1)}, u32[]{:S(2)}, u32[]{:S(2)}) collective-permute-start(bf16[256,64]{1,0:T(8,128)(2,1)S(1)} %get-tuple-element.45), channel_id=1, source_target_pairs={{0,24},{2,26},{4,28},{6,30},{8,0},{10,2},{12,4},{14,6},{16,8},{18,... | collective-permute-start | bytes 98312 | tf_op jit(solution)/shard_map/ppermute | solution.py:341
  209.8 7.0 %collective-permute-start.12 = (bf16[256,64]{1,0:T(8,128)(2,1)S(1)}, bf16[256,64]{1,0:T(8,128)(2,1)S(1)}, u32[]{:S(2)}, u32[]{:S(2)}) collective-permute-start(bf16[256,64]{1,0:T(8,128)(2,1)S(1)} %get-tuple-element.46), channel_id=1, source_target_pairs={{0,16},{2,18},{4,20},{6,22},{8,24},{10,26},{12,28},{14,30},{16,0},... | collective-permute-start | bytes 98312 | tf_op jit(solution)/shard_map/ppermute | solution.py:341
  209.8 7.0 %collective-permute-start.11 = (bf16[256,64]{1,0:T(8,128)(2,1)S(1)}, bf16[256,64]{1,0:T(8,128)(2,1)S(1)}, u32[]{:S(2)}, u32[]{:S(2)}) collective-permute-start(bf16[256,64]{1,0:T(8,128)(2,1)S(1)} %get-tuple-element.44), channel_id=1, source_target_pairs={{0,8},{2,10},{4,12},{6,14},{8,16},{10,18},{12,20},{14,22},{16,24},... | collective-permute-start | bytes 98312 | tf_op jit(solution)/shard_map/ppermute | solution.py:341
  210.7 7.0 %collective-permute-start.31 = (bf16[8,64,128]{2,0,1:T(8,128)(2,1)S(1)}, bf16[8,64,128]{2,0,1:T(8,128)(2,1)S(1)}, u32[]{:S(2)}, u32[]{:S(2)}) collective-permute-start(bf16[8,64,128]{2,0,1:T(8,128)(2,1)S(1)} %bitcast.193), channel_id=1, source_target_pairs={{0,1},{1,0},{2,3},{3,2},{4,5},{5,4},{6,7},{7,6},{8,9},{9,8},{10,11... | collective-permute-start | bytes 393224 | tf_op jit(solution)/shard_map/ppermute | solution.py:299

commit v2 on v0

v2 whole, which is shorter than its diff:
```python
import functools
import math

import jax
import jax.numpy as jnp
from jax import lax
from jax.experimental import pallas as pl
from jax.experimental.pallas import tpu as pltpu
from jax.sharding import PartitionSpec as P

GROUP = 4
HALO = 2
STEP = 32
SWEEP_COST = 10000
CHUNKS = (1, 1)
EXTRA = 4
VMEM = 14 * 1024 * 1024

SLOW = pl.BlockSpec(memory_space=pltpu.HBM)
FAST = pl.BlockSpec(memory_space=pltpu.VMEM)
SCALAR = pl.BlockSpec(memory_space=pltpu.SMEM)


def call(kernel, name, in_specs, out_shape, scratch, flops, *operands):
    return pl.pallas_call(
        kernel,
        in_specs=in_specs,
        out_specs=jax.tree.map(lambda _: FAST, out_shape),
        out_shape=out_shape,
        scratch_shapes=scratch,
        compiler_params=pltpu.CompilerParams(vmem_limit_bytes=VMEM),
        cost_estimate=pl.CostEstimate(flops=flops, bytes_accessed=1024, transcendentals=0),
        name=name,
    )(*operands)


def pack_kernel(plan, info, source, conductance, token, *refs):
    outs, field, sems = refs[:-2], refs[-2], refs[-1]
    member, core = info[0], info[1]
    copies, more = [], []
    values = conductance[0]
    high = values.astype(jnp.bfloat16)
    rest = values - high.astype(jnp.float32)
    middle = rest.astype(jnp.bfloat16)

    def add(group, source, target):
        copy = pltpu.make_async_copy(source, target, sems.at[len(copies) + len(more)])
        group.append(copy)

    for out, pieces in zip(outs, plan):
        at = 0
        for kind, *what in pieces:
            if kind == "set":
                blocks, _, block = source.shape[:3]
                for i in range(blocks):
                    add(copies, source.at[i, member ^ what[0]], out.at[pl.ds(at + i * block, block)])
                at += blocks * block
                add(more, field, out.at[pl.ds(at, EXTRA)])
                at += EXTRA
            else:
                start, size, flip = what
                spot = start + (1 - core if flip else core) * size
                add(copies, source.at[pl.ds(spot, size)], out.at[pl.ds(at, size)])
                at += size
    for copy in copies:
        copy.start()
    field[0] = high
    field[1] = middle
    field[2] = (rest - middle.astype(jnp.float32)).astype(jnp.bfloat16)
    field[3] = jnp.zeros_like(high)
    for copy in more:
        copy.start()
    for copy in copies + more:
        copy.wait()


def pack(info, source, conductance, token, plan):
    blocks, block = source.shape[0], source.shape[2]
    width_y, width_z = source.shape[-2:]
    lengths = {"set": lambda what: blocks * block + EXTRA, "half": lambda what: what[1]}
    shapes, count = [], 0
    for pieces in plan:
        entries = sum(lengths[kind](what) for kind, *what in pieces)
        shapes.append(jax.ShapeDtypeStruct((entries, width_y, width_z), source.dtype))
        count += sum(blocks + 1 if piece[0] == "set" else 1 for piece in pieces)
    scratch = [pltpu.VMEM((EXTRA, width_y, width_z), source.dtype), pltpu.SemaphoreType.DMA((count,))]
    return call(
        functools.partial(pack_kernel, plan),
        "pack",
        [SCALAR, SLOW, FAST, pl.BlockSpec(memory_space=pl.ANY)],
        shapes,
        scratch,
        1000,
        info,
        source,
        conductance,
        token,
    )


def join_kernel(*refs):
    out, at = refs[-1], 0
    for ref in refs[:-1]:
        out[at : at + ref.shape[0]] = ref[...]
        at += ref.shape[0]


def join(*arrays):
    shape = (sum(a.shape[0] for a in arrays),) + arrays[0].shape[1:]
    out_shape = jax.ShapeDtypeStruct(shape, arrays[0].dtype)
    return call(join_kernel, "join", [FAST] * len(arrays), out_shape, [], 1000, *arrays)


def along_z(rows, band):
    high = rows.astype(jnp.bfloat16)
    low = (rows - high.astype(jnp.float32)).astype(jnp.bfloat16)
    both = jnp.concatenate([high, low], axis=1)
    return jnp.dot(both, band[...], preferred_element_type=jnp.float32)


def sweep_kernel(adjoint, layout, begin, lead, place, *refs):
    planes = GROUP + 2 * HALO
    arrays = 1 + max(number for number, _ in layout)
    sources = [(refs[number], offset) for number, offset in layout]
    shift, band = refs[arrays], refs[arrays + 1]
    if lead is None:
        cond, out = refs[arrays + 2], refs[arrays + 3]
    else:
        out, cond = refs[arrays + 2], refs[arrays + 3]
    inverse, flat, start, gain, first, lateral = refs[-6:]
    _, width_y, step, width_z = start.shape
    count = out.shape[0]

    if adjoint:
        inverse[...] = 1.0 / cond[HALO : planes - HALO]
    if lead is not None:
        for slot, (source, offset) in enumerate(sources):
            terms = [source[offset + lead + i].astype(jnp.float32) for i in range(3)]
            cond[place[slot]] = (terms[0] + terms[1]) + terms[2]

    def relax(old, low, high, put):
        for plane in range(low, high):
            rows = old[plane].reshape(width_y * step, width_z)
            lateral[...] = along_z(rows, band).reshape(width_y, step, width_z)
            for y in range(width_y):
                total = old[plane - 1, y] + old[plane + 1, y]
                if y > 0:
                    total = total + old[plane, y - 1]
                if y < width_y - 1:
                    total = total + old[plane, y + 1]
                put(plane, y, start[plane, y] + gain[plane, y] * (total + lateral[y]))

    def keep(plane, y, state):
        first[plane, y] = state

    def one_pass(number, carry):
        at = pl.multiple_of(number * step, step)
        level = shift[pl.ds(begin + at, step), :]
        for slot, (source, offset) in enumerate(sources):
            plane = place[slot]
            piece = source[pl.ds(offset + begin + at, step)].astype(jnp.float32)
            flat[slot] = piece.reshape(step * width_y, width_z)
            for y in range(width_y):
                coeff = cond[plane, pl.ds(y, 1), :]
                diag = level + 6.0 * coeff
                guess = pltpu.reciprocal(diag, approx=True)
                recip = guess * (2.0 - diag * guess)
                scaled = recip * coeff
                force = flat[slot, pl.ds(y, step, stride=width_y), :]
                gain[plane, y] = scaled
                start[plane, y] = force * (scaled if adjoint else recip)

        def emit(plane, y, state):
            if adjoint:
                state = state * inverse[plane - HALO, pl.ds(y, 1), :]
            spot = ((plane - HALO) * width_y + y) * width_z
            out[pl.ds(at, step), spot : spot + width_z] = state.astype(jnp.bfloat16)

        relax(start, 1, planes - 1, keep)
        relax(first, HALO, planes - HALO, emit)
        return carry

    lax.fori_loop(0, count // step, one_pass, 0)


def sweep(adjoint, place, pair, near, far, early, late_near, late_far, shift, band, cond, span=None):
    width_z = shift.shape[1]
    begin, count = span or (0, shift.shape[0])
    sources = [pair, near, far, early, late_near, late_far]
    size = near.shape[0]
    layout = [(0, 0), (0, size), (1, 0), (2, 0), (3, 0), (3, size), (4, 0), (5, 0)]
    width_y = near.shape[1]
    planes = GROUP + 2 * HALO
    step = min(STEP, count)
    cells = GROUP * width_y * width_z
    out_shape = [jax.ShapeDtypeStruct((count, cells), jnp.bfloat16)]
    if cond is None:
        out_shape += [jax.ShapeDtypeStruct((planes, width_y, width_z), jnp.float32)]
    field = pltpu.VMEM((planes, width_y, step, width_z), jnp.float32)
    scratch = [
        pltpu.VMEM((GROUP, width_y, width_z), jnp.float32),
        pltpu.VMEM((planes, step * width_y, width_z), jnp.float32),
        field,
        field,
        field,
        pltpu.VMEM((width_y, step, width_z), jnp.float32),
    ]
    operands = [place, *sources, shift, band] + ([] if cond is None else [cond])
    return call(
        functools.partial(sweep_kernel, adjoint, layout, begin, shift.shape[0] if cond is None else None),
        "adjoint_sweeps" if adjoint else "direct_sweeps",
        [SCALAR] + [FAST] * (len(operands) - 1),
        out_shape,
        scratch,
        SWEEP_COST * count * cells,
        *operands,
    )


def scaled_factors(factors, singular):
    return (factors * (1.0 / jnp.sqrt(singular[...]))).astype(jnp.bfloat16)


def slab(refs, at, depth):
    span = pl.ds(pl.multiple_of(at, 128), depth)
    return jnp.concatenate([ref[:, span] for ref in refs], axis=0)


def gram_kernel(start, blocks, parts, splits, last, info, factors, singular, *refs):
    own, far, direct = refs[:splits], refs[splits : 2 * splits], refs[2 * splits : 2 * splits + parts]
    rest = refs[2 * splits + parts :]
    if last:
        older, older_modes = rest[:2]
        rest = rest[2:]
        kept, sent, kept_modes, sent_modes = rest[0], rest[1:-4], rest[-4], rest[-3]
        pieces, modes = rest[-2:]
    else:
        pieces, modes = rest
    member, core, share = info[0], info[1], info[2]
    half, cells = splits * own[0].shape[0], own[0].shape[1]
    count, _, width = pieces.shape
    depth = cells // GROUP
    dims = (((1,), (1,)), ((), ()))
    total = jnp.zeros((2 * half, count * width), jnp.float32)
    for plane in range(GROUP):
        rows, cols = slab((*own, *far), plane * depth, depth), slab(direct, plane * depth, depth)
        total = total + lax.dot_general(rows, cols, dims, preferred_element_type=jnp.float32)
    for side in range(2):
        first = jnp.where(side == 0, core, 1 - core) * half
        spot = pl.ds(pl.multiple_of(first, half), half)
        for part in range(count):
            pieces[part, spot, :] = total[side * half : (side + 1) * half, part * width : (part + 1) * width]
    left = scaled_factors(factors[:, start : start + 2 * half], singular)
    lower, upper = left[:, :half], left[:, half:]
    swapped = jnp.concatenate(
        [jnp.where(core == 0, lower, upper), jnp.where(core == 0, upper, lower)], axis=1
    )
    term = jnp.dot(swapped, slab((*own, *far), member * depth, depth), preferred_element_type=jnp.float32)
    if not last:
        modes[...] = term
        return
    modes[...] = older_modes[...] + term
    for number in range(len(sent) + 1):
        index = info[4 + number]
        if number == 0:
            kept[0:start, :] = older[index]
            kept[start:, :] = pieces[index]
        else:
            sent[number - 1][0:start, :] = older[index].astype(jnp.bfloat16)
            sent[number - 1][start:, :] = pieces[index].astype(jnp.bfloat16)
    shares = sent_modes.shape[0] + 1
    wide = depth // shares
    for step in range(shares):
        piece = modes[:, pl.ds(pl.multiple_of(((share + step) % shares) * wide, wide), wide)]
        if step == 0:
            kept_modes[...] = piece
        else:
            sent_modes[step - 1] = piece.astype(jnp.bfloat16)


def gram_part(info, start, own, far, factors, singular, direct, blocks, older, layers):
    half, cells = len(own) * own[0].shape[0], own[0].shape[1]
    width = direct[0].shape[0]
    mode_count, rows = factors.shape
    shares = len(direct) // blocks
    depth = cells // GROUP
    pieces = (shares * blocks, 2 * half, width)
    operands = [info, factors, singular, *own, *far, *direct]
    if older is None:
        out_shape = [
            jax.ShapeDtypeStruct(pieces, jnp.float32),
            jax.ShapeDtypeStruct((mode_count, depth), jnp.float32),
        ]
        scratch = []
    else:
        operands += older
        out_shape = [jax.ShapeDtypeStruct((rows, width), jnp.float32)]
        out_shape += [jax.ShapeDtypeStruct((rows, width), jnp.bfloat16)] * (layers - 1)
        out_shape += [
            jax.ShapeDtypeStruct((mode_count, depth // shares), jnp.float32),
            jax.ShapeDtypeStruct((shares - 1, mode_count, depth // shares), jnp.bfloat16),
        ]
        scratch = [pltpu.VMEM(pieces, jnp.float32), pltpu.VMEM((mode_count, depth), jnp.float32)]
    return call(
        functools.partial(gram_kernel, start, blocks, len(direct), len(own), older is not None),
        "gram_part",
        [SCALAR] + [FAST] * (len(operands) - 1),
        out_shape,
        scratch,
        2 * half * cells,
        *operands,
    )


def modes_kernel(parts, shares, info, factors, singular, *refs):
    direct, kept, sent = refs[:parts], refs[parts], refs[parts + 1 :]
    member, share = info[0], info[2]
    depth = direct[0].shape[1] // GROUP
    wide = depth // shares
    right = scaled_factors(factors[...], singular)
    for mask in range(GROUP):
        at = (member ^ mask) * depth + share * wide
        term = jnp.dot(right, slab(direct, at, wide), preferred_element_type=jnp.float32)
        if mask == 0:
            kept[...] = term
        else:
            sent[mask - 1][...] = term.astype(jnp.bfloat16)


def direct_part(info, factors, singular, direct, shares):
    width, cells = direct[0].shape
    shape = (factors.shape[0], cells // GROUP // shares)
    operands = [info, factors, singular, *direct]
    return call(
        functools.partial(modes_kernel, len(direct), shares),
        "direct_modes_part",
        [SCALAR] + [FAST] * (len(operands) - 1),
        [jax.ShapeDtypeStruct(shape, jnp.float32)] + [jax.ShapeDtypeStruct(shape, jnp.bfloat16)] * (GROUP - 1),
        [],
        width * cells,
        *operands,
    )


def band_matrix(width):
    near = (jnp.abs(jnp.arange(width)[:, None] - jnp.arange(width)[None, :]) == 1).astype(jnp.bfloat16)
    return jnp.concatenate([near, near])


def lookup(indices, shift_list):
    levels = jnp.arange(shift_list.shape[0], dtype=jnp.int32)
    picked = jnp.where(indices[:, None] == levels[None, :], shift_list[None, :], jnp.float32(0.0))
    return jnp.sum(picked, axis=1)


def pick(array, index, axis=0):
    return lax.dynamic_index_in_dim(array, index, axis, keepdims=False)


def after(array, *others):
    return lax.optimization_barrier((array, *others))[0]


def per_device(
    forcing_direct,
    forcing_adjoint,
    conductance,
    shift_table,
    freq_direct,
    freq_adjoint,
    left_factors,
    right_factors,
    singular_values,
):
    n_space, n_snap = lax.axis_size("space"), lax.axis_size("snap")
    rows, plane_x, width_y, width_z = forcing_direct.shape
    layers = n_space // GROUP
    block = rows * n_snap // n_space
    blocks = rows // (GROUP * block)
    mode_count = left_factors.shape[1]
    rows_y = width_y // n_snap
    weight = 1.0 / math.sqrt(plane_x * n_space * width_y * width_z)

    spot, share = lax.axis_index("space"), lax.axis_index("snap")
    layer, member = spot // GROUP, spot % GROUP
    core, high = member % 2, member // 2

    def piece_index(target):
        return ((share - target // blocks) % n_snap) * blocks + target % blocks

    info = jnp.stack(
        [member, core, share, layer] + [piece_index((layer + step) % layers) for step in range(layers)]
    ).astype(jnp.int32)

    def swap(array, mask):
        return lax.ppermute(array, "space", [(i, i ^ mask) for i in range(n_space)])

    def around(array, step):
        return lax.ppermute(array, "snap", [(i, (i + step) % n_snap) for i in range(n_snap)])

    ups = [(i, i + GROUP) for i in range(n_space - GROUP)]
    downs = [(i + GROUP, i) for i in range(n_space - GROUP)]
    upper = lambda pairs, wanted: [p for p in pairs if (p[0] % GROUP) // 2 == wanted]
    early = lambda array: lax.ppermute(array, "space", upper(ups, 1) + upper(downs, 0))
    late = lambda array: lax.ppermute(array, "space", upper(ups, 0) + upper(downs, 1))

    sizes = [rows * part // sum(CHUNKS) // 2 for part in CHUNKS]
    starts = [2 * sum(sizes[:i]) for i in range(len(sizes))]
    sets = forcing_direct.reshape(blocks, GROUP, block, width_y, width_z)
    rows_adj = forcing_adjoint.reshape(rows, width_y, width_z)
    own = lambda i: ("half", starts[i], sizes[i], False)
    cross = lambda i: ("half", starts[i], sizes[i], True)
    near_d, far_d, cross_d, own_d = pack(info, sets, conductance, info, [[("set", mask)] for mask in (2, 3, 1, 0)])
    crossed_d = swap(cross_d, 1)
    to_core, own_0, cross_0, own_1, cross_1 = pack(
        info, rows_adj, conductance, crossed_d, [[cross(0), cross(1)], [own(0)], [cross(0)], [own(1)], [cross(1)]]
    )

    wide = lambda values: jnp.broadcast_to(values[:, None], (values.shape[0], width_z))
    dir_levels = lookup(freq_direct, shift_table).reshape(blocks, GROUP, block)
    dir_shift = wide(pick(dir_levels, member, 1).reshape(-1))
    adj_levels = lookup(freq_adjoint, shift_table)
    adj_shift = [
        wide(lax.dynamic_slice_in_dim(adj_levels, at + core * size, size, 0)) for at, size in zip(starts, sizes)
    ]
    inside = lambda index: HALO + index
    below = lambda index: index - HALO
    above = lambda index: index + GROUP + HALO
    place = jnp.stack(
        [inside(member ^ k) for k in range(4)]
        + [jnp.where(high == 1, below(member ^ k), above(member ^ k)) for k in (0, 1)]
        + [jnp.where(high == 1, above(member ^ k), below(member ^ k)) for k in (2, 3)]
    ).astype(jnp.int32)
    band = band_matrix(width_z)

    y_0, y_1 = swap(near_d, 2), swap(far_d, 3)
    crossed = swap(to_core, 1)
    pair_d = join(own_d, crossed_d)
    pair_0, pair_1 = join(own_0, crossed[: sizes[0]]), join(own_1, crossed[sizes[0] :])
    e_d = early(pair_d)
    l_0, l_1 = late(y_0), late(y_1)
    y_2 = swap(after(own_0, y_1), 2)
    y_3 = swap(after(cross_0, y_0, pair_d, pair_0, pair_1), 3)
    e_0 = early(after(pair_0, y_0))
    dir_state, cond = sweep(False, place, pair_d, y_0, y_1, e_d, l_0, l_1, dir_shift, band, None, (0, block))
    dir_states = [dir_state] + [
        sweep(False, place, pair_d, y_0, y_1, e_d, l_0, l_1, dir_shift, band, cond, (i * block, block))[0]
        for i in range(1, blocks)
    ]
    dir_state = dir_states[-1]
    moved = [[around(state, step) for state in dir_states] for step in range(1, n_snap)]
    everyone = dir_states + [state for states in moved for state in states]
    l_2, l_3 = late(y_2), late(after(y_3, dir_state))
    y_4 = swap(after(own_1, y_2, l_0), 2)
    y_5 = swap(after(cross_1, y_3, dir_state), 3)
    e_1 = early(after(pair_1, y_4))
    l_4 = late(after(y_4, l_2))
    state_0 = sweep(True, place, pair_0, y_2, after(y_3, y_4, everyone[blocks]), e_0, l_2, l_3, adj_shift[0], band, cond)[0]
    other_0 = swap(state_0, 1)
    l_5 = late(after(y_5, state_0, l_4))
    part = sizes[1] // 2
    state_1 = [
        sweep(True, place, pair_1, y_4, after(y_5, everyone[-1]), e_1, l_4, l_5, adj_shift[1], band, cond, (at, part))[0]
        for at in (0, part)
    ]
    other_1 = [swap(state, 1) for state in state_1]

    singular = singular_values.reshape(1, mode_count).T
    left = lax.dynamic_slice_in_dim(left_factors.T, share * rows, rows, 1)
    right_sets = right_factors.T.reshape(mode_count, n_snap, blocks, GROUP, block)
    right_sets = pick(right_sets, member, 3).reshape(mode_count, n_snap, blocks * block)
    right = jnp.concatenate([pick(right_sets, (share - step) % n_snap, 1) for step in range(n_snap)], axis=1)
    kept, *sent = direct_part(info, right, singular, everyone, n_snap)
    for mask in range(1, GROUP):
        kept = kept + swap(sent[mask - 1], mask).astype(jnp.float32)
    direct_modes = kept.reshape(mode_count, 1, rows_y, width_z)

    outs = gram_part(info, 0, [state_0], [other_0], left, singular, everyone, blocks, None, layers)
    outs = gram_part(
        info, starts[1], state_1, other_1, left, singular, everyone, blocks, list(outs), layers
    )
    kept, *sent, kept_modes, sent_modes = outs
    for step in range(1, layers):
        pairs = [(i, (i + GROUP * step) % n_space) for i in range(n_space)]
        kept = kept + lax.ppermute(sent[step - 1], "space", pairs).astype(jnp.float32)
    gram = kept * weight
    for step in range(1, n_snap):
        kept_modes = kept_modes + around(sent_modes[step - 1], step).astype(jnp.float32)
    adjoint_modes = kept_modes.reshape(mode_count, 1, rows_y, width_z)
    return (gram, direct_modes, adjoint_modes)


def solution(mesh):
    placed = (
        P("snap", "space", None, None),
        P("snap", "space", None, None),
        P("space", None, None),
        P(),
        P("snap"),
        P("snap"),
        P(),
        P(),
        P(),
    )
    return jax.shard_map(
        per_device,
        mesh=mesh,
        in_specs=placed,
        out_specs=(
            P("snap", "space"),
            P(None, "space", "snap", None),
            P(None, "space", "snap", None),
        ),
        check_vma=False,
    )
```

time: 683 us -> 169 us (0.25)
  waiting for transfers between devices: 374 us -> 43.9 us
  starting transfers between devices: 171 us -> 50.9 us
  local copies, waits for them, and re-layouts: 69.2 us -> 18.3 us
  Pallas kernels: 0 us -> 50.5 us
  other arithmetic: 43.2 us -> 2.3 us
  between operations: 13.9 us -> 1.31 us
  matrix products: 11.9 us -> 0 us
    all_gather x1 -> x0, waiting for transfers between devices: 291 us -> none  [per_device(): column_piece = lax.all_gather(snapshots[0], 'snap', axis=0, tiled=True)]
    ppermute x4 -> x29, starting transfers between devices: 171 us -> 50.9 us  [the longest x6 28.2 us: per_device(): lax.ppermute(array, 'space', upper(ups, 0) + upper(downs, 1))]
    reduce_scatter x3 -> x0, waiting for transfers between devices: 82.8 us -> none  [the longest x1 63.4 us: per_device(): lax.psum_scatter(cross_rows, 'space', scatter_dimension=1, tiled=True)]
    slice x6 -> x1, local copies, waits for them, and re-layouts: 53.7 us -> 1.38 us  [per_device(): crossed[:sizes[0]]]
    pallas_call x0 -> x13, Pallas kernels: none -> 50.5 us  [call(): pl.pallas_call(kernel, in_specs=in_specs, out_specs=jax.tree.map(lambda _...]
    ppermute x4 -> x29, waiting for transfers between devices: 0.01 us -> 43.9 us  [the longest x14 19.6 us: swap(): return lax.ppermute(array, 'space', [(i, i ^ mask) for i in range(n_space)])]
    mul x4 -> x1, other arithmetic: 21.7 us -> 0.08 us  [per_device(): gram = kept * weight]
    convert_element_type x1 -> x0, other arithmetic: 20.7 us -> none  [per_device(): snapshots = state.astype(jnp.bfloat16)]
  transfers between devices with their start and end apart: 8 -> 29, of which waited for: 4 -> 9; matrix products, arithmetic and copies ran while one was open for 10% -> 6% of each run, Pallas kernels for 0% -> 29%
where the time goes in v2:
time: 169 us; the launch traced here: 167 us
  starting transfers between devices  50.9 us (30%)
  Pallas kernels  50.5 us (30%)
  waiting for transfers between devices  43.9 us (26%)
  local copies, waits for them, and re-layouts  18.3 us (11%)
  other arithmetic  2.3 us (1%)
    pallas_call x13, Pallas kernels, call(): pl.pallas_call(kernel, in_specs=in_specs, out_specs=jax.tree.map(lambda _...  50.5 us
    ppermute x6, starting transfers between devices, per_device(): lax.ppermute(array, 'space', upper(ups, 0) + upper(downs, 1))  28.2 us
    ppermute x14, waiting for transfers between devices, swap(): return lax.ppermute(array, 'space', [(i, i ^ mask) for i in range(n_space)])  19.6 us
    ppermute x6, waiting for transfers between devices, per_device(): lax.ppermute(array, 'space', upper(ups, 0) + upper(downs, 1))  17.4 us
    unnamed x45, local copies, waits for them, and re-layouts  10.8 us
    ppermute x14, starting transfers between devices, swap(): return lax.ppermute(array, 'space', [(i, i ^ mask) for i in range(n_space)])  8.89 us
    ppermute x3, starting transfers between devices, per_device(): lax.ppermute(sent[step - 1], 'space', pairs).astype(jnp.float32)  7.23 us
    ppermute x3, waiting for transfers between devices, per_device(): lax.ppermute(sent[step - 1], 'space', pairs).astype(jnp.float32)  4.03 us
  transfers between devices with their start and end apart: 29, of which 9 were waited for; matrix products, arithmetic and copies ran while one was open for 6% of the time, Pallas kernels for 29%

profile of v2, /device:TPU:0, one launch (start us, length us, event | category | flops | bytes accessed | tf_op | source)
XLA Modules:
  0.0 167.1 jit_solution(15186369530238195628)
XLA Ops:
  0.9 0.1 stack.62.info.token
  1.0 1.6 copy-done.4
  2.6 0.7 copy-done.13
  3.3 0.9 pack.2
  4.2 0.5 collective-permute-start
  4.7 1.6 collective-permute-done.token.refs_1_
  6.3 1.6 pack.3
  8.0 0.8 copy-done.15
  8.8 0.4 collective-permute-start.1
  9.2 2.7 %collective-permute-start.4 = (bf16[132,16,128]{2,1,0:T(8,128)(2,1)S(1)}, bf16[132,16,128]{2,1,0:T(8,128)(2,1)}, u32[]{:S(2)}, u32[]{:S(2)}) collective-permute-start(bf16[132,16,128]{2,1,0:T(8,128)(2,1)S(1)} %get-tuple-element.43), channel_id=1, source_target_pairs={{0,4},{2,6},{4,0},{6,2},{8,12},{10,14},{12,8},{14,10},{16,20},{18,... | collective-permute-start | bytes 1622024 | tf_op jit(solution)/shard_map/ppermute | solution.py:396
  11.9 1.3 collective-permute-start.8
  13.2 11.8 %collective-permute-done.4.refs_1_ = bf16[132,16,128]{2,1,0:T(8,128)(2,1)} collective-permute-done((bf16[132,16,128]{2,1,0:T(8,128)(2,1)S(1)}, bf16[132,16,128]{2,1,0:T(8,128)(2,1)}, u32[]{:S(2)}, u32[]{:S(2)}) %collective-permute-start.4) | collective-permute-done | bytes 540704 | tf_op jit(solution)/shard_map/ppermute | solution.py:396
  25.0 4.7 %collective-permute-start.5 = (bf16[132,16,128]{2,1,0:T(8,128)(2,1)}, bf16[132,16,128]{2,1,0:T(8,128)(2,1)}, u32[]{:S(2)}, u32[]{:S(2)}) collective-permute-start(bf16[132,16,128]{2,1,0:T(8,128)(2,1)} %collective-permute-done.4.refs_1_), channel_id=1, source_target_pairs={{0,8},{2,10},{8,16},{10,18},{16,24},{18,26},{12,4},{14,6},{20,12},... | collective-permute-start | bytes 1622024 | tf_op jit(solution)/shard_map/ppermute | solution.py:405
  29.8 6.2 %collective-permute-done.2.refs_2_ = bf16[132,16,128]{2,1,0:T(8,128)(2,1)} collective-permute-done((bf16[132,16,128]{2,1,0:T(8,128)(2,1)S(1)}, bf16[132,16,128]{2,1,0:T(8,128)(2,1)}, u32[]{:S(2)}, u32[]{:S(2)}) %collective-permute-start.2) | collective-permute-done | bytes 540704 | tf_op jit(solution)/shard_map/ppermute | solution.py:396
  36.0 4.3 %collective-permute-start.9 = (bf16[132,16,128]{2,1,0:T(8,128)(2,1)}, bf16[132,16,128]{2,1,0:T(8,128)(2,1)}, u32[]{:S(2)}, u32[]{:S(2)}) collective-permute-start(bf16[132,16,128]{2,1,0:T(8,128)(2,1)} %collective-permute-done.2.refs_2_), channel_id=1, source_target_pairs={{0,8},{2,10},{8,16},{10,18},{16,24},{18,26},{12,4},{14,6},{20,12},... | collective-permute-start | bytes 1622024 | tf_op jit(solution)/shard_map/ppermute | solution.py:405
  40.3 0.1 select_reduce_fusion
  40.8 1.4 fusion.1
  42.2 1.1 join.5.refs_0_
  43.3 1.1 join.3.refs_0_
  44.5 1.0 copy-done.8
  45.4 1.7 %collective-permute-start.7 = (bf16[128,16,128]{2,1,0:T(8,128)(2,1)S(1)}, bf16[128,16,128]{2,1,0:T(8,128)(2,1)}, u32[]{:S(2)}, u32[]{:S(2)}) collective-permute-start(bf16[128,16,128]{2,1,0:T(8,128)(2,1)S(1)} %copy-done.16), channel_id=1, source_target_pairs={{0,6},{2,4},{4,2},{6,0},{8,14},{10,12},{12,10},{14,8},{16,22},{18,... | collective-permute-start | bytes 1572872 | tf_op jit(solution)/shard_map/ppermute | solution.py:396
  47.1 5.0 %collective-permute-done.9.refs_5_ = bf16[132,16,128]{2,1,0:T(8,128)(2,1)} collective-permute-done((bf16[132,16,128]{2,1,0:T(8,128)(2,1)}, bf16[132,16,128]{2,1,0:T(8,128)(2,1)}, u32[]{:S(2)}, u32[]{:S(2)}) %collective-permute-start.9) | collective-permute-done | bytes 540704 | tf_op jit(solution)/shard_map/ppermute | solution.py:405
  52.2 5.9 %direct_sweeps.2 = (bf16[64,8192]{1,0:T(8,128)(2,1)S(1)}, f32[8,16,128]{2,1,0:T(8,128)S(1)}) custom-call(s32[8]{0:T(128)S(1)} %stack.71.place, bf16[264,16,128]{2,1,0:T(8,128)(2,1)S(1)} %join.4.refs_0_, bf16[132,16,128]{2,1,0:T(8,128)(2,1)} %collective-permute-done.4.refs_1_, bf16[132,16,128]{2,1,0:T(8,128)(2,1)} %collective-permute-done.2.refs_2_, ...), custom_call_target="tpu_custom_call" | custom-call | flops 5242880000 | bytes 1024 | tf_op jit(solution)/shard_map/direct_sweeps/pallas_call | solution.py:25
  58.1 1.6 collective-permute-start.15
  59.7 1.3 collective-permute-start.16
  61.0 5.8 %collective-permute-start.13 = (bf16[128,16,128]{2,1,0:T(8,128)(2,1)}, bf16[128,16,128]{2,1,0:T(8,128)(2,1)}, u32[]{:S(2)}, u32[]{:S(2)}) collective-permute-start(bf16[128,16,128]{2,1,0:T(8,128)(2,1)} %collective-permute-done.3.refs_1_), channel_id=1, source_target_pairs={{0,8},{2,10},{8,16},{10,18},{16,24},{18,26},{12,4},{14,6},{20,12},... | collective-permute-start | bytes 1572872 | tf_op jit(solution)/shard_map/ppermute | solution.py:405
  66.8 1.1 collective-permute-start.6
  67.9 1.2 copy-done.7
  69.1 5.9 %direct_sweeps.3.refs_3_.refs_5_.refs_1_ = bf16[64,8192]{1,0:T(8,128)(2,1)S(1)} custom-call(s32[8]{0:T(128)S(1)} %stack.71.place, bf16[264,16,128]{2,1,0:T(8,128)(2,1)S(1)} %copy-done.7, bf16[132,16,128]{2,1,0:T(8,128)(2,1)} %collective-permute-done.4.refs_1_, bf16[132,16,128]{2,1,0:T(8,128)(2,1)} %collective-permute-done.2.refs_2_, ...), custom_call_target="tpu_custom_call" | custom-call | flops 5242880000 | bytes 1024 | tf_op jit(solution)/shard_map/direct_sweeps/pallas_call | solution.py:25
  75.0 5.3 %collective-permute-start.17 = (bf16[128,16,128]{2,1,0:T(8,128)(2,1)}, bf16[128,16,128]{2,1,0:T(8,128)(2,1)}, u32[]{:S(2)}, u32[]{:S(2)}) collective-permute-start(bf16[128,16,128]{2,1,0:T(8,128)(2,1)} %collective-permute-done.7.refs_2_), channel_id=1, source_target_pairs={{0,8},{2,10},{8,16},{10,18},{16,24},{18,26},{12,4},{14,6},{20,12},... | collective-permute-start | bytes 1572872 | tf_op jit(solution)/shard_map/ppermute | solution.py:405
  80.4 3.4 %collective-permute-start.14 = (bf16[128,16,128]{2,1,0:T(8,128)(2,1)}, bf16[128,16,128]{2,1,0:T(8,128)(2,1)S(1)}, u32[]{:S(2)}, u32[]{:S(2)}) collective-permute-start(bf16[128,16,128]{2,1,0:T(8,128)(2,1)} %collective-permute-done.6.refs_1_), channel_id=1, source_target_pairs={{0,8},{2,10},{8,16},{10,18},{16,24},{18,26},{12,4},{14,6},{20,12},... | collective-permute-start | bytes 1572872 | tf_op jit(solution)/shard_map/ppermute | solution.py:405
  83.8 1.3 collective-permute-start.12
  85.1 0.6 collective-permute-start.11
  85.7 1.9 %collective-permute-done.16.refs_3_ = bf16[256,16,128]{2,1,0:T(8,128)(2,1)} collective-permute-done((bf16[256,16,128]{2,1,0:T(8,128)(2,1)}, bf16[256,16,128]{2,1,0:T(8,128)(2,1)}, u32[]{:S(2)}, u32[]{:S(2)}) %collective-permute-start.16) | collective-permute-done | bytes 1048608 | tf_op jit(solution)/shard_map/ppermute | solution.py:404
  87.7 4.6 %collective-permute-done.17.refs_5_ = bf16[128,16,128]{2,1,0:T(8,128)(2,1)} collective-permute-done((bf16[128,16,128]{2,1,0:T(8,128)(2,1)}, bf16[128,16,128]{2,1,0:T(8,128)(2,1)}, u32[]{:S(2)}, u32[]{:S(2)}) %collective-permute-start.17) | collective-permute-done | bytes 524320 | tf_op jit(solution)/shard_map/ppermute | solution.py:405
  92.3 11.7 %adjoint_sweeps.3.refs_0_ = bf16[128,8192]{1,0:T(8,128)(2,1)} custom-call(s32[8]{0:T(128)S(1)} %stack.71.place, bf16[256,16,128]{2,1,0:T(8,128)(2,1)} %join.5.refs_0_, bf16[128,16,128]{2,1,0:T(8,128)(2,1)} %collective-permute-done.3.refs_1_, bf16[128,16,128]{2,1,0:T(8,128)(2,1)} %collective-permute-done.7.refs_2_, ...), custom_call_target="tpu_custom_call" | custom-call | flops 10485760000 | bytes 1024 | tf_op jit(solution)/shard_map/adjoint_sweeps/pallas_call | solution.py:25
  104.0 4.6 %collective-permute-start.18 = (bf16[128,16,128]{2,1,0:T(8,128)(2,1)S(1)}, bf16[128,16,128]{2,1,0:T(8,128)(2,1)S(1)}, u32[]{:S(2)}, u32[]{:S(2)}) collective-permute-start(bf16[128,16,128]{2,1,0:T(8,128)(2,1)S(1)} %collective-permute-done.10.refs_2_), channel_id=1, source_target_pairs={{0,8},{2,10},{8,16},{10,18},{16,24},{18,26},{12,4},{14,6},{20,12},... | collective-permute-start | bytes 1572872 | tf_op jit(solution)/shard_map/ppermute | solution.py:405
  108.7 0.9 collective-permute-done.12.refs_3_
  109.6 7.9 %collective-permute-done.18.refs_5_ = bf16[128,16,128]{2,1,0:T(8,128)(2,1)S(1)} collective-permute-done((bf16[128,16,128]{2,1,0:T(8,128)(2,1)S(1)}, bf16[128,16,128]{2,1,0:T(8,128)(2,1)S(1)}, u32[]{:S(2)}, u32[]{:S(2)}) %collective-permute-start.18) | collective-permute-done | bytes 524320 | tf_op jit(solution)/shard_map/ppermute | solution.py:405
  117.5 6.2 %adjoint_sweeps.5.refs_1_ = bf16[64,8192]{1,0:T(8,128)(2,1)} custom-call(s32[8]{0:T(128)S(1)} %stack.71.place, bf16[256,16,128]{2,1,0:T(8,128)(2,1)S(1)} %copy-done.9, bf16[128,16,128]{2,1,0:T(8,128)(2,1)} %collective-permute-done.6.refs_1_, bf16[128,16,128]{2,1,0:T(8,128)(2,1)S(1)} %collective-permute-done.10.refs_2_, ...), custom_call_target="tpu_custom_call" | custom-call | flops 5242880000 | bytes 1024 | tf_op jit(solution)/shard_map/adjoint_sweeps/pallas_call | solution.py:25
  123.7 6.1 %adjoint_sweeps.4.refs_0_ = bf16[64,8192]{1,0:T(8,128)(2,1)} custom-call(s32[8]{0:T(128)S(1)} %stack.71.place, bf16[256,16,128]{2,1,0:T(8,128)(2,1)S(1)} %copy-done.9, bf16[128,16,128]{2,1,0:T(8,128)(2,1)} %collective-permute-done.6.refs_1_, bf16[128,16,128]{2,1,0:T(8,128)(2,1)S(1)} %collective-permute-done.10.refs_2_, ...), custom_call_target="tpu_custom_call" | custom-call | flops 5242880000 | bytes 1024 | tf_op jit(solution)/shard_map/adjoint_sweeps/pallas_call | solution.py:25
  129.8 0.5 collective-permute-start.19
  130.3 0.1 copy.27.singular
  130.4 2.1 %reshape.38 = f32[64,2,2,4,64]{4,3,2,1,0:T(4,128)} reshape(f32[64,1024]{1,0:T(8,128)} %bitcast.45) | data formatting | bytes 524288 | tf_op jit(solution)/shard_map/reshape | solution.py:470
  132.5 2.2 %dynamic-slice_reduce_fusion = f32[64,2,2,64]{3,2,1,0:T(2,128)} fusion(f32[64,2,2,4,64]{4,3,2,1,0:T(4,128)} %reshape.38, s32[]{:T(128)S(6)} %select_n.153), kind=kLoop, calls=%fused_computation.3 | loop fusion | bytes 131076 | tf_op jit(solution)/shard_map/jit(dynamic_index_in_dim)/dynamic_slice | solution.py:357
  134.7 1.1 reshape.42
  135.8 1.2 copy-done.2
  137.0 1.7 %direct_modes_part.1 = (f32[64,1024]{1,0:T(8,128)S(1)}, bf16[64,1024]{1,0:T(8,128)(2,1)}, bf16[64,1024]{1,0:T(8,128)(2,1)}, bf16[64,1024]{1,0:T(8,128)(2,1)}) custom-call(s32[8]{0:T(128)S(1)} %stack.62.info.token, f32[64,256]{1,0:T(8,128)S(1)} %pad_maximum_fusion.factors, f32[64,1]{1,0:T(8,128)S(1)} %copy.27.singular, ...), custom_call_target="tpu_custom_call" | custom-call | flops 524288 | bytes 1024 | tf_op jit(solution)/shard_map/direct_modes_part/pallas_call | solution.py:25
  138.8 0.7 copy-done.10
  139.5 1.4 collective-permute-start.26
  140.9 0.4 collective-permute-start.27
  141.4 1.2 copy-done.3
  142.6 3.8 %gram_part.2 = (f32[4,256,64]{2,1,0:T(8,128)S(1)}, f32[64,2048]{1,0:T(8,128)S(1)}) custom-call(s32[8]{0:T(128)S(1)} %stack.62.info.token, f32[64,512]{1,0:T(8,128)S(1)} %dynamic-slice_bitcast_fusion.factors, f32[64,1]{1,0:T(8,128)S(1)} %copy.27.singular, bf16[128,8192]{1,0:T(8,128)(2,1)} %adjoint_sweeps.3.refs_0_, ...), custom_call_target="tpu_custom_call" | custom-call | flops 2097152 | bytes 1024 | tf_op jit(solution)/shard_map/gram_part/pallas_call | solution.py:25
  146.4 4.4 %gram_part.3 = (f32[512,64]{1,0:T(8,128)S(1)}, bf16[512,64]{1,0:T(8,128)(2,1)S(1)}, bf16[512,64]{1,0:T(8,128)(2,1)S(1)}, bf16[512,64]{1,0:T(8,128)(2,1)S(1)}, f3...) custom-call(s32[8]{0:T(128)S(1)} %stack.62.info.token, f32[64,512]{1,0:T(8,128)S(1)} %dynamic-slice_bitcast_fusion.factors, ...), custom_call_target="tpu_custom_call" | custom-call | flops 2097152 | bytes 1024 | tf_op jit(solution)/shard_map/gram_part/pallas_call | solution.py:25
  150.8 2.5 %collective-permute-start.22 = (bf16[512,64]{1,0:T(8,128)(2,1)S(1)}, bf16[512,64]{1,0:T(8,128)(2,1)S(1)}, u32[]{:S(2)}, u32[]{:S(2)}) collective-permute-start(bf16[512,64]{1,0:T(8,128)(2,1)S(1)} %get-tuple-element.62), channel_id=1, source_target_pairs={{0,8},{2,10},{4,12},{6,14},{8,16},{10,18},{12,20},{14,22},{16,24},... | collective-permute-start | bytes 196616 | tf_op jit(solution)/shard_map/ppermute | solution.py:485
  153.3 2.1 %collective-permute-start.23 = (bf16[512,64]{1,0:T(8,128)(2,1)S(1)}, bf16[512,64]{1,0:T(8,128)(2,1)S(1)}, u32[]{:S(2)}, u32[]{:S(2)}) collective-permute-start(bf16[512,64]{1,0:T(8,128)(2,1)S(1)} %get-tuple-element.63), channel_id=1, source_target_pairs={{0,16},{2,18},{4,20},{6,22},{8,24},{10,26},{12,28},{14,30},{16,0},... | collective-permute-start | bytes 196616 | tf_op jit(solution)/shard_map/ppermute | solution.py:485
  155.4 2.6 %collective-permute-start.24 = (bf16[512,64]{1,0:T(8,128)(2,1)S(1)}, bf16[512,64]{1,0:T(8,128)(2,1)S(1)}, u32[]{:S(2)}, u32[]{:S(2)}) collective-permute-start(bf16[512,64]{1,0:T(8,128)(2,1)S(1)} %get-tuple-element.64), channel_id=1, source_target_pairs={{0,24},{2,26},{4,28},{6,30},{8,0},{10,2},{12,4},{14,6},{16,8},{18,... | collective-permute-start | bytes 196616 | tf_op jit(solution)/shard_map/ppermute | solution.py:485
  158.1 1.1 add_bitcast_fusion.1
  159.2 0.8 copy.36
  159.9 0.5 collective-permute-start.28
  160.5 4.0 %collective-permute-done.23 = bf16[512,64]{1,0:T(8,128)(2,1)S(1)} collective-permute-done((bf16[512,64]{1,0:T(8,128)(2,1)S(1)}, bf16[512,64]{1,0:T(8,128)(2,1)S(1)}, u32[]{:S(2)}, u32[]{:S(2)}) %collective-permute-start.23) | collective-permute-done | bytes 65568 | tf_op jit(solution)/shard_map/ppermute | solution.py:485
  164.6 0.8 copy.30
  165.4 1.0 add_bitcast_fusion
  166.3 0.8 copy.37
  (75 shorter events, 1.1 us)
Async XLA Ops:
  0.6 140.7 %copy-start = (f32[1024,64]{0,1:T(8,128)S(1)}, f32[1024,64]{0,1:T(8,128)}, u32[]{:S(2)}) copy-start(f32[1024,64]{0,1:T(8,128)} %param.15) | copy-start | bytes 786436
  1.0 1.6 copy-start.4
  2.6 0.7 copy-start.13
  3.3 3.0 %copy-start.5 = (bf16[512,1,16,128]{3,2,1,0:T(8,128)(2,1)S(1)}, bf16[512,1,16,128]{3,2,1,0:T(8,128)(2,1)}, u32[]{:S(2)}) copy-start(bf16[512,1,16,128]{3,2,1,0:T(8,128)(2,1)} %param.10) | copy-start | bytes 6291460
  4.2 2.1 %collective-permute-start = (bf16[132,16,128]{2,1,0:T(8,128)(2,1)S(1)}, bf16[132,16,128]{2,1,0:T(8,128)(2,1)S(1)}, u32[]{:S(2)}, u32[]{:S(2)}) collective-permute-start(bf16[132,16,128]{2,1,0:T(8,128)(2,1)S(1)} %get-tuple-element.37), channel_id=1, source_target_pairs={{0,2},{2,0},{4,6},{6,4},{8,10},{10,8},{12,14},{14,12},{16,18},{18,... | collective-permute-start | bytes 1622024 | tf_op jit(solution)/shard_map/ppermute | solution.py:396
  6.3 34.0 %copy-start.17 = (s32[512]{0:T(512)S(1)}, s32[512]{0:T(512)}, u32[]{:S(2)}) copy-start(s32[512]{0:T(512)} %param.14) | copy-start | bytes 6148
  6.3 34.0 %copy-start.18 = (s32[512]{0:T(512)S(1)}, s32[512]{0:T(512)}, u32[]{:S(2)}) copy-start(s32[512]{0:T(512)} %param.13) | copy-start | bytes 6148
  6.3 34.0 %copy-start.20 = (f32[16]{0:T(128)S(1)}, f32[16]{0:T(128)}, u32[]{:S(2)}) copy-start(f32[16]{0:T(128)} %param.12) | copy-start | bytes 196
  8.0 0.8 copy-start.15
  8.8 27.2 %copy-start.14 = (bf16[128,16,128]{2,1,0:T(8,128)(2,1)}, bf16[128,16,128]{2,1,0:T(8,128)(2,1)S(1)}, u32[]{:S(2)}) copy-start(bf16[128,16,128]{2,1,0:T(8,128)(2,1)S(1)} %get-tuple-element.50) | copy-start | bytes 1572868
  8.8 32.0 %collective-permute-start.1 = (bf16[256,16,128]{2,1,0:T(8,128)(2,1)S(1)}, bf16[256,16,128]{2,1,0:T(8,128)(2,1)}, u32[]{:S(2)}, u32[]{:S(2)}) collective-permute-start(bf16[256,16,128]{2,1,0:T(8,128)(2,1)S(1)} %get-tuple-element.39), channel_id=1, source_target_pairs={{0,2},{2,0},{4,6},{6,4},{8,10},{10,8},{12,14},{14,12},{16,18},{18,... | collective-permute-start | bytes 3145736 | tf_op jit(solution)/shard_map/ppermute | solution.py:396
  9.2 15.9 %collective-permute-start.4 = (bf16[132,16,128]{2,1,0:T(8,128)(2,1)S(1)}, bf16[132,16,128]{2,1,0:T(8,128)(2,1)}, u32[]{:S(2)}, u32[]{:S(2)}) collective-permute-start(bf16[132,16,128]{2,1,0:T(8,128)(2,1)S(1)} %get-tuple-element.43), channel_id=1, source_target_pairs={{0,4},{2,6},{4,0},{6,2},{8,12},{10,14},{12,8},{14,10},{16,20},{18,... | collective-permute-start | bytes 1622024 | tf_op jit(solution)/shard_map/ppermute | solution.py:396
  11.8 24.2 %collective-permute-start.2 = (bf16[132,16,128]{2,1,0:T(8,128)(2,1)S(1)}, bf16[132,16,128]{2,1,0:T(8,128)(2,1)}, u32[]{:S(2)}, u32[]{:S(2)}) collective-permute-start(bf16[132,16,128]{2,1,0:T(8,128)(2,1)S(1)} %get-tuple-element.41), channel_id=1, source_target_pairs={{0,6},{2,4},{4,2},{6,0},{8,14},{10,12},{12,10},{14,8},{16,22},{18,... | collective-permute-start | bytes 1622024 | tf_op jit(solution)/shard_map/ppermute | solution.py:396
  11.9 40.3 %copy-start.6 = (bf16[264,16,128]{2,1,0:T(8,128)(2,1)}, bf16[264,16,128]{2,1,0:T(8,128)(2,1)S(1)}, u32[]{:S(2)}) copy-start(bf16[264,16,128]{2,1,0:T(8,128)(2,1)S(1)} %join.4.refs_0_) | copy-start | bytes 3244036
  11.9 40.2 %collective-permute-start.8 = (bf16[264,16,128]{2,1,0:T(8,128)(2,1)S(1)}, bf16[264,16,128]{2,1,0:T(8,128)(2,1)}, u32[]{:S(2)}, u32[]{:S(2)}) collective-permute-start(bf16[264,16,128]{2,1,0:T(8,128)(2,1)S(1)} %join.4.refs_0_), channel_id=1, source_target_pairs={{4,12},{6,14},{12,20},{14,22},{20,28},{22,30},{8,0},{10,2},{16,8},... | collective-permute-start | bytes 3244040 | tf_op jit(solution)/shard_map/ppermute | solution.py:404
  25.0 22.1 %collective-permute-start.5 = (bf16[132,16,128]{2,1,0:T(8,128)(2,1)}, bf16[132,16,128]{2,1,0:T(8,128)(2,1)}, u32[]{:S(2)}, u32[]{:S(2)}) collective-permute-start(bf16[132,16,128]{2,1,0:T(8,128)(2,1)} %collective-permute-done.4.refs_1_), channel_id=1, source_target_pairs={{0,8},{2,10},{8,16},{10,18},{16,24},{18,26},{12,4},{14,6},{20,12},... | collective-permute-start | bytes 1622024 | tf_op jit(solution)/shard_map/ppermute | solution.py:405
  36.0 16.1 %collective-permute-start.9 = (bf16[132,16,128]{2,1,0:T(8,128)(2,1)}, bf16[132,16,128]{2,1,0:T(8,128)(2,1)}, u32[]{:S(2)}, u32[]{:S(2)}) collective-permute-start(bf16[132,16,128]{2,1,0:T(8,128)(2,1)} %collective-permute-done.2.refs_2_), channel_id=1, source_target_pairs={{0,8},{2,10},{8,16},{10,18},{16,24},{18,26},{12,4},{14,6},{20,12},... | collective-permute-start | bytes 1622024 | tf_op jit(solution)/shard_map/ppermute | solution.py:405
  40.7 20.2 %collective-permute-start.3 = (bf16[128,16,128]{2,1,0:T(8,128)(2,1)S(1)}, bf16[128,16,128]{2,1,0:T(8,128)(2,1)}, u32[]{:S(2)}, u32[]{:S(2)}) collective-permute-start(bf16[128,16,128]{2,1,0:T(8,128)(2,1)S(1)} %get-tuple-element.42.refs_0_), channel_id=1, source_target_pairs={{0,4},{2,6},{4,0},{6,2},{8,12},{10,14},{12,8},{14,10},{16,20},{18,... | collective-permute-start | bytes 1572872 | tf_op jit(solution)/shard_map/ppermute | solution.py:396
  42.2 3.2 %copy-start.16 = (bf16[128,16,128]{2,1,0:T(8,128)(2,1)S(1)}, bf16[128,16,128]{2,1,0:T(8,128)(2,1)}, u32[]{:S(2)}) copy-start(bf16[128,16,128]{2,1,0:T(8,128)(2,1)} %copy-done.15) | copy-start | bytes 1572868
  44.4 1.0 copy-start.8
  45.4 29.5 %collective-permute-start.7 = (bf16[128,16,128]{2,1,0:T(8,128)(2,1)S(1)}, bf16[128,16,128]{2,1,0:T(8,128)(2,1)}, u32[]{:S(2)}, u32[]{:S(2)}) collective-permute-start(bf16[128,16,128]{2,1,0:T(8,128)(2,1)S(1)} %copy-done.16), channel_id=1, source_target_pairs={{0,6},{2,4},{4,2},{6,0},{8,14},{10,12},{12,10},{14,8},{16,22},{18,... | collective-permute-start | bytes 1572872 | tf_op jit(solution)/shard_map/ppermute | solution.py:396
  58.1 27.0 %collective-permute-start.15 = (bf16[64,8192]{1,0:T(8,128)(2,1)S(1)}, bf16[64,8192]{1,0:T(8,128)(2,1)S(1)}, u32[]{:S(2)}, u32[]{:S(2)}) collective-permute-start(bf16[64,8192]{1,0:T(8,128)(2,1)S(1)} %get-tuple-element.54.refs_2_.refs_4_.refs_0_), channel_id=1, source_target_pairs={{0,1},{1,0},{2,3},{3,2},{4,5},{5,4},{6,7},{7,6},{8,9},{9,8},{10,11... | collective-permute-start | bytes 3145736 | tf_op jit(solution)/shard_map/ppermute | solution.py:399
  59.7 28.0 %collective-permute-start.16 = (bf16[256,16,128]{2,1,0:T(8,128)(2,1)}, bf16[256,16,128]{2,1,0:T(8,128)(2,1)}, u32[]{:S(2)}, u32[]{:S(2)}) collective-permute-start(bf16[256,16,128]{2,1,0:T(8,128)(2,1)} %join.5.refs_0_), channel_id=1, source_target_pairs={{4,12},{6,14},{12,20},{14,22},{20,28},{22,30},{8,0},{10,2},{16,8},... | collective-permute-start | bytes 3145736 | tf_op jit(solution)/shard_map/ppermute | solution.py:404
  61.0 19.4 %collective-permute-start.13 = (bf16[128,16,128]{2,1,0:T(8,128)(2,1)}, bf16[128,16,128]{2,1,0:T(8,128)(2,1)}, u32[]{:S(2)}, u32[]{:S(2)}) collective-permute-start(bf16[128,16,128]{2,1,0:T(8,128)(2,1)} %collective-permute-done.3.refs_1_), channel_id=1, source_target_pairs={{0,8},{2,10},{8,16},{10,18},{16,24},{18,26},{12,4},{14,6},{20,12},... | collective-permute-start | bytes 1572872 | tf_op jit(solution)/shard_map/ppermute | solution.py:405
  66.8 13.6 %collective-permute-start.6 = (bf16[128,16,128]{2,1,0:T(8,128)(2,1)}, bf16[128,16,128]{2,1,0:T(8,128)(2,1)}, u32[]{:S(2)}, u32[]{:S(2)}) collective-permute-start(bf16[128,16,128]{2,1,0:T(8,128)(2,1)} %get-tuple-element.44.refs_0_), channel_id=1, source_target_pairs={{0,4},{2,6},{4,0},{6,2},{8,12},{10,14},{12,8},{14,10},{16,20},{18,... | collective-permute-start | bytes 1572872 | tf_op jit(solution)/shard_map/ppermute | solution.py:396
  67.9 1.2 copy-start.7
  75.0 17.2 %collective-permute-start.17 = (bf16[128,16,128]{2,1,0:T(8,128)(2,1)}, bf16[128,16,128]{2,1,0:T(8,128)(2,1)}, u32[]{:S(2)}, u32[]{:S(2)}) collective-permute-start(bf16[128,16,128]{2,1,0:T(8,128)(2,1)} %collective-permute-done.7.refs_2_), channel_id=1, source_target_pairs={{0,8},{2,10},{8,16},{10,18},{16,24},{18,26},{12,4},{14,6},{20,12},... | collective-permute-start | bytes 1572872 | tf_op jit(solution)/shard_map/ppermute | solution.py:405
  80.4 23.5 %collective-permute-start.14 = (bf16[128,16,128]{2,1,0:T(8,128)(2,1)}, bf16[128,16,128]{2,1,0:T(8,128)(2,1)S(1)}, u32[]{:S(2)}, u32[]{:S(2)}) collective-permute-start(bf16[128,16,128]{2,1,0:T(8,128)(2,1)} %collective-permute-done.6.refs_1_), channel_id=1, source_target_pairs={{0,8},{2,10},{8,16},{10,18},{16,24},{18,26},{12,4},{14,6},{20,12},... | collective-permute-start | bytes 1572872 | tf_op jit(solution)/shard_map/ppermute | solution.py:405
  83.8 25.7 %collective-permute-start.12 = (bf16[256,16,128]{2,1,0:T(8,128)(2,1)}, bf16[256,16,128]{2,1,0:T(8,128)(2,1)S(1)}, u32[]{:S(2)}, u32[]{:S(2)}) collective-permute-start(bf16[256,16,128]{2,1,0:T(8,128)(2,1)} %copy-done.8), channel_id=1, source_target_pairs={{4,12},{6,14},{12,20},{14,22},{20,28},{22,30},{8,0},{10,2},{16,8},... | collective-permute-start | bytes 3145736 | tf_op jit(solution)/shard_map/ppermute | solution.py:404
  85.1 23.5 %collective-permute-start.11 = (bf16[64,8192]{1,0:T(8,128)(2,1)S(1)}, bf16[64,8192]{1,0:T(8,128)(2,1)S(1)}, u32[]{:S(2)}, u32[]{:S(2)}) collective-permute-start(bf16[64,8192]{1,0:T(8,128)(2,1)S(1)} %direct_sweeps.3.refs_3_.refs_5_.refs_1_), channel_id=1, source_target_pairs={{0,1},{1,0},{2,3},{3,2},{4,5},{5,4},{6,7},{7,6},{8,9},{9,8},{10,11... | collective-permute-start | bytes 3145736 | tf_op jit(solution)/shard_map/ppermute | solution.py:399
  87.6 16.3 %collective-permute-start.10 = (bf16[128,16,128]{2,1,0:T(8,128)(2,1)}, bf16[128,16,128]{2,1,0:T(8,128)(2,1)S(1)}, u32[]{:S(2)}, u32[]{:S(2)}) collective-permute-start(bf16[128,16,128]{2,1,0:T(8,128)(2,1)} %copy-done.14), channel_id=1, source_target_pairs={{0,6},{2,4},{4,2},{6,0},{8,14},{10,12},{12,10},{14,8},{16,22},{18,... | collective-permute-start | bytes 1572872 | tf_op jit(solution)/shard_map/ppermute | solution.py:396
  92.3 25.2 %copy-start.9 = (bf16[256,16,128]{2,1,0:T(8,128)(2,1)S(1)}, bf16[256,16,128]{2,1,0:T(8,128)(2,1)}, u32[]{:S(2)}) copy-start(bf16[256,16,128]{2,1,0:T(8,128)(2,1)} %copy-done.8) | copy-start | bytes 3145732
  104.0 13.5 %collective-permute-start.18 = (bf16[128,16,128]{2,1,0:T(8,128)(2,1)S(1)}, bf16[128,16,128]{2,1,0:T(8,128)(2,1)S(1)}, u32[]{:S(2)}, u32[]{:S(2)}) collective-permute-start(bf16[128,16,128]{2,1,0:T(8,128)(2,1)S(1)} %collective-permute-done.10.refs_2_), channel_id=1, source_target_pairs={{0,8},{2,10},{8,16},{10,18},{16,24},{18,26},{12,4},{14,6},{20,12},... | collective-permute-start | bytes 1572872 | tf_op jit(solution)/shard_map/ppermute | solution.py:405
  108.6 32.3 %collective-permute-start.21 = (bf16[128,8192]{1,0:T(8,128)(2,1)}, bf16[128,8192]{1,0:T(8,128)(2,1)}, u32[]{:S(2)}, u32[]{:S(2)}) collective-permute-start(bf16[128,8192]{1,0:T(8,128)(2,1)} %adjoint_sweeps.3.refs_0_), channel_id=1, source_target_pairs={{0,2},{2,0},{4,6},{6,4},{8,10},{10,8},{12,14},{14,12},{16,18},{18,... | collective-permute-start | bytes 6291464 | tf_op jit(solution)/shard_map/ppermute | solution.py:396
  108.7 15.0 %copy-start.1 = (bf16[64,8192]{1,0:T(8,128)(2,1)}, bf16[64,8192]{1,0:T(8,128)(2,1)S(1)}, u32[]{:S(2)}) copy-start(bf16[64,8192]{1,0:T(8,128)(2,1)S(1)} %collective-permute-done.11.refs_5_.refs_7_.refs_3_) | copy-start | bytes 3145732
  123.7 6.6 %copy-start.19 = (f32[64]{0:T(128)S(1)}, f32[64]{0:T(128)}, u32[]{:S(2)}) copy-start(f32[64]{0:T(128)} %param.17) | copy-start | bytes 772
  123.7 22.6 %collective-permute-start.20 = (bf16[64,8192]{1,0:T(8,128)(2,1)}, bf16[64,8192]{1,0:T(8,128)(2,1)}, u32[]{:S(2)}, u32[]{:S(2)}) collective-permute-start(bf16[64,8192]{1,0:T(8,128)(2,1)} %adjoint_sweeps.5.refs_1_), channel_id=1, source_target_pairs={{0,2},{2,0},{4,6},{6,4},{8,10},{10,8},{12,14},{14,12},{16,18},{18,... | collective-permute-start | bytes 3145736 | tf_op jit(solution)/shard_map/ppermute | solution.py:396
  129.8 16.5 %collective-permute-start.19 = (bf16[64,8192]{1,0:T(8,128)(2,1)}, bf16[64,8192]{1,0:T(8,128)(2,1)}, u32[]{:S(2)}, u32[]{:S(2)}) collective-permute-start(bf16[64,8192]{1,0:T(8,128)(2,1)} %adjoint_sweeps.4.refs_0_), channel_id=1, source_target_pairs={{0,2},{2,0},{4,6},{6,4},{8,10},{10,8},{12,14},{14,12},{16,18},{18,... | collective-permute-start | bytes 3145736 | tf_op jit(solution)/shard_map/ppermute | solution.py:396
  135.8 1.2 copy-start.2
  138.8 0.7 copy-start.10
  139.5 15.9 %collective-permute-start.25 = (bf16[64,1024]{1,0:T(8,128)(2,1)}, bf16[64,1024]{1,0:T(8,128)(2,1)}, u32[]{:S(2)}, u32[]{:S(2)}) collective-permute-start(bf16[64,1024]{1,0:T(8,128)(2,1)} %get-tuple-element.66), channel_id=1, source_target_pairs={{0,2},{2,0},{4,6},{6,4},{8,10},{10,8},{12,14},{14,12},{16,18},{18,... | collective-permute-start | bytes 393224 | tf_op jit(solution)/shard_map/ppermute | solution.py:396
  139.5 18.6 %collective-permute-start.26 = (bf16[64,1024]{1,0:T(8,128)(2,1)}, bf16[64,1024]{1,0:T(8,128)(2,1)}, u32[]{:S(2)}, u32[]{:S(2)}) collective-permute-start(bf16[64,1024]{1,0:T(8,128)(2,1)} %get-tuple-element.67), channel_id=1, source_target_pairs={{0,4},{2,6},{4,0},{6,2},{8,12},{10,14},{12,8},{14,10},{16,20},{18,... | collective-permute-start | bytes 393224 | tf_op jit(solution)/shard_map/ppermute | solution.py:396
  140.9 17.1 %collective-permute-start.27 = (bf16[64,1024]{1,0:T(8,128)(2,1)}, bf16[64,1024]{1,0:T(8,128)(2,1)}, u32[]{:S(2)}, u32[]{:S(2)}) collective-permute-start(bf16[64,1024]{1,0:T(8,128)(2,1)} %get-tuple-element.68), channel_id=1, source_target_pairs={{0,6},{2,4},{4,2},{6,0},{8,14},{10,12},{12,10},{14,8},{16,22},{18,... | collective-permute-start | bytes 393224 | tf_op jit(solution)/shard_map/ppermute | solution.py:396
  141.4 1.2 copy-start.3
  146.4 11.7 %copy-start.11 = (f32[64,1024]{1,0:T(8,128)S(1)}, f32[64,1024]{1,0:T(8,128)}, u32[]{:S(2)}) copy-start(f32[64,1024]{1,0:T(8,128)} %copy-done.10) | copy-start | bytes 786436
  150.8 8.4 %copy-start.12 = (f32[64,1024]{1,0:T(8,128)}, f32[64,1024]{1,0:T(8,128)S(1)}, u32[]{:S(2)}) copy-start(f32[64,1024]{1,0:T(8,128)S(1)} %get-tuple-element.69) | copy-start | bytes 786436
  150.8 9.7 %collective-permute-start.22 = (bf16[512,64]{1,0:T(8,128)(2,1)S(1)}, bf16[512,64]{1,0:T(8,128)(2,1)S(1)}, u32[]{:S(2)}, u32[]{:S(2)}) collective-permute-start(bf16[512,64]{1,0:T(8,128)(2,1)S(1)} %get-tuple-element.62), channel_id=1, source_target_pairs={{0,8},{2,10},{4,12},{6,14},{8,16},{10,18},{12,20},{14,22},{16,24},... | collective-permute-start | bytes 196616 | tf_op jit(solution)/shard_map/ppermute | solution.py:485
  153.3 11.2 %collective-permute-start.23 = (bf16[512,64]{1,0:T(8,128)(2,1)S(1)}, bf16[512,64]{1,0:T(8,128)(2,1)S(1)}, u32[]{:S(2)}, u32[]{:S(2)}) collective-permute-start(bf16[512,64]{1,0:T(8,128)(2,1)S(1)} %get-tuple-element.63), channel_id=1, source_target_pairs={{0,16},{2,18},{4,20},{6,22},{8,24},{10,26},{12,28},{14,30},{16,0},... | collective-permute-start | bytes 196616 | tf_op jit(solution)/shard_map/ppermute | solution.py:485
  155.4 9.1 %collective-permute-start.24 = (bf16[512,64]{1,0:T(8,128)(2,1)S(1)}, bf16[512,64]{1,0:T(8,128)(2,1)S(1)}, u32[]{:S(2)}, u32[]{:S(2)}) collective-permute-start(bf16[512,64]{1,0:T(8,128)(2,1)S(1)} %get-tuple-element.64), channel_id=1, source_target_pairs={{0,24},{2,26},{4,28},{6,30},{8,0},{10,2},{12,4},{14,6},{16,8},{18,... | collective-permute-start | bytes 196616 | tf_op jit(solution)/shard_map/ppermute | solution.py:485
  159.9 5.4 %collective-permute-start.28 = (bf16[64,1024]{1,0:T(8,128)(2,1)}, bf16[64,1024]{1,0:T(8,128)(2,1)S(1)}, u32[]{:S(2)}, u32[]{:S(2)}) collective-permute-start(bf16[64,1024]{1,0:T(8,128)(2,1)} %bitcast.24), channel_id=1, source_target_pairs={{0,1},{1,0},{2,3},{3,2},{4,5},{5,4},{6,7},{7,6},{8,9},{9,8},{10,11... | collective-permute-start | bytes 393224 | tf_op jit(solution)/shard_map/ppermute | solution.py:399

commit v3 on v2

--- a/solution.py
+++ b/solution.py
@@ -11,10 +11,10 @@
 GROUP = 4
 HALO = 2
 STEP = 32
-SWEEP_COST = 10000
-CHUNKS = (1, 1)
+SWEEP_COST = 5000
+CHUNKS = (3, 3, 2)
 EXTRA = 4
-VMEM = 14 * 1024 * 1024
+VMEM = 20 * 1024 * 1024
 
 SLOW = pl.BlockSpec(memory_space=pltpu.HBM)
 FAST = pl.BlockSpec(memory_space=pltpu.VMEM)
@@ -98,17 +98,17 @@
     )
 
 
-def join_kernel(*refs):
-    out, at = refs[-1], 0
-    for ref in refs[:-1]:
-        out[at : at + ref.shape[0]] = ref[...]
-        at += ref.shape[0]
-
-
-def join(*arrays):
-    shape = (sum(a.shape[0] for a in arrays),) + arrays[0].shape[1:]
-    out_shape = jax.ShapeDtypeStruct(shape, arrays[0].dtype)
-    return call(join_kernel, "join", [FAST] * len(arrays), out_shape, [], 1000, *arrays)
+def join_kernel(start, own, other, out):
+    size = own.shape[0]
+    out[:size] = own[...]
+    out[size:] = other[start : start + size]
+
+
+def join(own, other, start):
+    shape = (2 * own.shape[0],) + own.shape[1:]
+    out_shape = jax.ShapeDtypeStruct(shape, own.dtype)
+    kernel = functools.partial(join_kernel, start)
+    return call(kernel, "join", [FAST] * 2, out_shape, [], 1000, own, other)
 
 
 def along_z(rows, band):
@@ -183,15 +183,14 @@
     lax.fori_loop(0, count // step, one_pass, 0)
 
 
-def sweep(adjoint, place, pair, near, far, early, late_near, late_far, shift, band, cond, span=None):
+def sweep(adjoint, place, sources, shift, band, cond, span=None):
     width_z = shift.shape[1]
     begin, count = span or (0, shift.shape[0])
-    sources = [pair, near, far, early, late_near, late_far]
-    size = near.shape[0]
-    layout = [(0, 0), (0, size), (1, 0), (2, 0), (3, 0), (3, size), (4, 0), (5, 0)]
-    width_y = near.shape[1]
+    size = sources[0].shape[0] // 2
+    layout = [(i, at) for i, array in enumerate(sources) for at in range(0, array.shape[0], size)]
+    width_y = sources[0].shape[1]
     planes = GROUP + 2 * HALO
-    step = min(STEP, count)
+    step = STEP if count % STEP == 0 else STEP // 2
     cells = GROUP * width_y * width_z
     out_shape = [jax.ShapeDtypeStruct((count, cells), jnp.bfloat16)]
     if cond is None:
@@ -226,36 +225,41 @@
     return jnp.concatenate([ref[:, span] for ref in refs], axis=0)
 
 
-def gram_kernel(start, blocks, parts, splits, last, info, factors, singular, *refs):
-    own, far, direct = refs[:splits], refs[splits : 2 * splits], refs[2 * splits : 2 * splits + parts]
-    rest = refs[2 * splits + parts :]
+def gram_kernel(start, chunks, parts, shares, last, info, factors, singular, *refs):
+    own, far, direct = refs[:chunks], refs[chunks : 2 * chunks], refs[2 * chunks : 2 * chunks + parts]
+    rest = refs[2 * chunks + parts :]
     if last:
         older, older_modes = rest[:2]
         rest = rest[2:]
         kept, sent, kept_modes, sent_modes = rest[0], rest[1:-4], rest[-4], rest[-3]
-        pieces, modes = rest[-2:]
-    else:
-        pieces, modes = rest
+    pieces, modes = rest[-2:]
     member, core, share = info[0], info[1], info[2]
-    half, cells = splits * own[0].shape[0], own[0].shape[1]
+    adjoint = [ref for pair in zip(own, far) for ref in pair]
+    rows_total, cells = sum(ref.shape[0] for ref in adjoint), own[0].shape[1]
     count, _, width = pieces.shape
     depth = cells // GROUP
     dims = (((1,), (1,)), ((), ()))
-    total = jnp.zeros((2 * half, count * width), jnp.float32)
+    total = jnp.zeros((rows_total, count * width), jnp.float32)
     for plane in range(GROUP):
-        rows, cols = slab((*own, *far), plane * depth, depth), slab(direct, plane * depth, depth)
+        rows, cols = slab(adjoint, plane * depth, depth), slab(direct, plane * depth, depth)
         total = total + lax.dot_general(rows, cols, dims, preferred_element_type=jnp.float32)
-    for side in range(2):
-        first = jnp.where(side == 0, core, 1 - core) * half
-        spot = pl.ds(pl.multiple_of(first, half), half)
-        for part in range(count):
-            pieces[part, spot, :] = total[side * half : (side + 1) * half, part * width : (part + 1) * width]
-    left = scaled_factors(factors[:, start : start + 2 * half], singular)
-    lower, upper = left[:, :half], left[:, half:]
-    swapped = jnp.concatenate(
-        [jnp.where(core == 0, lower, upper), jnp.where(core == 0, upper, lower)], axis=1
-    )
-    term = jnp.dot(swapped, slab((*own, *far), member * depth, depth), preferred_element_type=jnp.float32)
+    per_share = factors.shape[1] // shares
+    window = factors[:, pl.ds(pl.multiple_of(share * per_share, per_share), per_share)]
+    window = scaled_factors(window[:, start : start + rows_total], singular)
+    left, at = [], 0
+    for ref in own:
+        half = ref.shape[0]
+        for side in range(2):
+            spot = pl.ds(pl.multiple_of(at + jnp.where(side == 0, core, 1 - core) * half, 16), half)
+            held = at + side * half
+            for part in range(count):
+                pieces[part, spot, :] = total[held : held + half, part * width : (part + 1) * width]
+        lower, upper = window[:, at : at + half], window[:, at + half : at + 2 * half]
+        left += [jnp.where(core == 0, lower, upper), jnp.where(core == 0, upper, lower)]
+        at += 2 * half
+    term = jnp.dot(
+        jnp.concatenate(left, axis=1), slab(adjoint, member * depth, depth), preferred_element_type=jnp.float32
+    )
     if not last:
         modes[...] = term
         return
@@ -268,7 +272,6 @@
         else:
             sent[number - 1][0:start, :] = older[index].astype(jnp.bfloat16)
             sent[number - 1][start:, :] = pieces[index].astype(jnp.bfloat16)
-    shares = sent_modes.shape[0] + 1
     wide = depth // shares
     for step in range(shares):
         piece = modes[:, pl.ds(pl.multiple_of(((share + step) % shares) * wide, wide), wide)]
@@ -279,12 +282,13 @@
 
 
 def gram_part(info, start, own, far, factors, singular, direct, blocks, older, layers):
-    half, cells = len(own) * own[0].shape[0], own[0].shape[1]
+    cells = own[0].shape[1]
     width = direct[0].shape[0]
-    mode_count, rows = factors.shape
     shares = len(direct) // blocks
+    mode_count, rows = factors.shape[0], factors.shape[1] // shares
     depth = cells // GROUP
-    pieces = (shares * blocks, 2 * half, width)
+    height = 2 * sum(a.shape[0] for a in own)
+    pieces = (shares * blocks, height, width)
     operands = [info, factors, singular, *own, *far, *direct]
     if older is None:
         out_shape = [
@@ -302,12 +306,12 @@
         ]
         scratch = [pltpu.VMEM(pieces, jnp.float32), pltpu.VMEM((mode_count, depth), jnp.float32)]
     return call(
-        functools.partial(gram_kernel, start, blocks, len(direct), len(own), older is not None),
+        functools.partial(gram_kernel, start, len(own), len(direct), shares, older is not None),
         "gram_part",
         [SCALAR] + [FAST] * (len(operands) - 1),
         out_shape,
         scratch,
-        2 * half * cells,
+        height * cells,
         *operands,
     )
 
@@ -317,7 +321,19 @@
     member, share = info[0], info[2]
     depth = direct[0].shape[1] // GROUP
     wide = depth // shares
-    right = scaled_factors(factors[...], singular)
+    width = direct[0].shape[0]
+    blocks = parts // shares
+
+    def columns(owner, number):
+        base = (owner * blocks + number) * GROUP * width
+        spans = [factors[:, base + i * width : base + (i + 1) * width] for i in range(GROUP)]
+        return sum(jnp.where(member == i, span, 0.0) for i, span in enumerate(spans))
+
+    right = []
+    for part in range(parts):
+        owner = (share + shares - part // blocks) % shares
+        right.append(sum(jnp.where(owner == i, columns(i, part % blocks), 0.0) for i in range(shares)))
+    right = scaled_factors(jnp.concatenate(right, axis=1), singular)
     for mask in range(GROUP):
         at = (member ^ mask) * depth + share * wide
         term = jnp.dot(right, slab(direct, at, wide), preferred_element_type=jnp.float32)
@@ -404,7 +420,8 @@
     early = lambda array: lax.ppermute(array, "space", upper(ups, 1) + upper(downs, 0))
     late = lambda array: lax.ppermute(array, "space", upper(ups, 0) + upper(downs, 1))
 
-    sizes = [rows * part // sum(CHUNKS) // 2 for part in CHUNKS]
+    sizes = [rows * part // sum(CHUNKS) // 32 * 16 for part in CHUNKS[1:]]
+    sizes = [rows // 2 - sum(sizes)] + sizes
     starts = [2 * sum(sizes[:i]) for i in range(len(sizes))]
     sets = forcing_direct.reshape(blocks, GROUP, block, width_y, width_z)
     rows_adj = forcing_adjoint.reshape(rows, width_y, width_z)
@@ -412,8 +429,12 @@
     cross = lambda i: ("half", starts[i], sizes[i], True)
     near_d, far_d, cross_d, own_d = pack(info, sets, conductance, info, [[("set", mask)] for mask in (2, 3, 1, 0)])
     crossed_d = swap(cross_d, 1)
-    to_core, own_0, cross_0, own_1, cross_1 = pack(
-        info, rows_adj, conductance, crossed_d, [[cross(0), cross(1)], [own(0)], [cross(0)], [own(1)], [cross(1)]]
+    to_core, *own_adj = pack(
+        info,
+        rows_adj,
+        conductance,
+        crossed_d,
+        [[cross(i) for i in range(len(sizes))]] + [[own(i)] for i in range(len(sizes))],
     )
 
     wide = lambda values: jnp.broadcast_to(values[:, None], (values.shape[0], width_z))
@@ -433,51 +454,46 @@
     ).astype(jnp.int32)
     band = band_matrix(width_z)
 
-    y_0, y_1 = swap(near_d, 2), swap(far_d, 3)
+    near, far = swap(near_d, 2), swap(far_d, 3)
     crossed = swap(to_core, 1)
-    pair_d = join(own_d, crossed_d)
-    pair_0, pair_1 = join(own_0, crossed[: sizes[0]]), join(own_1, crossed[sizes[0] :])
+    pair_d = join(own_d, crossed_d, 0)
+    spots = [sum(sizes[:i]) for i in range(len(sizes))]
+    pairs = [join(own, crossed, at) for own, at in zip(own_adj, spots)]
     e_d = early(pair_d)
-    l_0, l_1 = late(y_0), late(y_1)
-    y_2 = swap(after(own_0, y_1), 2)
-    y_3 = swap(after(cross_0, y_0, pair_d, pair_0, pair_1), 3)
-    e_0 = early(after(pair_0, y_0))
-    dir_state, cond = sweep(False, place, pair_d, y_0, y_1, e_d, l_0, l_1, dir_shift, band, None, (0, block))
+    late_near, late_far = late(near), late(far)
+    sources = [pair_d, near, far, e_d, late_near, late_far]
+    dir_state, cond = sweep(False, place, sources, dir_shift, band, None, (0, block))
     dir_states = [dir_state] + [
-        sweep(False, place, pair_d, y_0, y_1, e_d, l_0, l_1, dir_shift, band, cond, (i * block, block))[0]
-        for i in range(1, blocks)
+        sweep(False, place, sources, dir_shift, band, cond, (i * block, block))[0] for i in range(1, blocks)
     ]
-    dir_state = dir_states[-1]
     moved = [[around(state, step) for state in dir_states] for step in range(1, n_snap)]
     everyone = dir_states + [state for states in moved for state in states]
-    l_2, l_3 = late(y_2), late(after(y_3, dir_state))
-    y_4 = swap(after(own_1, y_2, l_0), 2)
-    y_5 = swap(after(cross_1, y_3, dir_state), 3)
-    e_1 = early(after(pair_1, y_4))
-    l_4 = late(after(y_4, l_2))
-    state_0 = sweep(True, place, pair_0, y_2, after(y_3, y_4, everyone[blocks]), e_0, l_2, l_3, adj_shift[0], band, cond)[0]
-    other_0 = swap(state_0, 1)
-    l_5 = late(after(y_5, state_0, l_4))
-    part = sizes[1] // 2
-    state_1 = [
-        sweep(True, place, pair_1, y_4, after(y_5, everyone[-1]), e_1, l_4, l_5, adj_shift[1], band, cond, (at, part))[0]
-        for at in (0, part)
-    ]
-    other_1 = [swap(state, 1) for state in state_1]
+    y_adj, e_adj, l_adj, own_states, far_states = [], [], [], [], []
+    for i, pair in enumerate(pairs):
+        y_after = [near, far, late_near] if i == 0 else [y_adj[-1], dir_states[0]]
+        e_after = [e_d] if i == 0 else [e_adj[-1], dir_states[-1]]
+        y_adj.append(swap(after(pair, *y_after), 2))
+        e_adj.append(early(after(pair, *e_after)))
+        l_adj.append(late(after(y_adj[i], l_adj[-1]) if i else y_adj[i]))
+        arrived = after(y_adj[i], everyone[blocks]) if i == 1 else y_adj[i]
+        if i == 2:
+            arrived = after(y_adj[i], everyone[-1])
+        sources = [pair, arrived, e_adj[i], l_adj[i]]
+        own_states.append(sweep(True, place, sources, adj_shift[i], band, cond)[0])
+        far_states.append(swap(own_states[i], 1))
 
     singular = singular_values.reshape(1, mode_count).T
-    left = lax.dynamic_slice_in_dim(left_factors.T, share * rows, rows, 1)
-    right_sets = right_factors.T.reshape(mode_count, n_snap, blocks, GROUP, block)
-    right_sets = pick(right_sets, member, 3).reshape(mode_count, n_snap, blocks * block)
-    right = jnp.concatenate([pick(right_sets, (share - step) % n_snap, 1) for step in range(n_snap)], axis=1)
+    left, right = left_factors.T, right_factors.T
     kept, *sent = direct_part(info, right, singular, everyone, n_snap)
     for mask in range(1, GROUP):
         kept = kept + swap(sent[mask - 1], mask).astype(jnp.float32)
     direct_modes = kept.reshape(mode_count, 1, rows_y, width_z)
 
-    outs = gram_part(info, 0, [state_0], [other_0], left, singular, everyone, blocks, None, layers)
     outs = gram_part(
-        info, starts[1], state_1, other_1, left, singular, everyone, blocks, list(outs), layers
+        info, 0, own_states[:-1], far_states[:-1], left, singular, everyone, blocks, None, layers
+    )
+    outs = gram_part(
+        info, starts[-1], own_states[-1:], far_states[-1:], left, singular, everyone, blocks, list(outs), layers
     )
     kept, *sent, kept_modes, sent_modes = outs
     for step in range(1, layers):

time: 169 us -> 155 us (0.917)
  starting transfers between devices: 50.9 us -> 46.1 us
  waiting for transfers between devices: 43.9 us -> 40.2 us
  local copies, waits for them, and re-layouts: 18.3 us -> 14.8 us
  other arithmetic: 2.3 us -> 0.28 us
    ppermute x6 -> x5, waiting for transfers between devices: 17.4 us -> 9.12 us  [per_device(): lax.ppermute(array, 'space', upper(ups, 0) + upper(downs, 1))]
    ppermute x6 -> x5, starting transfers between devices: 28.2 us -> 22 us  [per_device(): lax.ppermute(array, 'space', upper(ups, 0) + upper(downs, 1))]
    ppermute x14 -> x13, waiting for transfers between devices: 19.6 us -> 24 us  [swap(): return lax.ppermute(array, 'space', [(i, i ^ mask) for i in range(n_space)])]
    ppermute x3, starting transfers between devices: 7.23 us -> 3.83 us  [per_device(): lax.ppermute(sent[step - 1], 'space', pairs).astype(jnp.float32)]
    unnamed x45 -> x55, local copies, waits for them, and re-layouts: 10.8 us -> 13.9 us
    reshape x2 -> x0, local copies, waits for them, and re-layouts: 3.16 us -> none  [the longest x1 2.1 us: per_device(): right_factors.T.reshape(mode_count, n_snap, blocks, GROUP, block)]
    ppermute x3, waiting for transfers between devices: 4.03 us -> 7.09 us  [per_device(): lax.ppermute(sent[step - 1], 'space', pairs).astype(jnp.float32)]
    ppermute x3 -> x4, waiting for transfers between devices: 2.81 us -> 0.01 us  [per_device(): lax.ppermute(array, 'space', upper(ups, 1) + upper(downs, 0))]
  transfers between devices with their start and end apart: 29 -> 28, of which waited for: 9 -> 9; matrix products, arithmetic and copies ran while one was open for 6% -> 2% of each run, Pallas kernels for 29% -> 33%
where the time goes in v3:
time: 155 us; the launch traced here: 154 us
  Pallas kernels  50.8 us (33%)
  starting transfers between devices  46.1 us (30%)
  waiting for transfers between devices  40.2 us (26%)
  local copies, waits for them, and re-layouts  14.8 us (10%)
    pallas_call x14, Pallas kernels, call(): pl.pallas_call(kernel, in_specs=in_specs, out_specs=jax.tree.map(lambda _...  50.8 us
    ppermute x13, waiting for transfers between devices, swap(): return lax.ppermute(array, 'space', [(i, i ^ mask) for i in range(n_space)])  24 us
    ppermute x5, starting transfers between devices, per_device(): lax.ppermute(array, 'space', upper(ups, 0) + upper(downs, 1))  22 us
    unnamed x55, local copies, waits for them, and re-layouts  13.9 us
    ppermute x13, starting transfers between devices, swap(): return lax.ppermute(array, 'space', [(i, i ^ mask) for i in range(n_space)])  10.6 us
    ppermute x5, waiting for transfers between devices, per_device(): lax.ppermute(array, 'space', upper(ups, 0) + upper(downs, 1))  9.12 us
    ppermute x3, waiting for transfers between devices, per_device(): lax.ppermute(sent[step - 1], 'space', pairs).astype(jnp.float32)  7.09 us
    ppermute x4, starting transfers between devices, per_device(): lax.ppermute(array, 'space', upper(ups, 1) + upper(downs, 0))  5.28 us
  transfers between devices with their start and end apart: 28, of which 9 were waited for; matrix products, arithmetic and copies ran while one was open for 2% of the time, Pallas kernels for 33%

profile of v3, /device:TPU:0, one launch (start us, length us, event | category | flops | bytes accessed | tf_op | source)
XLA Modules:
  0.0 153.5 jit_solution(1671877098977516021)
XLA Ops:
  0.9 0.1 stack.62.info.token
  1.0 1.6 %copy-done.4 = bf16[512,1,16,128]{3,2,1,0:T(8,128)(2,1)S(1)} copy-done((bf16[512,1,16,128]{3,2,1,0:T(8,128)(2,1)S(1)}, bf16[512,1,16,128]{3,2,1,0:T(8,128)(2,1)}, u32[]{:S(2)}) %copy-start.4) | copy-done | bytes 2097176
  2.6 0.7 copy-done.10
  3.3 0.9 pack.2
  4.2 0.5 collective-permute-start
  4.7 2.6 %collective-permute-start.2 = (bf16[132,16,128]{2,1,0:T(8,128)(2,1)S(1)}, bf16[132,16,128]{2,1,0:T(8,128)(2,1)S(1)}, u32[]{:S(2)}, u32[]{:S(2)}) collective-permute-start(bf16[132,16,128]{2,1,0:T(8,128)(2,1)S(1)} %get-tuple-element.40), channel_id=1, source_target_pairs={{0,4},{2,6},{4,0},{6,2},{8,12},{10,14},{12,8},{14,10},{16,20},{18,... | collective-permute-start | bytes 1622024 | tf_op jit(solution)/shard_map/ppermute | solution.py:412
  7.3 1.4 pack.3
  8.7 0.2 collective-permute-start.1
  9.0 1.8 %collective-permute-start.3 = (bf16[132,16,128]{2,1,0:T(8,128)(2,1)S(1)}, bf16[132,16,128]{2,1,0:T(8,128)(2,1)}, u32[]{:S(2)}, u32[]{:S(2)}) collective-permute-start(bf16[132,16,128]{2,1,0:T(8,128)(2,1)S(1)} %get-tuple-element.41), channel_id=1, source_target_pairs={{0,6},{2,4},{4,2},{6,0},{8,14},{10,12},{12,10},{14,8},{16,22},{18,... | collective-permute-start | bytes 1622024 | tf_op jit(solution)/shard_map/ppermute | solution.py:412
  10.9 1.4 collective-permute-start.6
  12.3 8.1 %collective-permute-done.2.refs_1_ = bf16[132,16,128]{2,1,0:T(8,128)(2,1)S(1)} collective-permute-done((bf16[132,16,128]{2,1,0:T(8,128)(2,1)S(1)}, bf16[132,16,128]{2,1,0:T(8,128)(2,1)S(1)}, u32[]{:S(2)}, u32[]{:S(2)}) %collective-permute-start.2) | collective-permute-done | bytes 540704 | tf_op jit(solution)/shard_map/ppermute | solution.py:412
  20.5 3.9 %collective-permute-start.4 = (bf16[132,16,128]{2,1,0:T(8,128)(2,1)S(1)}, bf16[132,16,128]{2,1,0:T(8,128)(2,1)S(1)}, u32[]{:S(2)}, u32[]{:S(2)}) collective-permute-start(bf16[132,16,128]{2,1,0:T(8,128)(2,1)S(1)} %collective-permute-done.2.refs_1_), channel_id=1, source_target_pairs={{0,8},{2,10},{8,16},{10,18},{16,24},{18,26},{12,4},{14,6},{20,12},... | collective-permute-start | bytes 1622024 | tf_op jit(solution)/shard_map/ppermute | solution.py:421
  24.4 7.2 %collective-permute-done.3.refs_2_ = bf16[132,16,128]{2,1,0:T(8,128)(2,1)} collective-permute-done((bf16[132,16,128]{2,1,0:T(8,128)(2,1)S(1)}, bf16[132,16,128]{2,1,0:T(8,128)(2,1)}, u32[]{:S(2)}, u32[]{:S(2)}) %collective-permute-start.3) | collective-permute-done | bytes 540704 | tf_op jit(solution)/shard_map/ppermute | solution.py:412
  31.6 4.3 %collective-permute-start.7 = (bf16[132,16,128]{2,1,0:T(8,128)(2,1)}, bf16[132,16,128]{2,1,0:T(8,128)(2,1)}, u32[]{:S(2)}, u32[]{:S(2)}) collective-permute-start(bf16[132,16,128]{2,1,0:T(8,128)(2,1)} %collective-permute-done.3.refs_2_), channel_id=1, source_target_pairs={{0,8},{2,10},{8,16},{10,18},{16,24},{18,26},{12,4},{14,6},{20,12},... | collective-permute-start | bytes 1622024 | tf_op jit(solution)/shard_map/ppermute | solution.py:421
  35.9 0.9 join.6.refs_0_
  36.9 0.8 collective-permute-start.5
  37.7 0.1 select_reduce_fusion
  37.8 0.1 reshape.31
  37.9 0.1 broadcast_in_dim.28
  38.1 0.9 join.5.refs_0_
  39.1 1.3 collective-permute-start.11
  40.3 7.4 %collective-permute-done.7.refs_5_ = bf16[132,16,128]{2,1,0:T(8,128)(2,1)} collective-permute-done((bf16[132,16,128]{2,1,0:T(8,128)(2,1)}, bf16[132,16,128]{2,1,0:T(8,128)(2,1)}, u32[]{:S(2)}, u32[]{:S(2)}) %collective-permute-start.7) | collective-permute-done | bytes 540704 | tf_op jit(solution)/shard_map/ppermute | solution.py:421
  47.8 1.0 copy-done.18
  48.9 5.6 %direct_sweeps.2 = (bf16[64,8192]{1,0:T(8,128)(2,1)S(1)}, f32[8,16,128]{2,1,0:T(8,128)S(1)}) custom-call(s32[8]{0:T(128)S(1)} %stack.71.place, bf16[264,16,128]{2,1,0:T(8,128)(2,1)S(1)} %join.7.refs_0_, bf16[132,16,128]{2,1,0:T(8,128)(2,1)S(1)} %copy-done.16, bf16[132,16,128]{2,1,0:T(8,128)(2,1)} %collective-permute-done.3.refs_2_, ...), custom_call_target="tpu_custom_call" | custom-call | flops 2621440000 | bytes 1024 | tf_op jit(solution)/shard_map/direct_sweeps/pallas_call | solution.py:25
  54.5 2.6 %collective-permute-done.5.refs_1_ = bf16[192,16,128]{2,1,0:T(8,128)(2,1)} collective-permute-done((bf16[192,16,128]{2,1,0:T(8,128)(2,1)}, bf16[192,16,128]{2,1,0:T(8,128)(2,1)}, u32[]{:S(2)}, u32[]{:S(2)}) %collective-permute-start.5) | collective-permute-done | bytes 786464 | tf_op jit(solution)/shard_map/ppermute | solution.py:412
  57.0 0.3 collective-permute-start.8
  57.3 3.2 %collective-permute-start.14 = (bf16[192,16,128]{2,1,0:T(8,128)(2,1)}, bf16[192,16,128]{2,1,0:T(8,128)(2,1)S(1)}, u32[]{:S(2)}, u32[]{:S(2)}) collective-permute-start(bf16[192,16,128]{2,1,0:T(8,128)(2,1)} %collective-permute-done.5.refs_1_), channel_id=1, source_target_pairs={{0,8},{2,10},{8,16},{10,18},{16,24},{18,26},{12,4},{14,6},{20,12},... | collective-permute-start | bytes 2359304 | tf_op jit(solution)/shard_map/ppermute | solution.py:421
  60.5 1.6 %collective-permute-start.18 = (bf16[64,8192]{1,0:T(8,128)(2,1)S(1)}, bf16[64,8192]{1,0:T(8,128)(2,1)S(1)}, u32[]{:S(2)}, u32[]{:S(2)}) collective-permute-start(bf16[64,8192]{1,0:T(8,128)(2,1)S(1)} %get-tuple-element.44.refs_4_.refs_2_.refs_0_), channel_id=1, source_target_pairs={{0,1},{1,0},{2,3},{3,2},{4,5},{5,4},{6,7},{7,6},{8,9},{9,8},{10,11... | collective-permute-start | bytes 3145736 | tf_op jit(solution)/shard_map/ppermute | solution.py:415
  62.0 1.2 copy-done.7
  63.3 5.6 %direct_sweeps.3.refs_5_.refs_3_.refs_1_ = bf16[64,8192]{1,0:T(8,128)(2,1)S(1)} custom-call(s32[8]{0:T(128)S(1)} %stack.71.place, bf16[264,16,128]{2,1,0:T(8,128)(2,1)S(1)} %copy-done.7, bf16[132,16,128]{2,1,0:T(8,128)(2,1)S(1)} %copy-done.16, bf16[132,16,128]{2,1,0:T(8,128)(2,1)} %collective-permute-done.3.refs_2_, ...), custom_call_target="tpu_custom_call" | custom-call | flops 2621440000 | bytes 1024 | tf_op jit(solution)/shard_map/direct_sweeps/pallas_call | solution.py:25
  68.9 1.3 collective-permute-start.12
  70.2 6.1 %collective-permute-done.8.refs_1_ = bf16[192,16,128]{2,1,0:T(8,128)(2,1)} collective-permute-done((bf16[192,16,128]{2,1,0:T(8,128)(2,1)}, bf16[192,16,128]{2,1,0:T(8,128)(2,1)}, u32[]{:S(2)}, u32[]{:S(2)}) %collective-permute-start.8) | collective-permute-done | bytes 786464 | tf_op jit(solution)/shard_map/ppermute | solution.py:412
  76.3 1.0 collective-permute-done.14.refs_3_
  77.2 0.9 copy-done.13
  78.1 5.2 %collective-permute-start.15 = (bf16[192,16,128]{2,1,0:T(8,128)(2,1)}, bf16[192,16,128]{2,1,0:T(8,128)(2,1)}, u32[]{:S(2)}, u32[]{:S(2)}) collective-permute-start(bf16[192,16,128]{2,1,0:T(8,128)(2,1)} %collective-permute-done.8.refs_1_), channel_id=1, source_target_pairs={{0,8},{2,10},{8,16},{10,18},{16,24},{18,26},{12,4},{14,6},{20,12},... | collective-permute-start | bytes 2359304 | tf_op jit(solution)/shard_map/ppermute | solution.py:421
  83.3 0.8 join.4.refs_0_
  84.2 1.6 %collective-permute-start.10 = (bf16[64,8192]{1,0:T(8,128)(2,1)}, bf16[64,8192]{1,0:T(8,128)(2,1)S(1)}, u32[]{:S(2)}, u32[]{:S(2)}) collective-permute-start(bf16[64,8192]{1,0:T(8,128)(2,1)} %copy-done), channel_id=1, source_target_pairs={{0,1},{1,0},{2,3},{3,2},{4,5},{5,4},{6,7},{7,6},{8,9},{9,8},{10,11... | collective-permute-start | bytes 3145736 | tf_op jit(solution)/shard_map/ppermute | solution.py:415
  85.9 1.1 copy-done.12
  87.0 1.1 copy-done.14
  88.2 0.8 copy-done.20
  89.0 8.7 %adjoint_sweeps.4.refs_0_ = bf16[96,8192]{1,0:T(8,128)(2,1)} custom-call(s32[8]{0:T(128)S(1)} %stack.71.place, bf16[192,16,128]{2,1,0:T(8,128)(2,1)} %join.6.refs_0_, bf16[192,16,128]{2,1,0:T(8,128)(2,1)} %collective-permute-done.5.refs_1_, bf16[192,16,128]{2,1,0:T(8,128)(2,1)S(1)} %copy-done.12, bf16[192,16,128]{2,1,0:T(8,128)(2,1)S(1)} %copy-done.14, ...), custom_call_target="tpu_custom_call" | custom-call | flops 3932160000 | bytes 1024 | tf_op jit(solution)/shard_map/adjoint_sweeps/pallas_call | solution.py:25
  97.7 1.3 collective-permute-start.13
  99.0 5.4 %collective-permute-start.16 = (bf16[128,16,128]{2,1,0:T(8,128)(2,1)}, bf16[128,16,128]{2,1,0:T(8,128)(2,1)}, u32[]{:S(2)}, u32[]{:S(2)}) collective-permute-start(bf16[128,16,128]{2,1,0:T(8,128)(2,1)} %collective-permute-done.9.refs_1_), channel_id=1, source_target_pairs={{0,8},{2,10},{8,16},{10,18},{16,24},{18,26},{12,4},{14,6},{20,12},... | collective-permute-start | bytes 1572872 | tf_op jit(solution)/shard_map/ppermute | solution.py:421
  104.5 9.1 %adjoint_sweeps.5.refs_1_ = bf16[96,8192]{1,0:T(8,128)(2,1)} custom-call(s32[8]{0:T(128)S(1)} %stack.71.place, bf16[192,16,128]{2,1,0:T(8,128)(2,1)} %join.5.refs_0_, bf16[192,16,128]{2,1,0:T(8,128)(2,1)} %collective-permute-done.8.refs_1_, bf16[192,16,128]{2,1,0:T(8,128)(2,1)} %collective-permute-done.12.refs_2_, ...), custom_call_target="tpu_custom_call" | custom-call | flops 3932160000 | bytes 1024 | tf_op jit(solution)/shard_map/adjoint_sweeps/pallas_call | solution.py:25
  113.7 1.0 copy-done.2
  114.7 0.8 collective-permute-done.16.refs_3_
  115.5 0.8 copy-done.21
  116.4 6.7 %adjoint_sweeps.3.refs_0_ = bf16[64,8192]{1,0:T(8,128)(2,1)} custom-call(s32[8]{0:T(128)S(1)} %stack.71.place, bf16[128,16,128]{2,1,0:T(8,128)(2,1)} %join.4.refs_0_, bf16[128,16,128]{2,1,0:T(8,128)(2,1)} %collective-permute-done.9.refs_1_, bf16[128,16,128]{2,1,0:T(8,128)(2,1)} %collective-permute-done.13.refs_2_, ...), custom_call_target="tpu_custom_call" | custom-call | flops 2621440000 | bytes 1024 | tf_op jit(solution)/shard_map/adjoint_sweeps/pallas_call | solution.py:25
  123.1 0.1 copy.25.singular
  123.2 1.2 copy-done.3
  124.5 1.1 direct_modes_part.1
  125.6 0.6 collective-permute-start.24
  126.2 3.8 %collective-permute-start.25 = (bf16[64,1024]{1,0:T(8,128)(2,1)S(1)}, bf16[64,1024]{1,0:T(8,128)(2,1)S(1)}, u32[]{:S(2)}, u32[]{:S(2)}) collective-permute-start(bf16[64,1024]{1,0:T(8,128)(2,1)S(1)} %get-tuple-element.63), channel_id=1, source_target_pairs={{0,4},{2,6},{4,0},{6,2},{8,12},{10,14},{12,8},{14,10},{16,20},{18,... | collective-permute-start | bytes 393224 | tf_op jit(solution)/shard_map/ppermute | solution.py:412
  130.0 5.0 %gram_part.2 = (f32[4,384,64]{2,1,0:T(8,128)S(1)}, f32[64,2048]{1,0:T(8,128)S(1)}) custom-call(s32[8]{0:T(128)S(1)} %stack.62.info.token, f32[64,1024]{1,0:T(8,128)S(1)} %bitcast.38, f32[64,1]{1,0:T(8,128)S(1)} %copy.25.singular, bf16[96,8192]{1,0:T(8,128)(2,1)} %adjoint_sweeps.4.refs_0_, bf16[96,8192]{1,0:T(8,128)(2,1)} %adjoint_sweeps.5.refs_1_, ...), custom_call_target="tpu_custom_call" | custom-call | flops 3145728 | bytes 1024 | tf_op jit(solution)/shard_map/gram_part/pallas_call | solution.py:25
  135.0 3.9 %gram_part.3 = (f32[512,64]{1,0:T(8,128)S(1)}, bf16[512,64]{1,0:T(8,128)(2,1)S(1)}, bf16[512,64]{1,0:T(8,128)(2,1)S(1)}, bf16[512,64]{1,0:T(8,128)(2,1)S(1)}, f3...) custom-call(s32[8]{0:T(128)S(1)} %stack.62.info.token, f32[64,1024]{1,0:T(8,128)S(1)} %bitcast.39, ...), custom_call_target="tpu_custom_call" | custom-call | flops 1048576 | bytes 1024 | tf_op jit(solution)/shard_map/gram_part/pallas_call | solution.py:25
  138.8 1.0 collective-permute-start.21
  139.8 2.2 %collective-permute-start.22 = (bf16[512,64]{1,0:T(8,128)(2,1)S(1)}, bf16[512,64]{1,0:T(8,128)(2,1)S(1)}, u32[]{:S(2)}, u32[]{:S(2)}) collective-permute-start(bf16[512,64]{1,0:T(8,128)(2,1)S(1)} %get-tuple-element.59), channel_id=1, source_target_pairs={{0,16},{2,18},{4,20},{6,22},{8,24},{10,26},{12,28},{14,30},{16,0},... | collective-permute-start | bytes 196616 | tf_op jit(solution)/shard_map/ppermute | solution.py:501
  142.0 0.6 collective-permute-start.23
  142.7 0.8 copy.30
  143.5 1.3 collective-permute-start.27
  144.8 2.3 %collective-permute-done.21 = bf16[512,64]{1,0:T(8,128)(2,1)S(1)} collective-permute-done((bf16[512,64]{1,0:T(8,128)(2,1)S(1)}, bf16[512,64]{1,0:T(8,128)(2,1)S(1)}, u32[]{:S(2)}, u32[]{:S(2)}) %collective-permute-start.21) | collective-permute-done | bytes 65568 | tf_op jit(solution)/shard_map/ppermute | solution.py:501
  147.1 4.8 %collective-permute-done.22 = bf16[512,64]{1,0:T(8,128)(2,1)S(1)} collective-permute-done((bf16[512,64]{1,0:T(8,128)(2,1)S(1)}, bf16[512,64]{1,0:T(8,128)(2,1)S(1)}, u32[]{:S(2)}, u32[]{:S(2)}) %collective-permute-start.22) | collective-permute-done | bytes 65568 | tf_op jit(solution)/shard_map/ppermute | solution.py:501
  152.0 0.8 copy.27
  152.8 0.8 copy.31
  (79 shorter events, 1.0 us)
Async XLA Ops:
  1.0 1.6 %copy-start.4 = (bf16[512,1,16,128]{3,2,1,0:T(8,128)(2,1)S(1)}, bf16[512,1,16,128]{3,2,1,0:T(8,128)(2,1)}, u32[]{:S(2)}) copy-start(bf16[512,1,16,128]{3,2,1,0:T(8,128)(2,1)} %param.9) | copy-start | bytes 6291460
  2.6 0.7 copy-start.10
  3.3 4.0 %copy-start.5 = (bf16[512,1,16,128]{3,2,1,0:T(8,128)(2,1)S(1)}, bf16[512,1,16,128]{3,2,1,0:T(8,128)(2,1)}, u32[]{:S(2)}) copy-start(bf16[512,1,16,128]{3,2,1,0:T(8,128)(2,1)} %param.10) | copy-start | bytes 6291460
  4.2 3.1 %collective-permute-start = (bf16[132,16,128]{2,1,0:T(8,128)(2,1)S(1)}, bf16[132,16,128]{2,1,0:T(8,128)(2,1)S(1)}, u32[]{:S(2)}, u32[]{:S(2)}) collective-permute-start(bf16[132,16,128]{2,1,0:T(8,128)(2,1)S(1)} %get-tuple-element.35), channel_id=1, source_target_pairs={{0,2},{2,0},{4,6},{6,4},{8,10},{10,8},{12,14},{14,12},{16,18},{18,... | collective-permute-start | bytes 1622024 | tf_op jit(solution)/shard_map/ppermute | solution.py:412
  4.7 15.7 %collective-permute-start.2 = (bf16[132,16,128]{2,1,0:T(8,128)(2,1)S(1)}, bf16[132,16,128]{2,1,0:T(8,128)(2,1)S(1)}, u32[]{:S(2)}, u32[]{:S(2)}) collective-permute-start(bf16[132,16,128]{2,1,0:T(8,128)(2,1)S(1)} %get-tuple-element.40), channel_id=1, source_target_pairs={{0,4},{2,6},{4,0},{6,2},{8,12},{10,14},{12,8},{14,10},{16,20},{18,... | collective-permute-start | bytes 1622024 | tf_op jit(solution)/shard_map/ppermute | solution.py:412
  8.7 27.2 %collective-permute-start.1 = (bf16[256,16,128]{2,1,0:T(8,128)(2,1)S(1)}, bf16[256,16,128]{2,1,0:T(8,128)(2,1)S(1)}, u32[]{:S(2)}, u32[]{:S(2)}) collective-permute-start(bf16[256,16,128]{2,1,0:T(8,128)(2,1)S(1)} %get-tuple-element.37), channel_id=1, source_target_pairs={{0,2},{2,0},{4,6},{6,4},{8,10},{10,8},{12,14},{14,12},{16,18},{18,... | collective-permute-start | bytes 3145736 | tf_op jit(solution)/shard_map/ppermute | solution.py:412
  9.0 22.7 %collective-permute-start.3 = (bf16[132,16,128]{2,1,0:T(8,128)(2,1)S(1)}, bf16[132,16,128]{2,1,0:T(8,128)(2,1)}, u32[]{:S(2)}, u32[]{:S(2)}) collective-permute-start(bf16[132,16,128]{2,1,0:T(8,128)(2,1)S(1)} %get-tuple-element.41), channel_id=1, source_target_pairs={{0,6},{2,4},{4,2},{6,0},{8,14},{10,12},{12,10},{14,8},{16,22},{18,... | collective-permute-start | bytes 1622024 | tf_op jit(solution)/shard_map/ppermute | solution.py:412
  10.8 37.0 %copy-start.6 = (bf16[264,16,128]{2,1,0:T(8,128)(2,1)}, bf16[264,16,128]{2,1,0:T(8,128)(2,1)S(1)}, u32[]{:S(2)}) copy-start(bf16[264,16,128]{2,1,0:T(8,128)(2,1)S(1)} %join.7.refs_0_) | copy-start | bytes 3244036
  10.8 26.8 %copy-start.22 = (s32[512]{0:T(512)S(1)}, s32[512]{0:T(512)}, u32[]{:S(2)}) copy-start(s32[512]{0:T(512)} %param.14) | copy-start | bytes 6148
  10.9 26.8 %copy-start.23 = (s32[512]{0:T(512)S(1)}, s32[512]{0:T(512)}, u32[]{:S(2)}) copy-start(s32[512]{0:T(512)} %param.13) | copy-start | bytes 6148
  10.9 26.8 %copy-start.25 = (f32[16]{0:T(128)S(1)}, f32[16]{0:T(128)}, u32[]{:S(2)}) copy-start(f32[16]{0:T(128)} %param.12) | copy-start | bytes 196
  10.9 28.2 %collective-permute-start.6 = (bf16[264,16,128]{2,1,0:T(8,128)(2,1)S(1)}, bf16[264,16,128]{2,1,0:T(8,128)(2,1)}, u32[]{:S(2)}, u32[]{:S(2)}) collective-permute-start(bf16[264,16,128]{2,1,0:T(8,128)(2,1)S(1)} %join.7.refs_0_), channel_id=1, source_target_pairs={{4,12},{6,14},{12,20},{14,22},{20,28},{22,30},{8,0},{10,2},{16,8},... | collective-permute-start | bytes 3244040 | tf_op jit(solution)/shard_map/ppermute | solution.py:420
  20.4 16.4 %copy-start.15 = (bf16[132,16,128]{2,1,0:T(8,128)(2,1)}, bf16[132,16,128]{2,1,0:T(8,128)(2,1)S(1)}, u32[]{:S(2)}) copy-start(bf16[132,16,128]{2,1,0:T(8,128)(2,1)S(1)} %collective-permute-done.2.refs_1_) | copy-start | bytes 1622020
  20.5 16.4 %collective-permute-start.4 = (bf16[132,16,128]{2,1,0:T(8,128)(2,1)S(1)}, bf16[132,16,128]{2,1,0:T(8,128)(2,1)S(1)}, u32[]{:S(2)}, u32[]{:S(2)}) collective-permute-start(bf16[132,16,128]{2,1,0:T(8,128)(2,1)S(1)} %collective-permute-done.2.refs_1_), channel_id=1, source_target_pairs={{0,8},{2,10},{8,16},{10,18},{16,24},{18,26},{12,4},{14,6},{20,12},... | collective-permute-start | bytes 1622024 | tf_op jit(solution)/shard_map/ppermute | solution.py:421
  31.6 16.1 %collective-permute-start.7 = (bf16[132,16,128]{2,1,0:T(8,128)(2,1)}, bf16[132,16,128]{2,1,0:T(8,128)(2,1)}, u32[]{:S(2)}, u32[]{:S(2)}) collective-permute-start(bf16[132,16,128]{2,1,0:T(8,128)(2,1)} %collective-permute-done.3.refs_2_), channel_id=1, source_target_pairs={{0,8},{2,10},{8,16},{10,18},{16,24},{18,26},{12,4},{14,6},{20,12},... | collective-permute-start | bytes 1622024 | tf_op jit(solution)/shard_map/ppermute | solution.py:421
  36.9 10.8 %copy-start.17 = (bf16[132,16,128]{2,1,0:T(8,128)(2,1)}, bf16[132,16,128]{2,1,0:T(8,128)(2,1)S(1)}, u32[]{:S(2)}) copy-start(bf16[132,16,128]{2,1,0:T(8,128)(2,1)S(1)} %collective-permute-done.4.refs_4_) | copy-start | bytes 1622020
  36.9 20.1 %collective-permute-start.5 = (bf16[192,16,128]{2,1,0:T(8,128)(2,1)}, bf16[192,16,128]{2,1,0:T(8,128)(2,1)}, u32[]{:S(2)}, u32[]{:S(2)}) collective-permute-start(bf16[192,16,128]{2,1,0:T(8,128)(2,1)} %join.6.refs_0_), channel_id=1, source_target_pairs={{0,4},{2,6},{4,0},{6,2},{8,12},{10,14},{12,8},{14,10},{16,20},{18,... | collective-permute-start | bytes 2359304 | tf_op jit(solution)/shard_map/ppermute | solution.py:412
  38.1 9.7 %copy-start.16 = (bf16[132,16,128]{2,1,0:T(8,128)(2,1)S(1)}, bf16[132,16,128]{2,1,0:T(8,128)(2,1)}, u32[]{:S(2)}) copy-start(bf16[132,16,128]{2,1,0:T(8,128)(2,1)} %copy-done.15) | copy-start | bytes 1622020
  39.1 29.8 %collective-permute-start.11 = (bf16[192,16,128]{2,1,0:T(8,128)(2,1)}, bf16[192,16,128]{2,1,0:T(8,128)(2,1)S(1)}, u32[]{:S(2)}, u32[]{:S(2)}) collective-permute-start(bf16[192,16,128]{2,1,0:T(8,128)(2,1)} %join.6.refs_0_), channel_id=1, source_target_pairs={{4,12},{6,14},{12,20},{14,22},{20,28},{22,30},{8,0},{10,2},{16,8},... | collective-permute-start | bytes 2359304 | tf_op jit(solution)/shard_map/ppermute | solution.py:420
  47.8 1.0 copy-start.18
  54.4 14.4 %copy-start.19 = (f32[8,16,128]{2,1,0:T(8,128)}, f32[8,16,128]{2,1,0:T(8,128)S(1)}, u32[]{:S(2)}) copy-start(f32[8,16,128]{2,1,0:T(8,128)S(1)} %get-tuple-element.47.refs_8_.refs_6_) | copy-start | bytes 196612
  57.0 19.2 %collective-permute-start.8 = (bf16[192,16,128]{2,1,0:T(8,128)(2,1)}, bf16[192,16,128]{2,1,0:T(8,128)(2,1)}, u32[]{:S(2)}, u32[]{:S(2)}) collective-permute-start(bf16[192,16,128]{2,1,0:T(8,128)(2,1)} %join.5.refs_0_), channel_id=1, source_target_pairs={{0,4},{2,6},{4,0},{6,2},{8,12},{10,14},{12,8},{14,10},{16,20},{18,... | collective-permute-start | bytes 2359304 | tf_op jit(solution)/shard_map/ppermute | solution.py:412
  57.3 19.9 %collective-permute-start.14 = (bf16[192,16,128]{2,1,0:T(8,128)(2,1)}, bf16[192,16,128]{2,1,0:T(8,128)(2,1)S(1)}, u32[]{:S(2)}, u32[]{:S(2)}) collective-permute-start(bf16[192,16,128]{2,1,0:T(8,128)(2,1)} %collective-permute-done.5.refs_1_), channel_id=1, source_target_pairs={{0,8},{2,10},{8,16},{10,18},{16,24},{18,26},{12,4},{14,6},{20,12},... | collective-permute-start | bytes 2359304 | tf_op jit(solution)/shard_map/ppermute | solution.py:421
  60.5 25.3 %collective-permute-start.18 = (bf16[64,8192]{1,0:T(8,128)(2,1)S(1)}, bf16[64,8192]{1,0:T(8,128)(2,1)S(1)}, u32[]{:S(2)}, u32[]{:S(2)}) collective-permute-start(bf16[64,8192]{1,0:T(8,128)(2,1)S(1)} %get-tuple-element.44.refs_4_.refs_2_.refs_0_), channel_id=1, source_target_pairs={{0,1},{1,0},{2,3},{3,2},{4,5},{5,4},{6,7},{7,6},{8,9},{9,8},{10,11... | collective-permute-start | bytes 3145736 | tf_op jit(solution)/shard_map/ppermute | solution.py:415
  62.0 1.2 copy-start.7
  68.9 15.3 %copy-start = (bf16[64,8192]{1,0:T(8,128)(2,1)}, bf16[64,8192]{1,0:T(8,128)(2,1)S(1)}, u32[]{:S(2)}) copy-start(bf16[64,8192]{1,0:T(8,128)(2,1)S(1)} %direct_sweeps.3.refs_5_.refs_3_.refs_1_) | copy-start | bytes 3145732
  68.9 15.3 %copy-start.11 = (bf16[192,16,128]{2,1,0:T(8,128)(2,1)}, bf16[192,16,128]{2,1,0:T(8,128)(2,1)S(1)}, u32[]{:S(2)}) copy-start(bf16[192,16,128]{2,1,0:T(8,128)(2,1)S(1)} %collective-permute-done.11.refs_2_) | copy-start | bytes 2359300
  68.9 28.8 %collective-permute-start.12 = (bf16[192,16,128]{2,1,0:T(8,128)(2,1)}, bf16[192,16,128]{2,1,0:T(8,128)(2,1)}, u32[]{:S(2)}, u32[]{:S(2)}) collective-permute-start(bf16[192,16,128]{2,1,0:T(8,128)(2,1)} %join.5.refs_0_), channel_id=1, source_target_pairs={{4,12},{6,14},{12,20},{14,22},{20,28},{22,30},{8,0},{10,2},{16,8},... | collective-permute-start | bytes 2359304 | tf_op jit(solution)/shard_map/ppermute | solution.py:420
  77.2 0.9 copy-start.13
  78.1 20.9 %collective-permute-start.15 = (bf16[192,16,128]{2,1,0:T(8,128)(2,1)}, bf16[192,16,128]{2,1,0:T(8,128)(2,1)}, u32[]{:S(2)}, u32[]{:S(2)}) collective-permute-start(bf16[192,16,128]{2,1,0:T(8,128)(2,1)} %collective-permute-done.8.refs_1_), channel_id=1, source_target_pairs={{0,8},{2,10},{8,16},{10,18},{16,24},{18,26},{12,4},{14,6},{20,12},... | collective-permute-start | bytes 2359304 | tf_op jit(solution)/shard_map/ppermute | solution.py:421
  84.2 14.9 %collective-permute-start.9 = (bf16[128,16,128]{2,1,0:T(8,128)(2,1)}, bf16[128,16,128]{2,1,0:T(8,128)(2,1)}, u32[]{:S(2)}, u32[]{:S(2)}) collective-permute-start(bf16[128,16,128]{2,1,0:T(8,128)(2,1)} %join.4.refs_0_), channel_id=1, source_target_pairs={{0,4},{2,6},{4,0},{6,2},{8,12},{10,14},{12,8},{14,10},{16,20},{18,... | collective-permute-start | bytes 1572872 | tf_op jit(solution)/shard_map/ppermute | solution.py:412
  84.2 29.5 %collective-permute-start.10 = (bf16[64,8192]{1,0:T(8,128)(2,1)}, bf16[64,8192]{1,0:T(8,128)(2,1)S(1)}, u32[]{:S(2)}, u32[]{:S(2)}) collective-permute-start(bf16[64,8192]{1,0:T(8,128)(2,1)} %copy-done), channel_id=1, source_target_pairs={{0,1},{1,0},{2,3},{3,2},{4,5},{5,4},{6,7},{7,6},{8,9},{9,8},{10,11... | collective-permute-start | bytes 3145736 | tf_op jit(solution)/shard_map/ppermute | solution.py:415
  85.9 1.1 copy-start.12
  87.0 1.1 copy-start.14
  88.2 0.8 copy-start.20
  97.7 32.3 %collective-permute-start.19 = (bf16[96,8192]{1,0:T(8,128)(2,1)}, bf16[96,8192]{1,0:T(8,128)(2,1)}, u32[]{:S(2)}, u32[]{:S(2)}) collective-permute-start(bf16[96,8192]{1,0:T(8,128)(2,1)} %adjoint_sweeps.4.refs_0_), channel_id=1, source_target_pairs={{0,2},{2,0},{4,6},{6,4},{8,10},{10,8},{12,14},{14,12},{16,18},{18,... | collective-permute-start | bytes 4718600 | tf_op jit(solution)/shard_map/ppermute | solution.py:412
  97.7 16.9 %collective-permute-start.13 = (bf16[128,16,128]{2,1,0:T(8,128)(2,1)}, bf16[128,16,128]{2,1,0:T(8,128)(2,1)}, u32[]{:S(2)}, u32[]{:S(2)}) collective-permute-start(bf16[128,16,128]{2,1,0:T(8,128)(2,1)} %join.4.refs_0_), channel_id=1, source_target_pairs={{4,12},{6,14},{12,20},{14,22},{20,28},{22,30},{8,0},{10,2},{16,8},... | collective-permute-start | bytes 1572872 | tf_op jit(solution)/shard_map/ppermute | solution.py:420
  99.0 16.4 %collective-permute-start.16 = (bf16[128,16,128]{2,1,0:T(8,128)(2,1)}, bf16[128,16,128]{2,1,0:T(8,128)(2,1)}, u32[]{:S(2)}, u32[]{:S(2)}) collective-permute-start(bf16[128,16,128]{2,1,0:T(8,128)(2,1)} %collective-permute-done.9.refs_1_), channel_id=1, source_target_pairs={{0,8},{2,10},{8,16},{10,18},{16,24},{18,26},{12,4},{14,6},{20,12},... | collective-permute-start | bytes 1572872 | tf_op jit(solution)/shard_map/ppermute | solution.py:421
  113.6 16.4 %collective-permute-start.20 = (bf16[96,8192]{1,0:T(8,128)(2,1)}, bf16[96,8192]{1,0:T(8,128)(2,1)}, u32[]{:S(2)}, u32[]{:S(2)}) collective-permute-start(bf16[96,8192]{1,0:T(8,128)(2,1)} %adjoint_sweeps.5.refs_1_), channel_id=1, source_target_pairs={{0,2},{2,0},{4,6},{6,4},{8,10},{10,8},{12,14},{14,12},{16,18},{18,... | collective-permute-start | bytes 4718600 | tf_op jit(solution)/shard_map/ppermute | solution.py:412
  113.7 1.0 copy-start.2
  115.5 0.8 copy-start.21
  116.4 6.8 %copy-start.24 = (f32[64]{0:T(128)S(1)}, f32[64]{0:T(128)}, u32[]{:S(2)}) copy-start(f32[64]{0:T(128)} %param.17) | copy-start | bytes 772
  116.4 6.8 %copy-start.1 = (bf16[64,8192]{1,0:T(8,128)(2,1)S(1)}, bf16[64,8192]{1,0:T(8,128)(2,1)}, u32[]{:S(2)}) copy-start(bf16[64,8192]{1,0:T(8,128)(2,1)} %copy-done) | copy-start | bytes 3145732
  116.4 6.8 %copy-start.9 = (f32[1024,64]{0,1:T(8,128)S(1)}, f32[1024,64]{0,1:T(8,128)}, u32[]{:S(2)}) copy-start(f32[1024,64]{0,1:T(8,128)} %param.16) | copy-start | bytes 786436
  123.1 11.8 %collective-permute-start.17 = (bf16[64,8192]{1,0:T(8,128)(2,1)}, bf16[64,8192]{1,0:T(8,128)(2,1)}, u32[]{:S(2)}, u32[]{:S(2)}) collective-permute-start(bf16[64,8192]{1,0:T(8,128)(2,1)} %adjoint_sweeps.3.refs_0_), channel_id=1, source_target_pairs={{0,2},{2,0},{4,6},{6,4},{8,10},{10,8},{12,14},{14,12},{16,18},{18,... | collective-permute-start | bytes 3145736 | tf_op jit(solution)/shard_map/ppermute | solution.py:412
  123.2 1.2 copy-start.3
  124.5 5.5 %copy-start.8 = (f32[1024,64]{0,1:T(8,128)S(1)}, f32[1024,64]{0,1:T(8,128)}, u32[]{:S(2)}) copy-start(f32[1024,64]{0,1:T(8,128)} %param.15) | copy-start | bytes 786436
  125.6 16.4 %collective-permute-start.24 = (bf16[64,1024]{1,0:T(8,128)(2,1)S(1)}, bf16[64,1024]{1,0:T(8,128)(2,1)S(1)}, u32[]{:S(2)}, u32[]{:S(2)}) collective-permute-start(bf16[64,1024]{1,0:T(8,128)(2,1)S(1)} %get-tuple-element.62), channel_id=1, source_target_pairs={{0,2},{2,0},{4,6},{6,4},{8,10},{10,8},{12,14},{14,12},{16,18},{18,... | collective-permute-start | bytes 393224 | tf_op jit(solution)/shard_map/ppermute | solution.py:412
  126.2 16.5 %collective-permute-start.25 = (bf16[64,1024]{1,0:T(8,128)(2,1)S(1)}, bf16[64,1024]{1,0:T(8,128)(2,1)S(1)}, u32[]{:S(2)}, u32[]{:S(2)}) collective-permute-start(bf16[64,1024]{1,0:T(8,128)(2,1)S(1)} %get-tuple-element.63), channel_id=1, source_target_pairs={{0,4},{2,6},{4,0},{6,2},{8,12},{10,14},{12,8},{14,10},{16,20},{18,... | collective-permute-start | bytes 393224 | tf_op jit(solution)/shard_map/ppermute | solution.py:412
  130.0 12.7 %collective-permute-start.26 = (bf16[64,1024]{1,0:T(8,128)(2,1)S(1)}, bf16[64,1024]{1,0:T(8,128)(2,1)S(1)}, u32[]{:S(2)}, u32[]{:S(2)}) collective-permute-start(bf16[64,1024]{1,0:T(8,128)(2,1)S(1)} %get-tuple-element.64), channel_id=1, source_target_pairs={{0,6},{2,4},{4,2},{6,0},{8,14},{10,12},{12,10},{14,8},{16,22},{18,... | collective-permute-start | bytes 393224 | tf_op jit(solution)/shard_map/ppermute | solution.py:412
  138.8 8.2 %collective-permute-start.21 = (bf16[512,64]{1,0:T(8,128)(2,1)S(1)}, bf16[512,64]{1,0:T(8,128)(2,1)S(1)}, u32[]{:S(2)}, u32[]{:S(2)}) collective-permute-start(bf16[512,64]{1,0:T(8,128)(2,1)S(1)} %get-tuple-element.58), channel_id=1, source_target_pairs={{0,8},{2,10},{4,12},{6,14},{8,16},{10,18},{12,20},{14,22},{16,24},... | collective-permute-start | bytes 196616 | tf_op jit(solution)/shard_map/ppermute | solution.py:501
  139.8 12.1 %collective-permute-start.22 = (bf16[512,64]{1,0:T(8,128)(2,1)S(1)}, bf16[512,64]{1,0:T(8,128)(2,1)S(1)}, u32[]{:S(2)}, u32[]{:S(2)}) collective-permute-start(bf16[512,64]{1,0:T(8,128)(2,1)S(1)} %get-tuple-element.59), channel_id=1, source_target_pairs={{0,16},{2,18},{4,20},{6,22},{8,24},{10,26},{12,28},{14,30},{16,0},... | collective-permute-start | bytes 196616 | tf_op jit(solution)/shard_map/ppermute | solution.py:501
  142.0 9.8 %collective-permute-start.23 = (bf16[512,64]{1,0:T(8,128)(2,1)S(1)}, bf16[512,64]{1,0:T(8,128)(2,1)S(1)}, u32[]{:S(2)}, u32[]{:S(2)}) collective-permute-start(bf16[512,64]{1,0:T(8,128)(2,1)S(1)} %get-tuple-element.60), channel_id=1, source_target_pairs={{0,24},{2,26},{4,28},{6,30},{8,0},{10,2},{12,4},{14,6},{16,8},{18,... | collective-permute-start | bytes 196616 | tf_op jit(solution)/shard_map/ppermute | solution.py:501
  143.5 9.2 %collective-permute-start.27 = (bf16[64,1024]{1,0:T(8,128)(2,1)}, bf16[64,1024]{1,0:T(8,128)(2,1)S(1)}, u32[]{:S(2)}, u32[]{:S(2)}) collective-permute-start(bf16[64,1024]{1,0:T(8,128)(2,1)} %bitcast.22), channel_id=1, source_target_pairs={{0,1},{1,0},{2,3},{3,2},{4,5},{5,4},{6,7},{7,6},{8,9},{9,8},{10,11... | collective-permute-start | bytes 393224 | tf_op jit(solution)/shard_map/ppermute | solution.py:415

commit v4 on v3

--- a/solution.py
+++ b/solution.py
@@ -11,7 +11,7 @@
 GROUP = 4
 HALO = 2
 STEP = 32
-SWEEP_COST = 5000
+SWEEP_COST = 6500
 CHUNKS = (3, 3, 2)
 EXTRA = 4
 VMEM = 20 * 1024 * 1024
@@ -236,27 +236,29 @@
     member, core, share = info[0], info[1], info[2]
     adjoint = [ref for pair in zip(own, far) for ref in pair]
     rows_total, cells = sum(ref.shape[0] for ref in adjoint), own[0].shape[1]
-    count, _, width = pieces.shape
+    count, width, _ = pieces.shape
     depth = cells // GROUP
     dims = (((1,), (1,)), ((), ()))
-    total = jnp.zeros((rows_total, count * width), jnp.float32)
+    total = jnp.zeros((count * width, rows_total), jnp.float32)
     for plane in range(GROUP):
         rows, cols = slab(adjoint, plane * depth, depth), slab(direct, plane * depth, depth)
-        total = total + lax.dot_general(rows, cols, dims, preferred_element_type=jnp.float32)
+        total = total + lax.dot_general(cols, rows, dims, preferred_element_type=jnp.float32)
     per_share = factors.shape[1] // shares
     window = factors[:, pl.ds(pl.multiple_of(share * per_share, per_share), per_share)]
     window = scaled_factors(window[:, start : start + rows_total], singular)
-    left, at = [], 0
+
+    def by_half(mine, other):
+        return [jnp.where(core == 0, mine, other), jnp.where(core == 0, other, mine)]
+
+    left, ordered, at = [], [], 0
     for ref in own:
-        half = ref.shape[0]
-        for side in range(2):
-            spot = pl.ds(pl.multiple_of(at + jnp.where(side == 0, core, 1 - core) * half, 16), half)
-            held = at + side * half
-            for part in range(count):
-                pieces[part, spot, :] = total[held : held + half, part * width : (part + 1) * width]
-        lower, upper = window[:, at : at + half], window[:, at + half : at + 2 * half]
-        left += [jnp.where(core == 0, lower, upper), jnp.where(core == 0, upper, lower)]
-        at += 2 * half
+        middle, end = at + ref.shape[0], at + 2 * ref.shape[0]
+        left += by_half(window[:, at:middle], window[:, middle:end])
+        ordered += by_half(total[:, at:middle], total[:, middle:end])
+        at = end
+    ordered = jnp.concatenate(ordered, axis=1)
+    for part in range(count):
+        pieces[part] = ordered[part * width : (part + 1) * width]
     term = jnp.dot(
         jnp.concatenate(left, axis=1), slab(adjoint, member * depth, depth), preferred_element_type=jnp.float32
     )
@@ -267,11 +269,11 @@
     for number in range(len(sent) + 1):
         index = info[4 + number]
         if number == 0:
-            kept[0:start, :] = older[index]
-            kept[start:, :] = pieces[index]
+            kept[:, 0:start] = older[index]
+            kept[:, start:] = pieces[index]
         else:
-            sent[number - 1][0:start, :] = older[index].astype(jnp.bfloat16)
-            sent[number - 1][start:, :] = pieces[index].astype(jnp.bfloat16)
+            sent[number - 1][:, 0:start] = older[index].astype(jnp.bfloat16)
+            sent[number - 1][:, start:] = pieces[index].astype(jnp.bfloat16)
     wide = depth // shares
     for step in range(shares):
         piece = modes[:, pl.ds(pl.multiple_of(((share + step) % shares) * wide, wide), wide)]
@@ -288,7 +290,7 @@
     mode_count, rows = factors.shape[0], factors.shape[1] // shares
     depth = cells // GROUP
     height = 2 * sum(a.shape[0] for a in own)
-    pieces = (shares * blocks, height, width)
+    pieces = (shares * blocks, width, height)
     operands = [info, factors, singular, *own, *far, *direct]
     if older is None:
         out_shape = [
@@ -298,8 +300,8 @@
         scratch = []
     else:
         operands += older
-        out_shape = [jax.ShapeDtypeStruct((rows, width), jnp.float32)]
-        out_shape += [jax.ShapeDtypeStruct((rows, width), jnp.bfloat16)] * (layers - 1)
+        out_shape = [jax.ShapeDtypeStruct((width, rows), jnp.float32)]
+        out_shape += [jax.ShapeDtypeStruct((width, rows), jnp.bfloat16)] * (layers - 1)
         out_shape += [
             jax.ShapeDtypeStruct((mode_count, depth // shares), jnp.float32),
             jax.ShapeDtypeStruct((shares - 1, mode_count, depth // shares), jnp.bfloat16),
@@ -499,7 +501,7 @@
     for step in range(1, layers):
         pairs = [(i, (i + GROUP * step) % n_space) for i in range(n_space)]
         kept = kept + lax.ppermute(sent[step - 1], "space", pairs).astype(jnp.float32)
-    gram = kept * weight
+    gram = (kept * weight).T
     for step in range(1, n_snap):
         kept_modes = kept_modes + around(sent_modes[step - 1], step).astype(jnp.float32)
     adjoint_modes = kept_modes.reshape(mode_count, 1, rows_y, width_z)

time: 155 us -> 148 us (0.955)
  waiting for transfers between devices: 40.2 us -> 33.4 us
  local copies, waits for them, and re-layouts: 14.8 us -> 10.5 us
  starting transfers between devices: 46.1 us -> 48.6 us
  Pallas kernels: 50.8 us -> 52.4 us
    unnamed x55 -> x52, local copies, waits for them, and re-layouts: 13.9 us -> 9.56 us
    ppermute x3, waiting for transfers between devices: 7.09 us -> 2.93 us  [per_device(): lax.ppermute(sent[step - 1], 'space', pairs).astype(jnp.float32)]
    ppermute x13, starting transfers between devices: 10.6 us -> 13.4 us  [swap(): return lax.ppermute(array, 'space', [(i, i ^ mask) for i in range(n_space)])]
    ppermute x13, waiting for transfers between devices: 24 us -> 21.6 us  [swap(): return lax.ppermute(array, 'space', [(i, i ^ mask) for i in range(n_space)])]
    pallas_call x14, Pallas kernels: 50.8 us -> 52.4 us  [call(): pl.pallas_call(kernel, in_specs=in_specs, out_specs=jax.tree.map(lambda _...]
  transfers between devices with their start and end apart: 28 -> 28, of which waited for: 9 -> 12; matrix products, arithmetic and copies ran while one was open for 2% -> 2% of each run, Pallas kernels for 33% -> 35%
where the time goes in v4:
time: 148 us; the launch traced here: 147 us
  Pallas kernels  52.4 us (35%)
  starting transfers between devices  48.6 us (33%)
  waiting for transfers between devices  33.4 us (23%)
  local copies, waits for them, and re-layouts  10.5 us (7%)
    pallas_call x14, Pallas kernels, call(): pl.pallas_call(kernel, in_specs=in_specs, out_specs=jax.tree.map(lambda _...  52.4 us
    ppermute x13, waiting for transfers between devices, swap(): return lax.ppermute(array, 'space', [(i, i ^ mask) for i in range(n_space)])  21.6 us
    ppermute x5, starting transfers between devices, per_device(): lax.ppermute(array, 'space', upper(ups, 0) + upper(downs, 1))  21.2 us
    ppermute x13, starting transfers between devices, swap(): return lax.ppermute(array, 'space', [(i, i ^ mask) for i in range(n_space)])  13.4 us
    unnamed x52, local copies, waits for them, and re-layouts  9.56 us
    ppermute x5, waiting for transfers between devices, per_device(): lax.ppermute(array, 'space', upper(ups, 0) + upper(downs, 1))  8.48 us
    ppermute x4, starting transfers between devices, per_device(): lax.ppermute(array, 'space', upper(ups, 1) + upper(downs, 0))  5.27 us
    ppermute x3, starting transfers between devices, per_device(): lax.ppermute(sent[step - 1], 'space', pairs).astype(jnp.float32)  4.38 us
  transfers between devices with their start and end apart: 28, of which 12 were waited for; matrix products, arithmetic and copies ran while one was open for 2% of the time, Pallas kernels for 35%

profile of v4, /device:TPU:0, one launch (start us, length us, event | category | flops | bytes accessed | tf_op | source)
XLA Modules:
  0.0 147.0 jit_solution(16125882290826466801)
XLA Ops:
  0.9 0.1 stack.62.info.token
  1.0 1.6 %copy-done = bf16[512,1,16,128]{3,2,1,0:T(8,128)(2,1)S(1)} copy-done((bf16[512,1,16,128]{3,2,1,0:T(8,128)(2,1)S(1)}, bf16[512,1,16,128]{3,2,1,0:T(8,128)(2,1)}, u32[]{:S(2)}) %copy-start) | copy-done | bytes 2097176
  2.6 0.7 copy-done.6
  3.3 0.9 pack.2
  4.2 0.5 collective-permute-start
  4.7 2.6 %collective-permute-start.2 = (bf16[132,16,128]{2,1,0:T(8,128)(2,1)S(1)}, bf16[132,16,128]{2,1,0:T(8,128)(2,1)S(1)}, u32[]{:S(2)}, u32[]{:S(2)}) collective-permute-start(bf16[132,16,128]{2,1,0:T(8,128)(2,1)S(1)} %get-tuple-element.40), channel_id=1, source_target_pairs={{0,4},{2,6},{4,0},{6,2},{8,12},{10,14},{12,8},{14,10},{16,20},{18,... | collective-permute-start | bytes 1622024 | tf_op jit(solution)/shard_map/ppermute | solution.py:414
  7.3 1.4 pack.3
  8.7 0.2 collective-permute-start.1
  9.1 1.4 collective-permute-start.6
  10.5 4.7 %collective-permute-start.3 = (bf16[132,16,128]{2,1,0:T(8,128)(2,1)S(1)}, bf16[132,16,128]{2,1,0:T(8,128)(2,1)S(1)}, u32[]{:S(2)}, u32[]{:S(2)}) collective-permute-start(bf16[132,16,128]{2,1,0:T(8,128)(2,1)S(1)} %get-tuple-element.41), channel_id=1, source_target_pairs={{0,6},{2,4},{4,2},{6,0},{8,14},{10,12},{12,10},{14,8},{16,22},{18,... | collective-permute-start | bytes 1622024 | tf_op jit(solution)/shard_map/ppermute | solution.py:414
  15.2 5.2 %collective-permute-done.2.refs_1_ = bf16[132,16,128]{2,1,0:T(8,128)(2,1)S(1)} collective-permute-done((bf16[132,16,128]{2,1,0:T(8,128)(2,1)S(1)}, bf16[132,16,128]{2,1,0:T(8,128)(2,1)S(1)}, u32[]{:S(2)}, u32[]{:S(2)}) %collective-permute-start.2) | collective-permute-done | bytes 540704 | tf_op jit(solution)/shard_map/ppermute | solution.py:414
  20.5 3.9 %collective-permute-start.4 = (bf16[132,16,128]{2,1,0:T(8,128)(2,1)S(1)}, bf16[132,16,128]{2,1,0:T(8,128)(2,1)S(1)}, u32[]{:S(2)}, u32[]{:S(2)}) collective-permute-start(bf16[132,16,128]{2,1,0:T(8,128)(2,1)S(1)} %collective-permute-done.2.refs_1_), channel_id=1, source_target_pairs={{0,8},{2,10},{8,16},{10,18},{16,24},{18,26},{12,4},{14,6},{20,12},... | collective-permute-start | bytes 1622024 | tf_op jit(solution)/shard_map/ppermute | solution.py:423
  24.4 7.1 %collective-permute-done.3.refs_2_ = bf16[132,16,128]{2,1,0:T(8,128)(2,1)S(1)} collective-permute-done((bf16[132,16,128]{2,1,0:T(8,128)(2,1)S(1)}, bf16[132,16,128]{2,1,0:T(8,128)(2,1)S(1)}, u32[]{:S(2)}, u32[]{:S(2)}) %collective-permute-start.3) | collective-permute-done | bytes 540704 | tf_op jit(solution)/shard_map/ppermute | solution.py:414
  31.5 4.3 %collective-permute-start.7 = (bf16[132,16,128]{2,1,0:T(8,128)(2,1)S(1)}, bf16[132,16,128]{2,1,0:T(8,128)(2,1)}, u32[]{:S(2)}, u32[]{:S(2)}) collective-permute-start(bf16[132,16,128]{2,1,0:T(8,128)(2,1)S(1)} %collective-permute-done.3.refs_2_), channel_id=1, source_target_pairs={{0,8},{2,10},{8,16},{10,18},{16,24},{18,26},{12,4},{14,6},{20,12},... | collective-permute-start | bytes 1622024 | tf_op jit(solution)/shard_map/ppermute | solution.py:423
  35.8 0.9 join.6.refs_0_
  36.8 0.8 copy-done.16
  37.6 0.9 collective-permute-start.5
  38.5 0.1 select_reduce_fusion
  38.6 0.1 reshape.31
  38.7 0.1 broadcast_in_dim.28
  38.9 1.0 join.5.refs_0_
  39.9 1.3 collective-permute-start.11
  41.2 6.2 %collective-permute-done.7.refs_5_ = bf16[132,16,128]{2,1,0:T(8,128)(2,1)} collective-permute-done((bf16[132,16,128]{2,1,0:T(8,128)(2,1)S(1)}, bf16[132,16,128]{2,1,0:T(8,128)(2,1)}, u32[]{:S(2)}, u32[]{:S(2)}) %collective-permute-start.7) | collective-permute-done | bytes 540704 | tf_op jit(solution)/shard_map/ppermute | solution.py:423
  47.5 1.0 copy-done.14
  48.6 5.5 %direct_sweeps.2 = (bf16[64,8192]{1,0:T(8,128)(2,1)S(1)}, f32[8,16,128]{2,1,0:T(8,128)S(1)}) custom-call(s32[8]{0:T(128)S(1)} %stack.71.place, bf16[264,16,128]{2,1,0:T(8,128)(2,1)S(1)} %join.7.refs_0_, bf16[132,16,128]{2,1,0:T(8,128)(2,1)S(1)} %copy-done.12, bf16[132,16,128]{2,1,0:T(8,128)(2,1)S(1)} %copy-done.14, ...), custom_call_target="tpu_custom_call" | custom-call | flops 3407872000 | bytes 1024 | tf_op jit(solution)/shard_map/direct_sweeps/pallas_call | solution.py:25
  54.1 3.7 %collective-permute-done.5.refs_1_ = bf16[192,16,128]{2,1,0:T(8,128)(2,1)} collective-permute-done((bf16[192,16,128]{2,1,0:T(8,128)(2,1)}, bf16[192,16,128]{2,1,0:T(8,128)(2,1)}, u32[]{:S(2)}, u32[]{:S(2)}) %collective-permute-start.5) | collective-permute-done | bytes 786464 | tf_op jit(solution)/shard_map/ppermute | solution.py:414
  57.8 0.2 collective-permute-start.8
  58.0 2.7 %collective-permute-start.14 = (bf16[192,16,128]{2,1,0:T(8,128)(2,1)}, bf16[192,16,128]{2,1,0:T(8,128)(2,1)S(1)}, u32[]{:S(2)}, u32[]{:S(2)}) collective-permute-start(bf16[192,16,128]{2,1,0:T(8,128)(2,1)} %collective-permute-done.5.refs_1_), channel_id=1, source_target_pairs={{0,8},{2,10},{8,16},{10,18},{16,24},{18,26},{12,4},{14,6},{20,12},... | collective-permute-start | bytes 2359304 | tf_op jit(solution)/shard_map/ppermute | solution.py:423
  60.8 1.6 %collective-permute-start.18 = (bf16[64,8192]{1,0:T(8,128)(2,1)S(1)}, bf16[64,8192]{1,0:T(8,128)(2,1)S(1)}, u32[]{:S(2)}, u32[]{:S(2)}) collective-permute-start(bf16[64,8192]{1,0:T(8,128)(2,1)S(1)} %get-tuple-element.44.refs_4_.refs_2_.refs_0_), channel_id=1, source_target_pairs={{0,1},{1,0},{2,3},{3,2},{4,5},{5,4},{6,7},{7,6},{8,9},{9,8},{10,11... | collective-permute-start | bytes 3145736 | tf_op jit(solution)/shard_map/ppermute | solution.py:417
  62.4 1.2 copy-done.3
  63.6 6.4 %direct_sweeps.3.refs_5_.refs_3_.refs_1_ = bf16[64,8192]{1,0:T(8,128)(2,1)} custom-call(s32[8]{0:T(128)S(1)} %stack.71.place, bf16[264,16,128]{2,1,0:T(8,128)(2,1)S(1)} %copy-done.3, bf16[132,16,128]{2,1,0:T(8,128)(2,1)S(1)} %copy-done.12, bf16[132,16,128]{2,1,0:T(8,128)(2,1)S(1)} %copy-done.15, bf16[264,16,128]{2,1,0:T(8,128)(2,1)} %collective-permute-done.6.refs_3_, ...), custom_call_target="tpu_custom_call" | custom-call | flops 3407872000 | bytes 1024 | tf_op jit(solution)/shard_map/direct_sweeps/pallas_call | solution.py:25
  70.0 0.9 copy-done.7
  70.9 1.3 collective-permute-start.12
  72.2 5.0 %collective-permute-done.8.refs_1_ = bf16[192,16,128]{2,1,0:T(8,128)(2,1)} collective-permute-done((bf16[192,16,128]{2,1,0:T(8,128)(2,1)}, bf16[192,16,128]{2,1,0:T(8,128)(2,1)}, u32[]{:S(2)}, u32[]{:S(2)}) %collective-permute-start.8) | collective-permute-done | bytes 786464 | tf_op jit(solution)/shard_map/ppermute | solution.py:414
  77.2 0.9 copy-done.9
  78.1 5.1 %collective-permute-start.15 = (bf16[192,16,128]{2,1,0:T(8,128)(2,1)}, bf16[192,16,128]{2,1,0:T(8,128)(2,1)}, u32[]{:S(2)}, u32[]{:S(2)}) collective-permute-start(bf16[192,16,128]{2,1,0:T(8,128)(2,1)} %collective-permute-done.8.refs_1_), channel_id=1, source_target_pairs={{0,8},{2,10},{8,16},{10,18},{16,24},{18,26},{12,4},{14,6},{20,12},... | collective-permute-start | bytes 2359304 | tf_op jit(solution)/shard_map/ppermute | solution.py:423
  83.2 0.8 join.4.refs_0_
  84.1 1.5 %collective-permute-start.10 = (bf16[64,8192]{1,0:T(8,128)(2,1)}, bf16[64,8192]{1,0:T(8,128)(2,1)S(1)}, u32[]{:S(2)}, u32[]{:S(2)}) collective-permute-start(bf16[64,8192]{1,0:T(8,128)(2,1)} %direct_sweeps.3.refs_5_.refs_3_.refs_1_), channel_id=1, source_target_pairs={{0,1},{1,0},{2,3},{3,2},{4,5},{5,4},{6,7},{7,6},{8,9},{9,8},{10,11... | collective-permute-start | bytes 3145736 | tf_op jit(solution)/shard_map/ppermute | solution.py:417
  85.7 8.7 %adjoint_sweeps.4.refs_0_ = bf16[96,8192]{1,0:T(8,128)(2,1)} custom-call(s32[8]{0:T(128)S(1)} %stack.71.place, bf16[192,16,128]{2,1,0:T(8,128)(2,1)} %join.6.refs_0_, bf16[192,16,128]{2,1,0:T(8,128)(2,1)} %collective-permute-done.5.refs_1_, bf16[192,16,128]{2,1,0:T(8,128)(2,1)S(1)} %copy-done.8, bf16[192,16,128]{2,1,0:T(8,128)(2,1)S(1)} %copy-done.10, ...), custom_call_target="tpu_custom_call" | custom-call | flops 5111808000 | bytes 1024 | tf_op jit(solution)/shard_map/adjoint_sweeps/pallas_call | solution.py:25
  94.4 1.3 collective-permute-start.13
  95.7 0.4 collective-permute-done.9.refs_1_
  96.1 1.6 %collective-permute-done.15.refs_3_ = bf16[192,16,128]{2,1,0:T(8,128)(2,1)} collective-permute-done((bf16[192,16,128]{2,1,0:T(8,128)(2,1)}, bf16[192,16,128]{2,1,0:T(8,128)(2,1)}, u32[]{:S(2)}, u32[]{:S(2)}) %collective-permute-start.15) | collective-permute-done | bytes 786464 | tf_op jit(solution)/shard_map/ppermute | solution.py:423
  97.7 5.2 %collective-permute-start.16 = (bf16[128,16,128]{2,1,0:T(8,128)(2,1)}, bf16[128,16,128]{2,1,0:T(8,128)(2,1)}, u32[]{:S(2)}, u32[]{:S(2)}) collective-permute-start(bf16[128,16,128]{2,1,0:T(8,128)(2,1)} %collective-permute-done.9.refs_1_), channel_id=1, source_target_pairs={{0,8},{2,10},{8,16},{10,18},{16,24},{18,26},{12,4},{14,6},{20,12},... | collective-permute-start | bytes 1572872 | tf_op jit(solution)/shard_map/ppermute | solution.py:423
  102.9 9.1 %adjoint_sweeps.5.refs_1_ = bf16[96,8192]{1,0:T(8,128)(2,1)} custom-call(s32[8]{0:T(128)S(1)} %stack.71.place, bf16[192,16,128]{2,1,0:T(8,128)(2,1)} %join.5.refs_0_, bf16[192,16,128]{2,1,0:T(8,128)(2,1)} %collective-permute-done.8.refs_1_, bf16[192,16,128]{2,1,0:T(8,128)(2,1)} %collective-permute-done.12.refs_2_, ...), custom_call_target="tpu_custom_call" | custom-call | flops 5111808000 | bytes 1024 | tf_op jit(solution)/shard_map/adjoint_sweeps/pallas_call | solution.py:25
  112.2 0.6 collective-permute-done.16.refs_3_
  112.9 0.8 copy-done.20
  113.7 6.7 %adjoint_sweeps.3.refs_0_ = bf16[64,8192]{1,0:T(8,128)(2,1)} custom-call(s32[8]{0:T(128)S(1)} %stack.71.place, bf16[128,16,128]{2,1,0:T(8,128)(2,1)} %join.4.refs_0_, bf16[128,16,128]{2,1,0:T(8,128)(2,1)} %collective-permute-done.9.refs_1_, bf16[128,16,128]{2,1,0:T(8,128)(2,1)} %collective-permute-done.13.refs_2_, ...), custom_call_target="tpu_custom_call" | custom-call | flops 3407872000 | bytes 1024 | tf_op jit(solution)/shard_map/adjoint_sweeps/pallas_call | solution.py:25
  120.4 0.1 copy.23.singular
  120.5 1.9 %direct_modes_part.1 = (f32[64,1024]{1,0:T(8,128)S(1)}, bf16[64,1024]{1,0:T(8,128)(2,1)S(1)}, bf16[64,1024]{1,0:T(8,128)(2,1)S(1)}, bf16[64,1024]{1,0:T(8,128)(2,1)S(1)}) custom-call(s32[8]{0:T(128)S(1)} %stack.62.info.token, f32[64,1024]{1,0:T(8,128)S(1)} %bitcast.42, f32[64,1]{1,0:T(8,128)S(1)} %copy.23.singular, ...), custom_call_target="tpu_custom_call" | custom-call | flops 524288 | bytes 1024 | tf_op jit(solution)/shard_map/direct_modes_part/pallas_call | solution.py:25
  122.4 0.6 collective-permute-start.24
  123.0 3.7 %collective-permute-start.25 = (bf16[64,1024]{1,0:T(8,128)(2,1)S(1)}, bf16[64,1024]{1,0:T(8,128)(2,1)S(1)}, u32[]{:S(2)}, u32[]{:S(2)}) collective-permute-start(bf16[64,1024]{1,0:T(8,128)(2,1)S(1)} %get-tuple-element.63), channel_id=1, source_target_pairs={{0,4},{2,6},{4,0},{6,2},{8,12},{10,14},{12,8},{14,10},{16,20},{18,... | collective-permute-start | bytes 393224 | tf_op jit(solution)/shard_map/ppermute | solution.py:414
  126.7 5.7 %gram_part.2 = (f32[4,64,384]{2,1,0:T(8,128)S(1)}, f32[64,2048]{1,0:T(8,128)S(1)}) custom-call(s32[8]{0:T(128)S(1)} %stack.62.info.token, f32[64,1024]{1,0:T(8,128)S(1)} %bitcast.40, f32[64,1]{1,0:T(8,128)S(1)} %copy.23.singular, bf16[96,8192]{1,0:T(8,128)(2,1)} %adjoint_sweeps.4.refs_0_, bf16[96,8192]{1,0:T(8,128)(2,1)} %adjoint_sweeps.5.refs_1_, ...), custom_call_target="tpu_custom_call" | custom-call | flops 3145728 | bytes 1024 | tf_op jit(solution)/shard_map/gram_part/pallas_call | solution.py:25
  132.4 3.3 %gram_part.3 = (f32[64,512]{1,0:T(8,128)S(1)}, bf16[64,512]{1,0:T(8,128)(2,1)S(1)}, bf16[64,512]{1,0:T(8,128)(2,1)S(1)}, bf16[64,512]{1,0:T(8,128)(2,1)S(1)}, f3...) custom-call(s32[8]{0:T(128)S(1)} %stack.62.info.token, f32[64,1024]{1,0:T(8,128)S(1)} %bitcast.41, ...), custom_call_target="tpu_custom_call" | custom-call | flops 1048576 | bytes 1024 | tf_op jit(solution)/shard_map/gram_part/pallas_call | solution.py:25
  135.7 1.7 %collective-permute-start.21 = (bf16[64,512]{1,0:T(8,128)(2,1)S(1)}, bf16[64,512]{1,0:T(8,128)(2,1)S(1)}, u32[]{:S(2)}, u32[]{:S(2)}) collective-permute-start(bf16[64,512]{1,0:T(8,128)(2,1)S(1)} %get-tuple-element.58), channel_id=1, source_target_pairs={{0,8},{2,10},{4,12},{6,14},{8,16},{10,18},{12,20},{14,22},{16,24},... | collective-permute-start | bytes 196616 | tf_op jit(solution)/shard_map/ppermute | solution.py:503
  137.4 2.0 %collective-permute-start.22 = (bf16[64,512]{1,0:T(8,128)(2,1)S(1)}, bf16[64,512]{1,0:T(8,128)(2,1)S(1)}, u32[]{:S(2)}, u32[]{:S(2)}) collective-permute-start(bf16[64,512]{1,0:T(8,128)(2,1)S(1)} %get-tuple-element.59), channel_id=1, source_target_pairs={{0,16},{2,18},{4,20},{6,22},{8,24},{10,26},{12,28},{14,30},{16,0},... | collective-permute-start | bytes 196616 | tf_op jit(solution)/shard_map/ppermute | solution.py:503
  139.4 0.7 collective-permute-start.23
  140.2 0.8 copy.27
  140.9 1.2 collective-permute-start.27
  142.2 0.5 collective-permute-done.21
  142.7 2.0 %collective-permute-done.22 = bf16[64,512]{1,0:T(8,128)(2,1)S(1)} collective-permute-done((bf16[64,512]{1,0:T(8,128)(2,1)S(1)}, bf16[64,512]{1,0:T(8,128)(2,1)S(1)}, u32[]{:S(2)}, u32[]{:S(2)}) %collective-permute-start.22) | collective-permute-done | bytes 65568 | tf_op jit(solution)/shard_map/ppermute | solution.py:503
  144.7 0.4 collective-permute-done.23
  145.1 0.7 multiply_bitcast_fusion
  145.8 0.4 collective-permute-done.27
  146.2 0.8 copy.28
  (76 shorter events, 0.9 us)
Async XLA Ops:
  1.0 1.6 %copy-start = (bf16[512,1,16,128]{3,2,1,0:T(8,128)(2,1)S(1)}, bf16[512,1,16,128]{3,2,1,0:T(8,128)(2,1)}, u32[]{:S(2)}) copy-start(bf16[512,1,16,128]{3,2,1,0:T(8,128)(2,1)} %param.9) | copy-start | bytes 6291460
  2.6 0.7 copy-start.6
  3.3 4.0 %copy-start.1 = (bf16[512,1,16,128]{3,2,1,0:T(8,128)(2,1)S(1)}, bf16[512,1,16,128]{3,2,1,0:T(8,128)(2,1)}, u32[]{:S(2)}) copy-start(bf16[512,1,16,128]{3,2,1,0:T(8,128)(2,1)} %param.10) | copy-start | bytes 6291460
  4.2 3.1 %collective-permute-start = (bf16[132,16,128]{2,1,0:T(8,128)(2,1)S(1)}, bf16[132,16,128]{2,1,0:T(8,128)(2,1)S(1)}, u32[]{:S(2)}, u32[]{:S(2)}) collective-permute-start(bf16[132,16,128]{2,1,0:T(8,128)(2,1)S(1)} %get-tuple-element.35), channel_id=1, source_target_pairs={{0,2},{2,0},{4,6},{6,4},{8,10},{10,8},{12,14},{14,12},{16,18},{18,... | collective-permute-start | bytes 1622024 | tf_op jit(solution)/shard_map/ppermute | solution.py:414
  4.7 15.7 %collective-permute-start.2 = (bf16[132,16,128]{2,1,0:T(8,128)(2,1)S(1)}, bf16[132,16,128]{2,1,0:T(8,128)(2,1)S(1)}, u32[]{:S(2)}, u32[]{:S(2)}) collective-permute-start(bf16[132,16,128]{2,1,0:T(8,128)(2,1)S(1)} %get-tuple-element.40), channel_id=1, source_target_pairs={{0,4},{2,6},{4,0},{6,2},{8,12},{10,14},{12,8},{14,10},{16,20},{18,... | collective-permute-start | bytes 1622024 | tf_op jit(solution)/shard_map/ppermute | solution.py:414
  8.7 27.1 %collective-permute-start.1 = (bf16[256,16,128]{2,1,0:T(8,128)(2,1)S(1)}, bf16[256,16,128]{2,1,0:T(8,128)(2,1)S(1)}, u32[]{:S(2)}, u32[]{:S(2)}) collective-permute-start(bf16[256,16,128]{2,1,0:T(8,128)(2,1)S(1)} %get-tuple-element.37), channel_id=1, source_target_pairs={{0,2},{2,0},{4,6},{6,4},{8,10},{10,8},{12,14},{14,12},{16,18},{18,... | collective-permute-start | bytes 3145736 | tf_op jit(solution)/shard_map/ppermute | solution.py:414
  9.0 38.4 %copy-start.2 = (bf16[264,16,128]{2,1,0:T(8,128)(2,1)}, bf16[264,16,128]{2,1,0:T(8,128)(2,1)S(1)}, u32[]{:S(2)}) copy-start(bf16[264,16,128]{2,1,0:T(8,128)(2,1)S(1)} %join.7.refs_0_) | copy-start | bytes 3244036
  9.0 29.4 %copy-start.21 = (s32[512]{0:T(512)S(1)}, s32[512]{0:T(512)}, u32[]{:S(2)}) copy-start(s32[512]{0:T(512)} %param.14) | copy-start | bytes 6148
  9.1 29.4 %copy-start.22 = (s32[512]{0:T(512)S(1)}, s32[512]{0:T(512)}, u32[]{:S(2)}) copy-start(s32[512]{0:T(512)} %param.13) | copy-start | bytes 6148
  9.1 29.4 %copy-start.24 = (f32[16]{0:T(128)S(1)}, f32[16]{0:T(128)}, u32[]{:S(2)}) copy-start(f32[16]{0:T(128)} %param.12) | copy-start | bytes 196
  9.1 30.8 %collective-permute-start.6 = (bf16[264,16,128]{2,1,0:T(8,128)(2,1)S(1)}, bf16[264,16,128]{2,1,0:T(8,128)(2,1)}, u32[]{:S(2)}, u32[]{:S(2)}) collective-permute-start(bf16[264,16,128]{2,1,0:T(8,128)(2,1)S(1)} %join.7.refs_0_), channel_id=1, source_target_pairs={{4,12},{6,14},{12,20},{14,22},{20,28},{22,30},{8,0},{10,2},{16,8},... | collective-permute-start | bytes 3244040 | tf_op jit(solution)/shard_map/ppermute | solution.py:422
  10.5 21.0 %collective-permute-start.3 = (bf16[132,16,128]{2,1,0:T(8,128)(2,1)S(1)}, bf16[132,16,128]{2,1,0:T(8,128)(2,1)S(1)}, u32[]{:S(2)}, u32[]{:S(2)}) collective-permute-start(bf16[132,16,128]{2,1,0:T(8,128)(2,1)S(1)} %get-tuple-element.41), channel_id=1, source_target_pairs={{0,6},{2,4},{4,2},{6,0},{8,14},{10,12},{12,10},{14,8},{16,22},{18,... | collective-permute-start | bytes 1622024 | tf_op jit(solution)/shard_map/ppermute | solution.py:414
  20.4 16.3 %copy-start.11 = (bf16[132,16,128]{2,1,0:T(8,128)(2,1)}, bf16[132,16,128]{2,1,0:T(8,128)(2,1)S(1)}, u32[]{:S(2)}) copy-start(bf16[132,16,128]{2,1,0:T(8,128)(2,1)S(1)} %collective-permute-done.2.refs_1_) | copy-start | bytes 1622020
  20.5 16.4 %collective-permute-start.4 = (bf16[132,16,128]{2,1,0:T(8,128)(2,1)S(1)}, bf16[132,16,128]{2,1,0:T(8,128)(2,1)S(1)}, u32[]{:S(2)}, u32[]{:S(2)}) collective-permute-start(bf16[132,16,128]{2,1,0:T(8,128)(2,1)S(1)} %collective-permute-done.2.refs_1_), channel_id=1, source_target_pairs={{0,8},{2,10},{8,16},{10,18},{16,24},{18,26},{12,4},{14,6},{20,12},... | collective-permute-start | bytes 1622024 | tf_op jit(solution)/shard_map/ppermute | solution.py:423
  31.5 8.4 %copy-start.13 = (bf16[132,16,128]{2,1,0:T(8,128)(2,1)}, bf16[132,16,128]{2,1,0:T(8,128)(2,1)S(1)}, u32[]{:S(2)}) copy-start(bf16[132,16,128]{2,1,0:T(8,128)(2,1)S(1)} %collective-permute-done.3.refs_2_) | copy-start | bytes 1622020
  31.5 15.9 %collective-permute-start.7 = (bf16[132,16,128]{2,1,0:T(8,128)(2,1)S(1)}, bf16[132,16,128]{2,1,0:T(8,128)(2,1)}, u32[]{:S(2)}, u32[]{:S(2)}) collective-permute-start(bf16[132,16,128]{2,1,0:T(8,128)(2,1)S(1)} %collective-permute-done.3.refs_2_), channel_id=1, source_target_pairs={{0,8},{2,10},{8,16},{10,18},{16,24},{18,26},{12,4},{14,6},{20,12},... | collective-permute-start | bytes 1622024 | tf_op jit(solution)/shard_map/ppermute | solution.py:423
  36.8 0.8 copy-start.16
  37.6 20.2 %collective-permute-start.5 = (bf16[192,16,128]{2,1,0:T(8,128)(2,1)}, bf16[192,16,128]{2,1,0:T(8,128)(2,1)}, u32[]{:S(2)}, u32[]{:S(2)}) collective-permute-start(bf16[192,16,128]{2,1,0:T(8,128)(2,1)} %join.6.refs_0_), channel_id=1, source_target_pairs={{0,4},{2,6},{4,0},{6,2},{8,12},{10,14},{12,8},{14,10},{16,20},{18,... | collective-permute-start | bytes 2359304 | tf_op jit(solution)/shard_map/ppermute | solution.py:414
  38.9 8.6 %copy-start.12 = (bf16[132,16,128]{2,1,0:T(8,128)(2,1)S(1)}, bf16[132,16,128]{2,1,0:T(8,128)(2,1)}, u32[]{:S(2)}) copy-start(bf16[132,16,128]{2,1,0:T(8,128)(2,1)} %copy-done.11) | copy-start | bytes 1622020
  38.9 8.6 %copy-start.17 = (bf16[132,16,128]{2,1,0:T(8,128)(2,1)S(1)}, bf16[132,16,128]{2,1,0:T(8,128)(2,1)}, u32[]{:S(2)}) copy-start(bf16[132,16,128]{2,1,0:T(8,128)(2,1)} %copy-done.16) | copy-start | bytes 1622020
  39.9 30.1 %collective-permute-start.11 = (bf16[192,16,128]{2,1,0:T(8,128)(2,1)}, bf16[192,16,128]{2,1,0:T(8,128)(2,1)S(1)}, u32[]{:S(2)}, u32[]{:S(2)}) collective-permute-start(bf16[192,16,128]{2,1,0:T(8,128)(2,1)} %join.6.refs_0_), channel_id=1, source_target_pairs={{4,12},{6,14},{12,20},{14,22},{20,28},{22,30},{8,0},{10,2},{16,8},... | collective-permute-start | bytes 2359304 | tf_op jit(solution)/shard_map/ppermute | solution.py:422
  47.5 1.0 copy-start.14
  48.5 13.8 %copy-start.15 = (bf16[132,16,128]{2,1,0:T(8,128)(2,1)S(1)}, bf16[132,16,128]{2,1,0:T(8,128)(2,1)}, u32[]{:S(2)}) copy-start(bf16[132,16,128]{2,1,0:T(8,128)(2,1)} %copy-done.13) | copy-start | bytes 1622020
  54.0 15.9 %copy-start.18 = (f32[8,16,128]{2,1,0:T(8,128)}, f32[8,16,128]{2,1,0:T(8,128)S(1)}, u32[]{:S(2)}) copy-start(f32[8,16,128]{2,1,0:T(8,128)S(1)} %get-tuple-element.47.refs_8_.refs_6_) | copy-start | bytes 196612
  57.8 19.4 %collective-permute-start.8 = (bf16[192,16,128]{2,1,0:T(8,128)(2,1)}, bf16[192,16,128]{2,1,0:T(8,128)(2,1)}, u32[]{:S(2)}, u32[]{:S(2)}) collective-permute-start(bf16[192,16,128]{2,1,0:T(8,128)(2,1)} %join.5.refs_0_), channel_id=1, source_target_pairs={{0,4},{2,6},{4,0},{6,2},{8,12},{10,14},{12,8},{14,10},{16,20},{18,... | collective-permute-start | bytes 2359304 | tf_op jit(solution)/shard_map/ppermute | solution.py:414
  58.0 19.2 %collective-permute-start.14 = (bf16[192,16,128]{2,1,0:T(8,128)(2,1)}, bf16[192,16,128]{2,1,0:T(8,128)(2,1)S(1)}, u32[]{:S(2)}, u32[]{:S(2)}) collective-permute-start(bf16[192,16,128]{2,1,0:T(8,128)(2,1)} %collective-permute-done.5.refs_1_), channel_id=1, source_target_pairs={{0,8},{2,10},{8,16},{10,18},{16,24},{18,26},{12,4},{14,6},{20,12},... | collective-permute-start | bytes 2359304 | tf_op jit(solution)/shard_map/ppermute | solution.py:423
  60.8 24.8 %collective-permute-start.18 = (bf16[64,8192]{1,0:T(8,128)(2,1)S(1)}, bf16[64,8192]{1,0:T(8,128)(2,1)S(1)}, u32[]{:S(2)}, u32[]{:S(2)}) collective-permute-start(bf16[64,8192]{1,0:T(8,128)(2,1)S(1)} %get-tuple-element.44.refs_4_.refs_2_.refs_0_), channel_id=1, source_target_pairs={{0,1},{1,0},{2,3},{3,2},{4,5},{5,4},{6,7},{7,6},{8,9},{9,8},{10,11... | collective-permute-start | bytes 3145736 | tf_op jit(solution)/shard_map/ppermute | solution.py:417
  62.3 1.2 copy-start.3
  70.0 0.9 copy-start.7
  70.9 23.5 %collective-permute-start.12 = (bf16[192,16,128]{2,1,0:T(8,128)(2,1)}, bf16[192,16,128]{2,1,0:T(8,128)(2,1)}, u32[]{:S(2)}, u32[]{:S(2)}) collective-permute-start(bf16[192,16,128]{2,1,0:T(8,128)(2,1)} %join.5.refs_0_), channel_id=1, source_target_pairs={{4,12},{6,14},{12,20},{14,22},{20,28},{22,30},{8,0},{10,2},{16,8},... | collective-permute-start | bytes 2359304 | tf_op jit(solution)/shard_map/ppermute | solution.py:422
  77.2 0.9 copy-start.9
  78.1 19.6 %collective-permute-start.15 = (bf16[192,16,128]{2,1,0:T(8,128)(2,1)}, bf16[192,16,128]{2,1,0:T(8,128)(2,1)}, u32[]{:S(2)}, u32[]{:S(2)}) collective-permute-start(bf16[192,16,128]{2,1,0:T(8,128)(2,1)} %collective-permute-done.8.refs_1_), channel_id=1, source_target_pairs={{0,8},{2,10},{8,16},{10,18},{16,24},{18,26},{12,4},{14,6},{20,12},... | collective-permute-start | bytes 2359304 | tf_op jit(solution)/shard_map/ppermute | solution.py:423
  83.2 2.5 %copy-start.8 = (bf16[192,16,128]{2,1,0:T(8,128)(2,1)S(1)}, bf16[192,16,128]{2,1,0:T(8,128)(2,1)}, u32[]{:S(2)}) copy-start(bf16[192,16,128]{2,1,0:T(8,128)(2,1)} %copy-done.7) | copy-start | bytes 2359300
  83.2 2.5 %copy-start.10 = (bf16[192,16,128]{2,1,0:T(8,128)(2,1)S(1)}, bf16[192,16,128]{2,1,0:T(8,128)(2,1)}, u32[]{:S(2)}) copy-start(bf16[192,16,128]{2,1,0:T(8,128)(2,1)} %copy-done.9) | copy-start | bytes 2359300
  83.2 2.5 %copy-start.19 = (f32[8,16,128]{2,1,0:T(8,128)S(1)}, f32[8,16,128]{2,1,0:T(8,128)}, u32[]{:S(2)}) copy-start(f32[8,16,128]{2,1,0:T(8,128)} %copy-done.18) | copy-start | bytes 196612
  84.0 12.1 %collective-permute-start.9 = (bf16[128,16,128]{2,1,0:T(8,128)(2,1)}, bf16[128,16,128]{2,1,0:T(8,128)(2,1)}, u32[]{:S(2)}, u32[]{:S(2)}) collective-permute-start(bf16[128,16,128]{2,1,0:T(8,128)(2,1)} %join.4.refs_0_), channel_id=1, source_target_pairs={{0,4},{2,6},{4,0},{6,2},{8,12},{10,14},{12,8},{14,10},{16,20},{18,... | collective-permute-start | bytes 1572872 | tf_op jit(solution)/shard_map/ppermute | solution.py:414
  84.1 28.1 %collective-permute-start.10 = (bf16[64,8192]{1,0:T(8,128)(2,1)}, bf16[64,8192]{1,0:T(8,128)(2,1)S(1)}, u32[]{:S(2)}, u32[]{:S(2)}) collective-permute-start(bf16[64,8192]{1,0:T(8,128)(2,1)} %direct_sweeps.3.refs_5_.refs_3_.refs_1_), channel_id=1, source_target_pairs={{0,1},{1,0},{2,3},{3,2},{4,5},{5,4},{6,7},{7,6},{8,9},{9,8},{10,11... | collective-permute-start | bytes 3145736 | tf_op jit(solution)/shard_map/ppermute | solution.py:417
  94.4 32.3 %collective-permute-start.19 = (bf16[96,8192]{1,0:T(8,128)(2,1)}, bf16[96,8192]{1,0:T(8,128)(2,1)}, u32[]{:S(2)}, u32[]{:S(2)}) collective-permute-start(bf16[96,8192]{1,0:T(8,128)(2,1)} %adjoint_sweeps.4.refs_0_), channel_id=1, source_target_pairs={{0,2},{2,0},{4,6},{6,4},{8,10},{10,8},{12,14},{14,12},{16,18},{18,... | collective-permute-start | bytes 4718600 | tf_op jit(solution)/shard_map/ppermute | solution.py:414
  94.4 17.8 %collective-permute-start.13 = (bf16[128,16,128]{2,1,0:T(8,128)(2,1)}, bf16[128,16,128]{2,1,0:T(8,128)(2,1)}, u32[]{:S(2)}, u32[]{:S(2)}) collective-permute-start(bf16[128,16,128]{2,1,0:T(8,128)(2,1)} %join.4.refs_0_), channel_id=1, source_target_pairs={{4,12},{6,14},{12,20},{14,22},{20,28},{22,30},{8,0},{10,2},{16,8},... | collective-permute-start | bytes 1572872 | tf_op jit(solution)/shard_map/ppermute | solution.py:422
  97.7 15.1 %collective-permute-start.16 = (bf16[128,16,128]{2,1,0:T(8,128)(2,1)}, bf16[128,16,128]{2,1,0:T(8,128)(2,1)}, u32[]{:S(2)}, u32[]{:S(2)}) collective-permute-start(bf16[128,16,128]{2,1,0:T(8,128)(2,1)} %collective-permute-done.9.refs_1_), channel_id=1, source_target_pairs={{0,8},{2,10},{8,16},{10,18},{16,24},{18,26},{12,4},{14,6},{20,12},... | collective-permute-start | bytes 1572872 | tf_op jit(solution)/shard_map/ppermute | solution.py:423
  112.1 14.6 %collective-permute-start.20 = (bf16[96,8192]{1,0:T(8,128)(2,1)}, bf16[96,8192]{1,0:T(8,128)(2,1)}, u32[]{:S(2)}, u32[]{:S(2)}) collective-permute-start(bf16[96,8192]{1,0:T(8,128)(2,1)} %adjoint_sweeps.5.refs_1_), channel_id=1, source_target_pairs={{0,2},{2,0},{4,6},{6,4},{8,10},{10,8},{12,14},{14,12},{16,18},{18,... | collective-permute-start | bytes 4718600 | tf_op jit(solution)/shard_map/ppermute | solution.py:414
  112.9 0.8 copy-start.20
  113.7 6.7 %copy-start.23 = (f32[64]{0:T(128)S(1)}, f32[64]{0:T(128)}, u32[]{:S(2)}) copy-start(f32[64]{0:T(128)} %param.17) | copy-start | bytes 772
  113.7 6.8 %copy-start.5 = (f32[1024,64]{0,1:T(8,128)S(1)}, f32[1024,64]{0,1:T(8,128)}, u32[]{:S(2)}) copy-start(f32[1024,64]{0,1:T(8,128)} %param.16) | copy-start | bytes 786436
  120.4 12.0 %collective-permute-start.17 = (bf16[64,8192]{1,0:T(8,128)(2,1)}, bf16[64,8192]{1,0:T(8,128)(2,1)}, u32[]{:S(2)}, u32[]{:S(2)}) collective-permute-start(bf16[64,8192]{1,0:T(8,128)(2,1)} %adjoint_sweeps.3.refs_0_), channel_id=1, source_target_pairs={{0,2},{2,0},{4,6},{6,4},{8,10},{10,8},{12,14},{14,12},{16,18},{18,... | collective-permute-start | bytes 3145736 | tf_op jit(solution)/shard_map/ppermute | solution.py:414
  120.5 6.1 %copy-start.4 = (f32[1024,64]{0,1:T(8,128)S(1)}, f32[1024,64]{0,1:T(8,128)}, u32[]{:S(2)}) copy-start(f32[1024,64]{0,1:T(8,128)} %param.15) | copy-start | bytes 786436
  122.4 17.0 %collective-permute-start.24 = (bf16[64,1024]{1,0:T(8,128)(2,1)S(1)}, bf16[64,1024]{1,0:T(8,128)(2,1)S(1)}, u32[]{:S(2)}, u32[]{:S(2)}) collective-permute-start(bf16[64,1024]{1,0:T(8,128)(2,1)S(1)} %get-tuple-element.62), channel_id=1, source_target_pairs={{0,2},{2,0},{4,6},{6,4},{8,10},{10,8},{12,14},{14,12},{16,18},{18,... | collective-permute-start | bytes 393224 | tf_op jit(solution)/shard_map/ppermute | solution.py:414
  123.0 17.1 %collective-permute-start.25 = (bf16[64,1024]{1,0:T(8,128)(2,1)S(1)}, bf16[64,1024]{1,0:T(8,128)(2,1)S(1)}, u32[]{:S(2)}, u32[]{:S(2)}) collective-permute-start(bf16[64,1024]{1,0:T(8,128)(2,1)S(1)} %get-tuple-element.63), channel_id=1, source_target_pairs={{0,4},{2,6},{4,0},{6,2},{8,12},{10,14},{12,8},{14,10},{16,20},{18,... | collective-permute-start | bytes 393224 | tf_op jit(solution)/shard_map/ppermute | solution.py:414
  126.6 13.5 %collective-permute-start.26 = (bf16[64,1024]{1,0:T(8,128)(2,1)S(1)}, bf16[64,1024]{1,0:T(8,128)(2,1)S(1)}, u32[]{:S(2)}, u32[]{:S(2)}) collective-permute-start(bf16[64,1024]{1,0:T(8,128)(2,1)S(1)} %get-tuple-element.64), channel_id=1, source_target_pairs={{0,6},{2,4},{4,2},{6,0},{8,14},{10,12},{12,10},{14,8},{16,22},{18,... | collective-permute-start | bytes 393224 | tf_op jit(solution)/shard_map/ppermute | solution.py:414
  135.7 7.0 %collective-permute-start.21 = (bf16[64,512]{1,0:T(8,128)(2,1)S(1)}, bf16[64,512]{1,0:T(8,128)(2,1)S(1)}, u32[]{:S(2)}, u32[]{:S(2)}) collective-permute-start(bf16[64,512]{1,0:T(8,128)(2,1)S(1)} %get-tuple-element.58), channel_id=1, source_target_pairs={{0,8},{2,10},{4,12},{6,14},{8,16},{10,18},{12,20},{14,22},{16,24},... | collective-permute-start | bytes 196616 | tf_op jit(solution)/shard_map/ppermute | solution.py:503
  137.4 7.3 %collective-permute-start.22 = (bf16[64,512]{1,0:T(8,128)(2,1)S(1)}, bf16[64,512]{1,0:T(8,128)(2,1)S(1)}, u32[]{:S(2)}, u32[]{:S(2)}) collective-permute-start(bf16[64,512]{1,0:T(8,128)(2,1)S(1)} %get-tuple-element.59), channel_id=1, source_target_pairs={{0,16},{2,18},{4,20},{6,22},{8,24},{10,26},{12,28},{14,30},{16,0},... | collective-permute-start | bytes 196616 | tf_op jit(solution)/shard_map/ppermute | solution.py:503
  139.4 5.7 %collective-permute-start.23 = (bf16[64,512]{1,0:T(8,128)(2,1)S(1)}, bf16[64,512]{1,0:T(8,128)(2,1)S(1)}, u32[]{:S(2)}, u32[]{:S(2)}) collective-permute-start(bf16[64,512]{1,0:T(8,128)(2,1)S(1)} %get-tuple-element.60), channel_id=1, source_target_pairs={{0,24},{2,26},{4,28},{6,30},{8,0},{10,2},{12,4},{14,6},{16,8},{18,... | collective-permute-start | bytes 196616 | tf_op jit(solution)/shard_map/ppermute | solution.py:503
  140.9 5.3 %collective-permute-start.27 = (bf16[64,1024]{1,0:T(8,128)(2,1)S(1)}, bf16[64,1024]{1,0:T(8,128)(2,1)S(1)}, u32[]{:S(2)}, u32[]{:S(2)}) collective-permute-start(bf16[64,1024]{1,0:T(8,128)(2,1)S(1)} %bitcast.43), channel_id=1, source_target_pairs={{0,1},{1,0},{2,3},{3,2},{4,5},{5,4},{6,7},{7,6},{8,9},{9,8},{10,11... | collective-permute-start | bytes 393224 | tf_op jit(solution)/shard_map/ppermute | solution.py:417

commit v5 on v4

--- a/solution.py
+++ b/solution.py
@@ -163,8 +163,7 @@
             for y in range(width_y):
                 coeff = cond[plane, pl.ds(y, 1), :]
                 diag = level + 6.0 * coeff
-                guess = pltpu.reciprocal(diag, approx=True)
-                recip = guess * (2.0 - diag * guess)
+                recip = pltpu.reciprocal(diag, approx=True)
                 scaled = recip * coeff
                 force = flat[slot, pl.ds(y, step, stride=width_y), :]
                 gain[plane, y] = scaled
@@ -470,6 +469,9 @@
     ]
     moved = [[around(state, step) for state in dir_states] for step in range(1, n_snap)]
     everyone = dir_states + [state for states in moved for state in states]
+    singular = singular_values.reshape(1, mode_count).T
+    left, right = left_factors.T, right_factors.T
+    kept, *sent = direct_part(info, right, singular, everyone, n_snap)
     y_adj, e_adj, l_adj, own_states, far_states = [], [], [], [], []
     for i, pair in enumerate(pairs):
         y_after = [near, far, late_near] if i == 0 else [y_adj[-1], dir_states[0]]
@@ -479,14 +481,11 @@
         l_adj.append(late(after(y_adj[i], l_adj[-1]) if i else y_adj[i]))
         arrived = after(y_adj[i], everyone[blocks]) if i == 1 else y_adj[i]
         if i == 2:
-            arrived = after(y_adj[i], everyone[-1])
+            arrived = after(y_adj[i], kept)
         sources = [pair, arrived, e_adj[i], l_adj[i]]
         own_states.append(sweep(True, place, sources, adj_shift[i], band, cond)[0])
         far_states.append(swap(own_states[i], 1))
 
-    singular = singular_values.reshape(1, mode_count).T
-    left, right = left_factors.T, right_factors.T
-    kept, *sent = direct_part(info, right, singular, everyone, n_snap)
     for mask in range(1, GROUP):
         kept = kept + swap(sent[mask - 1], mask).astype(jnp.float32)
     direct_modes = kept.reshape(mode_count, 1, rows_y, width_z)

time: 148 us -> 144 us (0.973)
  Pallas kernels: 52.4 us -> 50.7 us
    ppermute x3, waiting for transfers between devices: 2.93 us -> 0.66 us  [per_device(): lax.ppermute(sent[step - 1], 'space', pairs).astype(jnp.float32)]
    pallas_call x14, Pallas kernels: 52.4 us -> 50.7 us  [call(): pl.pallas_call(kernel, in_specs=in_specs, out_specs=jax.tree.map(lambda _...]
    ppermute x13, starting transfers between devices: 13.4 us -> 11.7 us  [swap(): return lax.ppermute(array, 'space', [(i, i ^ mask) for i in range(n_space)])]
    ppermute x3, waiting for transfers between devices: 0.44 us -> 2.14 us  [around(): lax.ppermute(array, 'snap', [(i, (i + step) % n_snap) for i in range(n_sn...]
    ppermute x3, starting transfers between devices: 4.38 us -> 6.01 us  [per_device(): lax.ppermute(sent[step - 1], 'space', pairs).astype(jnp.float32)]
  transfers between devices with their start and end apart: 28 -> 28, of which waited for: 12 -> 9; matrix products, arithmetic and copies ran while one was open for 2% -> 2% of each run, Pallas kernels for 35% -> 35%
where the time goes in v5:
time: 144 us; the launch traced here: 143 us
  Pallas kernels  50.7 us (35%)
  starting transfers between devices  48.9 us (34%)
  waiting for transfers between devices  32 us (22%)
  local copies, waits for them, and re-layouts  9.62 us (7%)
    pallas_call x14, Pallas kernels, call(): pl.pallas_call(kernel, in_specs=in_specs, out_specs=jax.tree.map(lambda _...  50.7 us
    ppermute x5, starting transfers between devices, per_device(): lax.ppermute(array, 'space', upper(ups, 0) + upper(downs, 1))  21.4 us
    ppermute x13, waiting for transfers between devices, swap(): return lax.ppermute(array, 'space', [(i, i ^ mask) for i in range(n_space)])  21.3 us
    ppermute x13, starting transfers between devices, swap(): return lax.ppermute(array, 'space', [(i, i ^ mask) for i in range(n_space)])  11.7 us
    unnamed x52, local copies, waits for them, and re-layouts  8.72 us
    ppermute x5, waiting for transfers between devices, per_device(): lax.ppermute(array, 'space', upper(ups, 0) + upper(downs, 1))  7.9 us
    ppermute x3, starting transfers between devices, per_device(): lax.ppermute(sent[step - 1], 'space', pairs).astype(jnp.float32)  6.01 us
    ppermute x4, starting transfers between devices, per_device(): lax.ppermute(array, 'space', upper(ups, 1) + upper(downs, 0))  5.27 us
  transfers between devices with their start and end apart: 28, of which 9 were waited for; matrix products, arithmetic and copies ran while one was open for 2% of the time, Pallas kernels for 35%

profile of v5, /device:TPU:0, one launch (start us, length us, event | category | flops | bytes accessed | tf_op | source)
XLA Modules:
  0.0 143.4 jit_solution(9463177131906371146)
XLA Ops:
  0.9 0.1 stack.62.info.token
  1.0 1.6 %copy-done = bf16[512,1,16,128]{3,2,1,0:T(8,128)(2,1)S(1)} copy-done((bf16[512,1,16,128]{3,2,1,0:T(8,128)(2,1)S(1)}, bf16[512,1,16,128]{3,2,1,0:T(8,128)(2,1)}, u32[]{:S(2)}) %copy-start) | copy-done | bytes 2097176
  2.6 0.7 copy-done.6
  3.3 0.9 pack.2
  4.2 0.5 collective-permute-start
  4.7 2.6 %collective-permute-start.2 = (bf16[132,16,128]{2,1,0:T(8,128)(2,1)S(1)}, bf16[132,16,128]{2,1,0:T(8,128)(2,1)S(1)}, u32[]{:S(2)}, u32[]{:S(2)}) collective-permute-start(bf16[132,16,128]{2,1,0:T(8,128)(2,1)S(1)} %get-tuple-element.40), channel_id=1, source_target_pairs={{0,4},{2,6},{4,0},{6,2},{8,12},{10,14},{12,8},{14,10},{16,20},{18,... | collective-permute-start | bytes 1622024 | tf_op jit(solution)/shard_map/ppermute | solution.py:413
  7.3 1.4 pack.3
  8.7 0.2 collective-permute-start.1
  9.1 1.4 collective-permute-start.6
  10.5 4.7 %collective-permute-start.3 = (bf16[132,16,128]{2,1,0:T(8,128)(2,1)S(1)}, bf16[132,16,128]{2,1,0:T(8,128)(2,1)S(1)}, u32[]{:S(2)}, u32[]{:S(2)}) collective-permute-start(bf16[132,16,128]{2,1,0:T(8,128)(2,1)S(1)} %get-tuple-element.41), channel_id=1, source_target_pairs={{0,6},{2,4},{4,2},{6,0},{8,14},{10,12},{12,10},{14,8},{16,22},{18,... | collective-permute-start | bytes 1622024 | tf_op jit(solution)/shard_map/ppermute | solution.py:413
  15.2 5.2 %collective-permute-done.2.refs_1_ = bf16[132,16,128]{2,1,0:T(8,128)(2,1)S(1)} collective-permute-done((bf16[132,16,128]{2,1,0:T(8,128)(2,1)S(1)}, bf16[132,16,128]{2,1,0:T(8,128)(2,1)S(1)}, u32[]{:S(2)}, u32[]{:S(2)}) %collective-permute-start.2) | collective-permute-done | bytes 540704 | tf_op jit(solution)/shard_map/ppermute | solution.py:413
  20.5 3.9 %collective-permute-start.4 = (bf16[132,16,128]{2,1,0:T(8,128)(2,1)S(1)}, bf16[132,16,128]{2,1,0:T(8,128)(2,1)S(1)}, u32[]{:S(2)}, u32[]{:S(2)}) collective-permute-start(bf16[132,16,128]{2,1,0:T(8,128)(2,1)S(1)} %collective-permute-done.2.refs_1_), channel_id=1, source_target_pairs={{0,8},{2,10},{8,16},{10,18},{16,24},{18,26},{12,4},{14,6},{20,12},... | collective-permute-start | bytes 1622024 | tf_op jit(solution)/shard_map/ppermute | solution.py:422
  24.4 7.1 %collective-permute-done.3.refs_2_ = bf16[132,16,128]{2,1,0:T(8,128)(2,1)S(1)} collective-permute-done((bf16[132,16,128]{2,1,0:T(8,128)(2,1)S(1)}, bf16[132,16,128]{2,1,0:T(8,128)(2,1)S(1)}, u32[]{:S(2)}, u32[]{:S(2)}) %collective-permute-start.3) | collective-permute-done | bytes 540704 | tf_op jit(solution)/shard_map/ppermute | solution.py:413
  31.5 4.3 %collective-permute-start.7 = (bf16[132,16,128]{2,1,0:T(8,128)(2,1)S(1)}, bf16[132,16,128]{2,1,0:T(8,128)(2,1)}, u32[]{:S(2)}, u32[]{:S(2)}) collective-permute-start(bf16[132,16,128]{2,1,0:T(8,128)(2,1)S(1)} %collective-permute-done.3.refs_2_), channel_id=1, source_target_pairs={{0,8},{2,10},{8,16},{10,18},{16,24},{18,26},{12,4},{14,6},{20,12},... | collective-permute-start | bytes 1622024 | tf_op jit(solution)/shard_map/ppermute | solution.py:422
  35.8 0.9 join.6.refs_0_
  36.8 0.8 copy-done.16
  37.6 0.9 collective-permute-start.5
  38.5 0.1 select_reduce_fusion
  38.6 0.1 reshape.31
  38.7 0.1 broadcast_in_dim.28
  38.8 0.1 stack.71.place
  38.9 1.0 join.5.refs_0_
  39.9 1.3 collective-permute-start.12
  41.2 6.2 %collective-permute-done.7.refs_5_ = bf16[132,16,128]{2,1,0:T(8,128)(2,1)} collective-permute-done((bf16[132,16,128]{2,1,0:T(8,128)(2,1)S(1)}, bf16[132,16,128]{2,1,0:T(8,128)(2,1)}, u32[]{:S(2)}, u32[]{:S(2)}) %collective-permute-start.7) | collective-permute-done | bytes 540704 | tf_op jit(solution)/shard_map/ppermute | solution.py:422
  47.5 1.0 copy-done.14
  48.6 5.8 %direct_sweeps.2 = (bf16[64,8192]{1,0:T(8,128)(2,1)S(1)}, f32[8,16,128]{2,1,0:T(8,128)S(1)}) custom-call(s32[8]{0:T(128)S(1)} %stack.71.place, bf16[264,16,128]{2,1,0:T(8,128)(2,1)S(1)} %join.7.refs_0_, bf16[132,16,128]{2,1,0:T(8,128)(2,1)S(1)} %copy-done.12, bf16[132,16,128]{2,1,0:T(8,128)(2,1)S(1)} %copy-done.14, ...), custom_call_target="tpu_custom_call" | custom-call | flops 3407872000 | bytes 1024 | tf_op jit(solution)/shard_map/direct_sweeps/pallas_call | solution.py:25
  54.4 3.4 %collective-permute-done.5.refs_1_ = bf16[192,16,128]{2,1,0:T(8,128)(2,1)} collective-permute-done((bf16[192,16,128]{2,1,0:T(8,128)(2,1)}, bf16[192,16,128]{2,1,0:T(8,128)(2,1)}, u32[]{:S(2)}, u32[]{:S(2)}) %collective-permute-start.5) | collective-permute-done | bytes 786464 | tf_op jit(solution)/shard_map/ppermute | solution.py:413
  57.8 0.2 collective-permute-start.8
  58.0 2.7 %collective-permute-start.15 = (bf16[192,16,128]{2,1,0:T(8,128)(2,1)}, bf16[192,16,128]{2,1,0:T(8,128)(2,1)S(1)}, u32[]{:S(2)}, u32[]{:S(2)}) collective-permute-start(bf16[192,16,128]{2,1,0:T(8,128)(2,1)} %collective-permute-done.5.refs_1_), channel_id=1, source_target_pairs={{0,8},{2,10},{8,16},{10,18},{16,24},{18,26},{12,4},{14,6},{20,12},... | collective-permute-start | bytes 2359304 | tf_op jit(solution)/shard_map/ppermute | solution.py:422
  60.8 1.6 %collective-permute-start.10 = (bf16[64,8192]{1,0:T(8,128)(2,1)S(1)}, bf16[64,8192]{1,0:T(8,128)(2,1)S(1)}, u32[]{:S(2)}, u32[]{:S(2)}) collective-permute-start(bf16[64,8192]{1,0:T(8,128)(2,1)S(1)} %get-tuple-element.44.refs_0_.refs_4_.refs_2_), channel_id=1, source_target_pairs={{0,1},{1,0},{2,3},{3,2},{4,5},{5,4},{6,7},{7,6},{8,9},{9,8},{10,11... | collective-permute-start | bytes 3145736 | tf_op jit(solution)/shard_map/ppermute | solution.py:416
  62.4 1.2 copy-done.3
  63.6 6.7 %direct_sweeps.3.refs_1_.refs_5_.refs_3_ = bf16[64,8192]{1,0:T(8,128)(2,1)} custom-call(s32[8]{0:T(128)S(1)} %stack.71.place, bf16[264,16,128]{2,1,0:T(8,128)(2,1)S(1)} %copy-done.3, bf16[132,16,128]{2,1,0:T(8,128)(2,1)S(1)} %copy-done.12, bf16[132,16,128]{2,1,0:T(8,128)(2,1)S(1)} %copy-done.15, bf16[264,16,128]{2,1,0:T(8,128)(2,1)} %collective-permute-done.6.refs_3_, ...), custom_call_target="tpu_custom_call" | custom-call | flops 3407872000 | bytes 1024 | tf_op jit(solution)/shard_map/direct_sweeps/pallas_call | solution.py:25
  70.3 0.9 copy-done.7
  71.2 1.3 collective-permute-start.13
  72.5 4.7 %collective-permute-done.8.refs_1_ = bf16[192,16,128]{2,1,0:T(8,128)(2,1)} collective-permute-done((bf16[192,16,128]{2,1,0:T(8,128)(2,1)}, bf16[192,16,128]{2,1,0:T(8,128)(2,1)}, u32[]{:S(2)}, u32[]{:S(2)}) %collective-permute-start.8) | collective-permute-done | bytes 786464 | tf_op jit(solution)/shard_map/ppermute | solution.py:413
  77.3 0.9 copy-done.9
  78.2 5.2 %collective-permute-start.16 = (bf16[192,16,128]{2,1,0:T(8,128)(2,1)}, bf16[192,16,128]{2,1,0:T(8,128)(2,1)}, u32[]{:S(2)}, u32[]{:S(2)}) collective-permute-start(bf16[192,16,128]{2,1,0:T(8,128)(2,1)} %collective-permute-done.8.refs_1_), channel_id=1, source_target_pairs={{0,8},{2,10},{8,16},{10,18},{16,24},{18,26},{12,4},{14,6},{20,12},... | collective-permute-start | bytes 2359304 | tf_op jit(solution)/shard_map/ppermute | solution.py:422
  83.4 0.8 join.4.refs_0_
  84.2 0.1 fusion
  84.3 1.5 %collective-permute-start.11 = (bf16[64,8192]{1,0:T(8,128)(2,1)}, bf16[64,8192]{1,0:T(8,128)(2,1)S(1)}, u32[]{:S(2)}, u32[]{:S(2)}) collective-permute-start(bf16[64,8192]{1,0:T(8,128)(2,1)} %direct_sweeps.3.refs_1_.refs_5_.refs_3_), channel_id=1, source_target_pairs={{0,1},{1,0},{2,3},{3,2},{4,5},{5,4},{6,7},{7,6},{8,9},{9,8},{10,11... | collective-permute-start | bytes 3145736 | tf_op jit(solution)/shard_map/ppermute | solution.py:416
  85.9 8.4 %adjoint_sweeps.4.refs_0_ = bf16[96,8192]{1,0:T(8,128)(2,1)} custom-call(s32[8]{0:T(128)S(1)} %stack.71.place, bf16[192,16,128]{2,1,0:T(8,128)(2,1)} %join.6.refs_0_, bf16[192,16,128]{2,1,0:T(8,128)(2,1)} %collective-permute-done.5.refs_1_, bf16[192,16,128]{2,1,0:T(8,128)(2,1)S(1)} %copy-done.8, bf16[192,16,128]{2,1,0:T(8,128)(2,1)S(1)} %copy-done.10, ...), custom_call_target="tpu_custom_call" | custom-call | flops 5111808000 | bytes 1024 | tf_op jit(solution)/shard_map/adjoint_sweeps/pallas_call | solution.py:25
  94.3 1.3 collective-permute-start.14
  95.6 0.8 collective-permute-done.9.refs_1_
  96.4 1.6 %collective-permute-done.16.refs_3_ = bf16[192,16,128]{2,1,0:T(8,128)(2,1)} collective-permute-done((bf16[192,16,128]{2,1,0:T(8,128)(2,1)}, bf16[192,16,128]{2,1,0:T(8,128)(2,1)}, u32[]{:S(2)}, u32[]{:S(2)}) %collective-permute-start.16) | collective-permute-done | bytes 786464 | tf_op jit(solution)/shard_map/ppermute | solution.py:422
  98.0 5.2 %collective-permute-start.17 = (bf16[128,16,128]{2,1,0:T(8,128)(2,1)}, bf16[128,16,128]{2,1,0:T(8,128)(2,1)}, u32[]{:S(2)}, u32[]{:S(2)}) collective-permute-start(bf16[128,16,128]{2,1,0:T(8,128)(2,1)} %collective-permute-done.9.refs_1_), channel_id=1, source_target_pairs={{0,8},{2,10},{8,16},{10,18},{16,24},{18,26},{12,4},{14,6},{20,12},... | collective-permute-start | bytes 1572872 | tf_op jit(solution)/shard_map/ppermute | solution.py:422
  103.3 8.9 %adjoint_sweeps.5.refs_1_ = bf16[96,8192]{1,0:T(8,128)(2,1)} custom-call(s32[8]{0:T(128)S(1)} %stack.71.place, bf16[192,16,128]{2,1,0:T(8,128)(2,1)} %join.5.refs_0_, bf16[192,16,128]{2,1,0:T(8,128)(2,1)} %collective-permute-done.8.refs_1_, bf16[192,16,128]{2,1,0:T(8,128)(2,1)} %collective-permute-done.13.refs_2_, ...), custom_call_target="tpu_custom_call" | custom-call | flops 5111808000 | bytes 1024 | tf_op jit(solution)/shard_map/adjoint_sweeps/pallas_call | solution.py:25
  112.2 0.1 dynamic_slice.14
  112.3 0.1 copy.24.singular
  112.4 1.9 %direct_modes_part.1 = (f32[64,1024]{1,0:T(8,128)S(1)}, bf16[64,1024]{1,0:T(8,128)(2,1)S(1)}, bf16[64,1024]{1,0:T(8,128)(2,1)S(1)}, bf16[64,1024]{1,0:T(8,128)(2,1)S(1)}) custom-call(s32[8]{0:T(128)S(1)} %stack.62.info.token, f32[64,1024]{1,0:T(8,128)S(1)} %bitcast.42, f32[64,1]{1,0:T(8,128)S(1)} %copy.24.singular, ...), custom_call_target="tpu_custom_call" | custom-call | flops 524288 | bytes 1024 | tf_op jit(solution)/shard_map/direct_modes_part/pallas_call | solution.py:25
  114.3 5.5 %adjoint_sweeps.3.refs_0_ = bf16[64,8192]{1,0:T(8,128)(2,1)S(1)} custom-call(s32[8]{0:T(128)S(1)} %stack.71.place, bf16[128,16,128]{2,1,0:T(8,128)(2,1)} %join.4.refs_0_, bf16[128,16,128]{2,1,0:T(8,128)(2,1)} %collective-permute-done.9.refs_1_, bf16[128,16,128]{2,1,0:T(8,128)(2,1)} %collective-permute-done.14.refs_2_, ...), custom_call_target="tpu_custom_call" | custom-call | flops 3407872000 | bytes 1024 | tf_op jit(solution)/shard_map/adjoint_sweeps/pallas_call | solution.py:25
  119.8 0.6 collective-permute-start.18
  120.4 0.1 collective-permute-start.24
  120.4 1.9 %collective-permute-start.25 = (bf16[64,1024]{1,0:T(8,128)(2,1)S(1)}, bf16[64,1024]{1,0:T(8,128)(2,1)S(1)}, u32[]{:S(2)}, u32[]{:S(2)}) collective-permute-start(bf16[64,1024]{1,0:T(8,128)(2,1)S(1)} %get-tuple-element.63), channel_id=1, source_target_pairs={{0,4},{2,6},{4,0},{6,2},{8,12},{10,14},{12,8},{14,10},{16,20},{18,... | collective-permute-start | bytes 393224 | tf_op jit(solution)/shard_map/ppermute | solution.py:413
  122.4 5.7 %gram_part.2 = (f32[4,64,384]{2,1,0:T(8,128)S(1)}, f32[64,2048]{1,0:T(8,128)S(1)}) custom-call(s32[8]{0:T(128)S(1)} %stack.62.info.token, f32[64,1024]{1,0:T(8,128)S(1)} %bitcast.40, f32[64,1]{1,0:T(8,128)S(1)} %copy.24.singular, bf16[96,8192]{1,0:T(8,128)(2,1)} %adjoint_sweeps.4.refs_0_, bf16[96,8192]{1,0:T(8,128)(2,1)} %adjoint_sweeps.5.refs_1_, ...), custom_call_target="tpu_custom_call" | custom-call | flops 3145728 | bytes 1024 | tf_op jit(solution)/shard_map/gram_part/pallas_call | solution.py:25
  128.1 2.7 %gram_part.3 = (f32[64,512]{1,0:T(8,128)S(1)}, bf16[64,512]{1,0:T(8,128)(2,1)S(1)}, bf16[64,512]{1,0:T(8,128)(2,1)S(1)}, bf16[64,512]{1,0:T(8,128)(2,1)S(1)}, f3...) custom-call(s32[8]{0:T(128)S(1)} %stack.62.info.token, f32[64,1024]{1,0:T(8,128)S(1)} %bitcast.41, ...), custom_call_target="tpu_custom_call" | custom-call | flops 1048576 | bytes 1024 | tf_op jit(solution)/shard_map/gram_part/pallas_call | solution.py:25
  130.8 1.7 %collective-permute-start.21 = (bf16[64,512]{1,0:T(8,128)(2,1)S(1)}, bf16[64,512]{1,0:T(8,128)(2,1)S(1)}, u32[]{:S(2)}, u32[]{:S(2)}) collective-permute-start(bf16[64,512]{1,0:T(8,128)(2,1)S(1)} %get-tuple-element.59), channel_id=1, source_target_pairs={{0,8},{2,10},{4,12},{6,14},{8,16},{10,18},{12,20},{14,22},{16,24},... | collective-permute-start | bytes 196616 | tf_op jit(solution)/shard_map/ppermute | solution.py:502
  132.5 2.0 %collective-permute-start.22 = (bf16[64,512]{1,0:T(8,128)(2,1)S(1)}, bf16[64,512]{1,0:T(8,128)(2,1)S(1)}, u32[]{:S(2)}, u32[]{:S(2)}) collective-permute-start(bf16[64,512]{1,0:T(8,128)(2,1)S(1)} %get-tuple-element.60), channel_id=1, source_target_pairs={{0,16},{2,18},{4,20},{6,22},{8,24},{10,26},{12,28},{14,30},{16,0},... | collective-permute-start | bytes 196616 | tf_op jit(solution)/shard_map/ppermute | solution.py:502
  134.5 2.3 %collective-permute-start.23 = (bf16[64,512]{1,0:T(8,128)(2,1)S(1)}, bf16[64,512]{1,0:T(8,128)(2,1)S(1)}, u32[]{:S(2)}, u32[]{:S(2)}) collective-permute-start(bf16[64,512]{1,0:T(8,128)(2,1)S(1)} %get-tuple-element.61), channel_id=1, source_target_pairs={{0,24},{2,26},{4,28},{6,30},{8,0},{10,2},{12,4},{14,6},{16,8},{18,... | collective-permute-start | bytes 196616 | tf_op jit(solution)/shard_map/ppermute | solution.py:502
  136.9 0.8 copy.27
  137.6 1.5 %collective-permute-start.27 = (bf16[64,1024]{1,0:T(8,128)(2,1)S(1)}, bf16[64,1024]{1,0:T(8,128)(2,1)S(1)}, u32[]{:S(2)}, u32[]{:S(2)}) collective-permute-start(bf16[64,1024]{1,0:T(8,128)(2,1)S(1)} %bitcast.43), channel_id=1, source_target_pairs={{0,1},{1,0},{2,3},{3,2},{4,5},{5,4},{6,7},{7,6},{8,9},{9,8},{10,11... | collective-permute-start | bytes 393224 | tf_op jit(solution)/shard_map/ppermute | solution.py:416
  139.1 0.7 collective-permute-done.22
  139.8 0.7 multiply_bitcast_fusion
  140.5 2.1 %collective-permute-done.27 = bf16[64,1024]{1,0:T(8,128)(2,1)S(1)} collective-permute-done((bf16[64,1024]{1,0:T(8,128)(2,1)S(1)}, bf16[64,1024]{1,0:T(8,128)(2,1)S(1)}, u32[]{:S(2)}, u32[]{:S(2)}) %collective-permute-start.27) | collective-permute-done | bytes 131104 | tf_op jit(solution)/shard_map/ppermute | solution.py:416
  142.6 0.8 copy.28
  (76 shorter events, 0.7 us)
Async XLA Ops:
  1.0 1.6 %copy-start = (bf16[512,1,16,128]{3,2,1,0:T(8,128)(2,1)S(1)}, bf16[512,1,16,128]{3,2,1,0:T(8,128)(2,1)}, u32[]{:S(2)}) copy-start(bf16[512,1,16,128]{3,2,1,0:T(8,128)(2,1)} %param.9) | copy-start | bytes 6291460
  2.6 0.7 copy-start.6
  3.3 4.0 %copy-start.1 = (bf16[512,1,16,128]{3,2,1,0:T(8,128)(2,1)S(1)}, bf16[512,1,16,128]{3,2,1,0:T(8,128)(2,1)}, u32[]{:S(2)}) copy-start(bf16[512,1,16,128]{3,2,1,0:T(8,128)(2,1)} %param.10) | copy-start | bytes 6291460
  4.2 3.1 %collective-permute-start = (bf16[132,16,128]{2,1,0:T(8,128)(2,1)S(1)}, bf16[132,16,128]{2,1,0:T(8,128)(2,1)S(1)}, u32[]{:S(2)}, u32[]{:S(2)}) collective-permute-start(bf16[132,16,128]{2,1,0:T(8,128)(2,1)S(1)} %get-tuple-element.35), channel_id=1, source_target_pairs={{0,2},{2,0},{4,6},{6,4},{8,10},{10,8},{12,14},{14,12},{16,18},{18,... | collective-permute-start | bytes 1622024 | tf_op jit(solution)/shard_map/ppermute | solution.py:413
  4.7 15.7 %collective-permute-start.2 = (bf16[132,16,128]{2,1,0:T(8,128)(2,1)S(1)}, bf16[132,16,128]{2,1,0:T(8,128)(2,1)S(1)}, u32[]{:S(2)}, u32[]{:S(2)}) collective-permute-start(bf16[132,16,128]{2,1,0:T(8,128)(2,1)S(1)} %get-tuple-element.40), channel_id=1, source_target_pairs={{0,4},{2,6},{4,0},{6,2},{8,12},{10,14},{12,8},{14,10},{16,20},{18,... | collective-permute-start | bytes 1622024 | tf_op jit(solution)/shard_map/ppermute | solution.py:413
  8.7 27.1 %collective-permute-start.1 = (bf16[256,16,128]{2,1,0:T(8,128)(2,1)S(1)}, bf16[256,16,128]{2,1,0:T(8,128)(2,1)S(1)}, u32[]{:S(2)}, u32[]{:S(2)}) collective-permute-start(bf16[256,16,128]{2,1,0:T(8,128)(2,1)S(1)} %get-tuple-element.37), channel_id=1, source_target_pairs={{0,2},{2,0},{4,6},{6,4},{8,10},{10,8},{12,14},{14,12},{16,18},{18,... | collective-permute-start | bytes 3145736 | tf_op jit(solution)/shard_map/ppermute | solution.py:413
  9.0 38.4 %copy-start.2 = (bf16[264,16,128]{2,1,0:T(8,128)(2,1)}, bf16[264,16,128]{2,1,0:T(8,128)(2,1)S(1)}, u32[]{:S(2)}) copy-start(bf16[264,16,128]{2,1,0:T(8,128)(2,1)S(1)} %join.7.refs_0_) | copy-start | bytes 3244036
  9.0 29.4 %copy-start.21 = (s32[512]{0:T(512)S(1)}, s32[512]{0:T(512)}, u32[]{:S(2)}) copy-start(s32[512]{0:T(512)} %param.14) | copy-start | bytes 6148
  9.1 29.4 %copy-start.22 = (s32[512]{0:T(512)S(1)}, s32[512]{0:T(512)}, u32[]{:S(2)}) copy-start(s32[512]{0:T(512)} %param.13) | copy-start | bytes 6148
  9.1 29.4 %copy-start.24 = (f32[16]{0:T(128)S(1)}, f32[16]{0:T(128)}, u32[]{:S(2)}) copy-start(f32[16]{0:T(128)} %param.12) | copy-start | bytes 196
  9.1 30.8 %collective-permute-start.6 = (bf16[264,16,128]{2,1,0:T(8,128)(2,1)S(1)}, bf16[264,16,128]{2,1,0:T(8,128)(2,1)}, u32[]{:S(2)}, u32[]{:S(2)}) collective-permute-start(bf16[264,16,128]{2,1,0:T(8,128)(2,1)S(1)} %join.7.refs_0_), channel_id=1, source_target_pairs={{4,12},{6,14},{12,20},{14,22},{20,28},{22,30},{8,0},{10,2},{16,8},... | collective-permute-start | bytes 3244040 | tf_op jit(solution)/shard_map/ppermute | solution.py:421
  10.5 21.0 %collective-permute-start.3 = (bf16[132,16,128]{2,1,0:T(8,128)(2,1)S(1)}, bf16[132,16,128]{2,1,0:T(8,128)(2,1)S(1)}, u32[]{:S(2)}, u32[]{:S(2)}) collective-permute-start(bf16[132,16,128]{2,1,0:T(8,128)(2,1)S(1)} %get-tuple-element.41), channel_id=1, source_target_pairs={{0,6},{2,4},{4,2},{6,0},{8,14},{10,12},{12,10},{14,8},{16,22},{18,... | collective-permute-start | bytes 1622024 | tf_op jit(solution)/shard_map/ppermute | solution.py:413
  20.4 16.3 %copy-start.11 = (bf16[132,16,128]{2,1,0:T(8,128)(2,1)}, bf16[132,16,128]{2,1,0:T(8,128)(2,1)S(1)}, u32[]{:S(2)}) copy-start(bf16[132,16,128]{2,1,0:T(8,128)(2,1)S(1)} %collective-permute-done.2.refs_1_) | copy-start | bytes 1622020
  20.5 16.4 %collective-permute-start.4 = (bf16[132,16,128]{2,1,0:T(8,128)(2,1)S(1)}, bf16[132,16,128]{2,1,0:T(8,128)(2,1)S(1)}, u32[]{:S(2)}, u32[]{:S(2)}) collective-permute-start(bf16[132,16,128]{2,1,0:T(8,128)(2,1)S(1)} %collective-permute-done.2.refs_1_), channel_id=1, source_target_pairs={{0,8},{2,10},{8,16},{10,18},{16,24},{18,26},{12,4},{14,6},{20,12},... | collective-permute-start | bytes 1622024 | tf_op jit(solution)/shard_map/ppermute | solution.py:422
  31.5 8.4 %copy-start.13 = (bf16[132,16,128]{2,1,0:T(8,128)(2,1)}, bf16[132,16,128]{2,1,0:T(8,128)(2,1)S(1)}, u32[]{:S(2)}) copy-start(bf16[132,16,128]{2,1,0:T(8,128)(2,1)S(1)} %collective-permute-done.3.refs_2_) | copy-start | bytes 1622020
  31.5 15.9 %collective-permute-start.7 = (bf16[132,16,128]{2,1,0:T(8,128)(2,1)S(1)}, bf16[132,16,128]{2,1,0:T(8,128)(2,1)}, u32[]{:S(2)}, u32[]{:S(2)}) collective-permute-start(bf16[132,16,128]{2,1,0:T(8,128)(2,1)S(1)} %collective-permute-done.3.refs_2_), channel_id=1, source_target_pairs={{0,8},{2,10},{8,16},{10,18},{16,24},{18,26},{12,4},{14,6},{20,12},... | collective-permute-start | bytes 1622024 | tf_op jit(solution)/shard_map/ppermute | solution.py:422
  36.8 0.8 copy-start.16
  37.6 20.2 %collective-permute-start.5 = (bf16[192,16,128]{2,1,0:T(8,128)(2,1)}, bf16[192,16,128]{2,1,0:T(8,128)(2,1)}, u32[]{:S(2)}, u32[]{:S(2)}) collective-permute-start(bf16[192,16,128]{2,1,0:T(8,128)(2,1)} %join.6.refs_0_), channel_id=1, source_target_pairs={{0,4},{2,6},{4,0},{6,2},{8,12},{10,14},{12,8},{14,10},{16,20},{18,... | collective-permute-start | bytes 2359304 | tf_op jit(solution)/shard_map/ppermute | solution.py:413
  38.9 8.6 %copy-start.12 = (bf16[132,16,128]{2,1,0:T(8,128)(2,1)S(1)}, bf16[132,16,128]{2,1,0:T(8,128)(2,1)}, u32[]{:S(2)}) copy-start(bf16[132,16,128]{2,1,0:T(8,128)(2,1)} %copy-done.11) | copy-start | bytes 1622020
  38.9 8.6 %copy-start.17 = (bf16[132,16,128]{2,1,0:T(8,128)(2,1)S(1)}, bf16[132,16,128]{2,1,0:T(8,128)(2,1)}, u32[]{:S(2)}) copy-start(bf16[132,16,128]{2,1,0:T(8,128)(2,1)} %copy-done.16) | copy-start | bytes 1622020
  39.9 30.4 %collective-permute-start.12 = (bf16[192,16,128]{2,1,0:T(8,128)(2,1)}, bf16[192,16,128]{2,1,0:T(8,128)(2,1)S(1)}, u32[]{:S(2)}, u32[]{:S(2)}) collective-permute-start(bf16[192,16,128]{2,1,0:T(8,128)(2,1)} %join.6.refs_0_), channel_id=1, source_target_pairs={{4,12},{6,14},{12,20},{14,22},{20,28},{22,30},{8,0},{10,2},{16,8},... | collective-permute-start | bytes 2359304 | tf_op jit(solution)/shard_map/ppermute | solution.py:421
  47.5 1.0 copy-start.14
  48.5 13.8 %copy-start.15 = (bf16[132,16,128]{2,1,0:T(8,128)(2,1)S(1)}, bf16[132,16,128]{2,1,0:T(8,128)(2,1)}, u32[]{:S(2)}) copy-start(bf16[132,16,128]{2,1,0:T(8,128)(2,1)} %copy-done.13) | copy-start | bytes 1622020
  54.4 15.9 %copy-start.18 = (f32[8,16,128]{2,1,0:T(8,128)}, f32[8,16,128]{2,1,0:T(8,128)S(1)}, u32[]{:S(2)}) copy-start(f32[8,16,128]{2,1,0:T(8,128)S(1)} %get-tuple-element.47.refs_8_.refs_6_) | copy-start | bytes 196612
  57.8 19.4 %collective-permute-start.8 = (bf16[192,16,128]{2,1,0:T(8,128)(2,1)}, bf16[192,16,128]{2,1,0:T(8,128)(2,1)}, u32[]{:S(2)}, u32[]{:S(2)}) collective-permute-start(bf16[192,16,128]{2,1,0:T(8,128)(2,1)} %join.5.refs_0_), channel_id=1, source_target_pairs={{0,4},{2,6},{4,0},{6,2},{8,12},{10,14},{12,8},{14,10},{16,20},{18,... | collective-permute-start | bytes 2359304 | tf_op jit(solution)/shard_map/ppermute | solution.py:413
  58.0 19.2 %collective-permute-start.15 = (bf16[192,16,128]{2,1,0:T(8,128)(2,1)}, bf16[192,16,128]{2,1,0:T(8,128)(2,1)S(1)}, u32[]{:S(2)}, u32[]{:S(2)}) collective-permute-start(bf16[192,16,128]{2,1,0:T(8,128)(2,1)} %collective-permute-done.5.refs_1_), channel_id=1, source_target_pairs={{0,8},{2,10},{8,16},{10,18},{16,24},{18,26},{12,4},{14,6},{20,12},... | collective-permute-start | bytes 2359304 | tf_op jit(solution)/shard_map/ppermute | solution.py:422
  60.8 25.0 %collective-permute-start.10 = (bf16[64,8192]{1,0:T(8,128)(2,1)S(1)}, bf16[64,8192]{1,0:T(8,128)(2,1)S(1)}, u32[]{:S(2)}, u32[]{:S(2)}) collective-permute-start(bf16[64,8192]{1,0:T(8,128)(2,1)S(1)} %get-tuple-element.44.refs_0_.refs_4_.refs_2_), channel_id=1, source_target_pairs={{0,1},{1,0},{2,3},{3,2},{4,5},{5,4},{6,7},{7,6},{8,9},{9,8},{10,11... | collective-permute-start | bytes 3145736 | tf_op jit(solution)/shard_map/ppermute | solution.py:416
  62.3 1.2 copy-start.3
  70.3 0.9 copy-start.7
  71.2 23.2 %collective-permute-start.13 = (bf16[192,16,128]{2,1,0:T(8,128)(2,1)}, bf16[192,16,128]{2,1,0:T(8,128)(2,1)}, u32[]{:S(2)}, u32[]{:S(2)}) collective-permute-start(bf16[192,16,128]{2,1,0:T(8,128)(2,1)} %join.5.refs_0_), channel_id=1, source_target_pairs={{4,12},{6,14},{12,20},{14,22},{20,28},{22,30},{8,0},{10,2},{16,8},... | collective-permute-start | bytes 2359304 | tf_op jit(solution)/shard_map/ppermute | solution.py:421
  77.3 0.9 copy-start.9
  78.2 19.9 %collective-permute-start.16 = (bf16[192,16,128]{2,1,0:T(8,128)(2,1)}, bf16[192,16,128]{2,1,0:T(8,128)(2,1)}, u32[]{:S(2)}, u32[]{:S(2)}) collective-permute-start(bf16[192,16,128]{2,1,0:T(8,128)(2,1)} %collective-permute-done.8.refs_1_), channel_id=1, source_target_pairs={{0,8},{2,10},{8,16},{10,18},{16,24},{18,26},{12,4},{14,6},{20,12},... | collective-permute-start | bytes 2359304 | tf_op jit(solution)/shard_map/ppermute | solution.py:422
  83.4 2.5 %copy-start.8 = (bf16[192,16,128]{2,1,0:T(8,128)(2,1)S(1)}, bf16[192,16,128]{2,1,0:T(8,128)(2,1)}, u32[]{:S(2)}) copy-start(bf16[192,16,128]{2,1,0:T(8,128)(2,1)} %copy-done.7) | copy-start | bytes 2359300
  83.4 2.5 %copy-start.10 = (bf16[192,16,128]{2,1,0:T(8,128)(2,1)S(1)}, bf16[192,16,128]{2,1,0:T(8,128)(2,1)}, u32[]{:S(2)}) copy-start(bf16[192,16,128]{2,1,0:T(8,128)(2,1)} %copy-done.9) | copy-start | bytes 2359300
  83.4 2.5 %copy-start.19 = (f32[8,16,128]{2,1,0:T(8,128)S(1)}, f32[8,16,128]{2,1,0:T(8,128)}, u32[]{:S(2)}) copy-start(f32[8,16,128]{2,1,0:T(8,128)} %copy-done.18) | copy-start | bytes 196612
  84.2 12.2 %collective-permute-start.9 = (bf16[128,16,128]{2,1,0:T(8,128)(2,1)}, bf16[128,16,128]{2,1,0:T(8,128)(2,1)}, u32[]{:S(2)}, u32[]{:S(2)}) collective-permute-start(bf16[128,16,128]{2,1,0:T(8,128)(2,1)} %join.4.refs_0_), channel_id=1, source_target_pairs={{0,4},{2,6},{4,0},{6,2},{8,12},{10,14},{12,8},{14,10},{16,20},{18,... | collective-permute-start | bytes 1572872 | tf_op jit(solution)/shard_map/ppermute | solution.py:413
  84.3 28.1 %collective-permute-start.11 = (bf16[64,8192]{1,0:T(8,128)(2,1)}, bf16[64,8192]{1,0:T(8,128)(2,1)S(1)}, u32[]{:S(2)}, u32[]{:S(2)}) collective-permute-start(bf16[64,8192]{1,0:T(8,128)(2,1)} %direct_sweeps.3.refs_1_.refs_5_.refs_3_), channel_id=1, source_target_pairs={{0,1},{1,0},{2,3},{3,2},{4,5},{5,4},{6,7},{7,6},{8,9},{9,8},{10,11... | collective-permute-start | bytes 3145736 | tf_op jit(solution)/shard_map/ppermute | solution.py:416
  94.3 28.0 %collective-permute-start.19 = (bf16[96,8192]{1,0:T(8,128)(2,1)}, bf16[96,8192]{1,0:T(8,128)(2,1)}, u32[]{:S(2)}, u32[]{:S(2)}) collective-permute-start(bf16[96,8192]{1,0:T(8,128)(2,1)} %adjoint_sweeps.4.refs_0_), channel_id=1, source_target_pairs={{0,2},{2,0},{4,6},{6,4},{8,10},{10,8},{12,14},{14,12},{16,18},{18,... | collective-permute-start | bytes 4718600 | tf_op jit(solution)/shard_map/ppermute | solution.py:413
  94.3 19.9 %collective-permute-start.14 = (bf16[128,16,128]{2,1,0:T(8,128)(2,1)}, bf16[128,16,128]{2,1,0:T(8,128)(2,1)}, u32[]{:S(2)}, u32[]{:S(2)}) collective-permute-start(bf16[128,16,128]{2,1,0:T(8,128)(2,1)} %join.4.refs_0_), channel_id=1, source_target_pairs={{4,12},{6,14},{12,20},{14,22},{20,28},{22,30},{8,0},{10,2},{16,8},... | collective-permute-start | bytes 1572872 | tf_op jit(solution)/shard_map/ppermute | solution.py:421
  98.0 16.2 %collective-permute-start.17 = (bf16[128,16,128]{2,1,0:T(8,128)(2,1)}, bf16[128,16,128]{2,1,0:T(8,128)(2,1)}, u32[]{:S(2)}, u32[]{:S(2)}) collective-permute-start(bf16[128,16,128]{2,1,0:T(8,128)(2,1)} %collective-permute-done.9.refs_1_), channel_id=1, source_target_pairs={{0,8},{2,10},{8,16},{10,18},{16,24},{18,26},{12,4},{14,6},{20,12},... | collective-permute-start | bytes 1572872 | tf_op jit(solution)/shard_map/ppermute | solution.py:422
  103.3 9.0 %copy-start.23 = (f32[64]{0:T(128)S(1)}, f32[64]{0:T(128)}, u32[]{:S(2)}) copy-start(f32[64]{0:T(128)} %param.17) | copy-start | bytes 772
  103.3 9.1 %copy-start.5 = (f32[1024,64]{0,1:T(8,128)S(1)}, f32[1024,64]{0,1:T(8,128)}, u32[]{:S(2)}) copy-start(f32[1024,64]{0,1:T(8,128)} %param.16) | copy-start | bytes 786436
  112.2 10.2 %collective-permute-start.20 = (bf16[96,8192]{1,0:T(8,128)(2,1)}, bf16[96,8192]{1,0:T(8,128)(2,1)}, u32[]{:S(2)}, u32[]{:S(2)}) collective-permute-start(bf16[96,8192]{1,0:T(8,128)(2,1)} %adjoint_sweeps.5.refs_1_), channel_id=1, source_target_pairs={{0,2},{2,0},{4,6},{6,4},{8,10},{10,8},{12,14},{14,12},{16,18},{18,... | collective-permute-start | bytes 4718600 | tf_op jit(solution)/shard_map/ppermute | solution.py:413
  112.4 2.0 %copy-start.20 = (f32[8,16,128]{2,1,0:T(8,128)S(1)}, f32[8,16,128]{2,1,0:T(8,128)}, u32[]{:S(2)}) copy-start(f32[8,16,128]{2,1,0:T(8,128)} %copy-done.18) | copy-start | bytes 196612
  114.3 8.0 %copy-start.4 = (f32[1024,64]{0,1:T(8,128)S(1)}, f32[1024,64]{0,1:T(8,128)}, u32[]{:S(2)}) copy-start(f32[1024,64]{0,1:T(8,128)} %param.15) | copy-start | bytes 786436
  119.8 8.3 %collective-permute-start.18 = (bf16[64,8192]{1,0:T(8,128)(2,1)S(1)}, bf16[64,8192]{1,0:T(8,128)(2,1)S(1)}, u32[]{:S(2)}, u32[]{:S(2)}) collective-permute-start(bf16[64,8192]{1,0:T(8,128)(2,1)S(1)} %adjoint_sweeps.3.refs_0_), channel_id=1, source_target_pairs={{0,2},{2,0},{4,6},{6,4},{8,10},{10,8},{12,14},{14,12},{16,18},{18,... | collective-permute-start | bytes 3145736 | tf_op jit(solution)/shard_map/ppermute | solution.py:413
  120.4 14.1 %collective-permute-start.24 = (bf16[64,1024]{1,0:T(8,128)(2,1)S(1)}, bf16[64,1024]{1,0:T(8,128)(2,1)S(1)}, u32[]{:S(2)}, u32[]{:S(2)}) collective-permute-start(bf16[64,1024]{1,0:T(8,128)(2,1)S(1)} %get-tuple-element.62), channel_id=1, source_target_pairs={{0,2},{2,0},{4,6},{6,4},{8,10},{10,8},{12,14},{14,12},{16,18},{18,... | collective-permute-start | bytes 393224 | tf_op jit(solution)/shard_map/ppermute | solution.py:413
  120.4 16.4 %collective-permute-start.25 = (bf16[64,1024]{1,0:T(8,128)(2,1)S(1)}, bf16[64,1024]{1,0:T(8,128)(2,1)S(1)}, u32[]{:S(2)}, u32[]{:S(2)}) collective-permute-start(bf16[64,1024]{1,0:T(8,128)(2,1)S(1)} %get-tuple-element.63), channel_id=1, source_target_pairs={{0,4},{2,6},{4,0},{6,2},{8,12},{10,14},{12,8},{14,10},{16,20},{18,... | collective-permute-start | bytes 393224 | tf_op jit(solution)/shard_map/ppermute | solution.py:413
  122.3 14.5 %collective-permute-start.26 = (bf16[64,1024]{1,0:T(8,128)(2,1)S(1)}, bf16[64,1024]{1,0:T(8,128)(2,1)S(1)}, u32[]{:S(2)}, u32[]{:S(2)}) collective-permute-start(bf16[64,1024]{1,0:T(8,128)(2,1)S(1)} %get-tuple-element.64), channel_id=1, source_target_pairs={{0,6},{2,4},{4,2},{6,0},{8,14},{10,12},{12,10},{14,8},{16,22},{18,... | collective-permute-start | bytes 393224 | tf_op jit(solution)/shard_map/ppermute | solution.py:413
  130.8 8.3 %collective-permute-start.21 = (bf16[64,512]{1,0:T(8,128)(2,1)S(1)}, bf16[64,512]{1,0:T(8,128)(2,1)S(1)}, u32[]{:S(2)}, u32[]{:S(2)}) collective-permute-start(bf16[64,512]{1,0:T(8,128)(2,1)S(1)} %get-tuple-element.59), channel_id=1, source_target_pairs={{0,8},{2,10},{4,12},{6,14},{8,16},{10,18},{12,20},{14,22},{16,24},... | collective-permute-start | bytes 196616 | tf_op jit(solution)/shard_map/ppermute | solution.py:502
  132.5 7.3 %collective-permute-start.22 = (bf16[64,512]{1,0:T(8,128)(2,1)S(1)}, bf16[64,512]{1,0:T(8,128)(2,1)S(1)}, u32[]{:S(2)}, u32[]{:S(2)}) collective-permute-start(bf16[64,512]{1,0:T(8,128)(2,1)S(1)} %get-tuple-element.60), channel_id=1, source_target_pairs={{0,16},{2,18},{4,20},{6,22},{8,24},{10,26},{12,28},{14,30},{16,0},... | collective-permute-start | bytes 196616 | tf_op jit(solution)/shard_map/ppermute | solution.py:502
  134.5 5.3 %collective-permute-start.23 = (bf16[64,512]{1,0:T(8,128)(2,1)S(1)}, bf16[64,512]{1,0:T(8,128)(2,1)S(1)}, u32[]{:S(2)}, u32[]{:S(2)}) collective-permute-start(bf16[64,512]{1,0:T(8,128)(2,1)S(1)} %get-tuple-element.61), channel_id=1, source_target_pairs={{0,24},{2,26},{4,28},{6,30},{8,0},{10,2},{12,4},{14,6},{16,8},{18,... | collective-permute-start | bytes 196616 | tf_op jit(solution)/shard_map/ppermute | solution.py:502
  137.6 5.0 %collective-permute-start.27 = (bf16[64,1024]{1,0:T(8,128)(2,1)S(1)}, bf16[64,1024]{1,0:T(8,128)(2,1)S(1)}, u32[]{:S(2)}, u32[]{:S(2)}) collective-permute-start(bf16[64,1024]{1,0:T(8,128)(2,1)S(1)} %bitcast.43), channel_id=1, source_target_pairs={{0,1},{1,0},{2,3},{3,2},{4,5},{5,4},{6,7},{7,6},{8,9},{9,8},{10,11... | collective-permute-start | bytes 393224 | tf_op jit(solution)/shard_map/ppermute | solution.py:416

commit v6 on v5

--- a/solution.py
+++ b/solution.py
@@ -238,10 +238,14 @@
     count, width, _ = pieces.shape
     depth = cells // GROUP
     dims = (((1,), (1,)), ((), ()))
-    total = jnp.zeros((count * width, rows_total), jnp.float32)
+    flip = rows_total > count * width
+    total = jnp.zeros((rows_total, count * width) if flip else (count * width, rows_total), jnp.float32)
     for plane in range(GROUP):
         rows, cols = slab(adjoint, plane * depth, depth), slab(direct, plane * depth, depth)
-        total = total + lax.dot_general(cols, rows, dims, preferred_element_type=jnp.float32)
+        pair = (rows, cols) if flip else (cols, rows)
+        total = total + lax.dot_general(*pair, dims, preferred_element_type=jnp.float32)
+    if flip:
+        total = total.T
     per_share = factors.shape[1] // shares
     window = factors[:, pl.ds(pl.multiple_of(share * per_share, per_share), per_share)]
     window = scaled_factors(window[:, start : start + rows_total], singular)
@@ -475,7 +479,7 @@
     y_adj, e_adj, l_adj, own_states, far_states = [], [], [], [], []
     for i, pair in enumerate(pairs):
         y_after = [near, far, late_near] if i == 0 else [y_adj[-1], dir_states[0]]
-        e_after = [e_d] if i == 0 else [e_adj[-1], dir_states[-1]]
+        e_after = [e_d] if i == 0 else [e_adj[-1], dir_states[-1] if i == 1 else y_adj[1]]
         y_adj.append(swap(after(pair, *y_after), 2))
         e_adj.append(early(after(pair, *e_after)))
         l_adj.append(late(after(y_adj[i], l_adj[-1]) if i else y_adj[i]))

time: 144 us -> 144 us (level)
  no operation moved by 1% of the time
where the time goes in v6:
time: 144 us; the launch traced here: 143 us
  Pallas kernels  50.5 us (35%)
  starting transfers between devices  48.9 us (34%)
  waiting for transfers between devices  32 us (22%)
  local copies, waits for them, and re-layouts  9.62 us (7%)
    pallas_call x14, Pallas kernels, call(): pl.pallas_call(kernel, in_specs=in_specs, out_specs=jax.tree.map(lambda _...  50.5 us
    ppermute x5, starting transfers between devices, per_device(): lax.ppermute(array, 'space', upper(ups, 0) + upper(downs, 1))  21.4 us
    ppermute x13, waiting for transfers between devices, swap(): return lax.ppermute(array, 'space', [(i, i ^ mask) for i in range(n_space)])  21.3 us
    ppermute x13, starting transfers between devices, swap(): return lax.ppermute(array, 'space', [(i, i ^ mask) for i in range(n_space)])  11.7 us
    unnamed x52, local copies, waits for them, and re-layouts  8.72 us
    ppermute x5, waiting for transfers between devices, per_device(): lax.ppermute(array, 'space', upper(ups, 0) + upper(downs, 1))  7.9 us
    ppermute x3, starting transfers between devices, per_device(): lax.ppermute(sent[step - 1], 'space', pairs).astype(jnp.float32)  6 us
    ppermute x4, starting transfers between devices, per_device(): lax.ppermute(array, 'space', upper(ups, 1) + upper(downs, 0))  5.27 us
  transfers between devices with their start and end apart: 28, of which 9 were waited for; matrix products, arithmetic and copies ran while one was open for 2% of the time, Pallas kernels for 35%

profile of v6, /device:TPU:0, one launch (start us, length us, event | category | flops | bytes accessed | tf_op | source)
XLA Modules:
  0.0 143.2 jit_solution(433390807140585620)
XLA Ops:
  0.9 0.1 stack.62.info.token
  1.0 1.6 %copy-done = bf16[512,1,16,128]{3,2,1,0:T(8,128)(2,1)S(1)} copy-done((bf16[512,1,16,128]{3,2,1,0:T(8,128)(2,1)S(1)}, bf16[512,1,16,128]{3,2,1,0:T(8,128)(2,1)}, u32[]{:S(2)}) %copy-start) | copy-done | bytes 2097176
  2.6 0.7 copy-done.6
  3.3 0.9 pack.2
  4.2 0.5 collective-permute-start
  4.7 2.6 %collective-permute-start.2 = (bf16[132,16,128]{2,1,0:T(8,128)(2,1)S(1)}, bf16[132,16,128]{2,1,0:T(8,128)(2,1)S(1)}, u32[]{:S(2)}, u32[]{:S(2)}) collective-permute-start(bf16[132,16,128]{2,1,0:T(8,128)(2,1)S(1)} %get-tuple-element.40), channel_id=1, source_target_pairs={{0,4},{2,6},{4,0},{6,2},{8,12},{10,14},{12,8},{14,10},{16,20},{18,... | collective-permute-start | bytes 1622024 | tf_op jit(solution)/shard_map/ppermute | solution.py:417
  7.3 1.4 pack.3
  8.7 0.2 collective-permute-start.1
  9.1 1.4 collective-permute-start.6
  10.5 4.7 %collective-permute-start.3 = (bf16[132,16,128]{2,1,0:T(8,128)(2,1)S(1)}, bf16[132,16,128]{2,1,0:T(8,128)(2,1)S(1)}, u32[]{:S(2)}, u32[]{:S(2)}) collective-permute-start(bf16[132,16,128]{2,1,0:T(8,128)(2,1)S(1)} %get-tuple-element.41), channel_id=1, source_target_pairs={{0,6},{2,4},{4,2},{6,0},{8,14},{10,12},{12,10},{14,8},{16,22},{18,... | collective-permute-start | bytes 1622024 | tf_op jit(solution)/shard_map/ppermute | solution.py:417
  15.2 5.2 %collective-permute-done.2.refs_1_ = bf16[132,16,128]{2,1,0:T(8,128)(2,1)S(1)} collective-permute-done((bf16[132,16,128]{2,1,0:T(8,128)(2,1)S(1)}, bf16[132,16,128]{2,1,0:T(8,128)(2,1)S(1)}, u32[]{:S(2)}, u32[]{:S(2)}) %collective-permute-start.2) | collective-permute-done | bytes 540704 | tf_op jit(solution)/shard_map/ppermute | solution.py:417
  20.5 3.9 %collective-permute-start.4 = (bf16[132,16,128]{2,1,0:T(8,128)(2,1)S(1)}, bf16[132,16,128]{2,1,0:T(8,128)(2,1)S(1)}, u32[]{:S(2)}, u32[]{:S(2)}) collective-permute-start(bf16[132,16,128]{2,1,0:T(8,128)(2,1)S(1)} %collective-permute-done.2.refs_1_), channel_id=1, source_target_pairs={{0,8},{2,10},{8,16},{10,18},{16,24},{18,26},{12,4},{14,6},{20,12},... | collective-permute-start | bytes 1622024 | tf_op jit(solution)/shard_map/ppermute | solution.py:426
  24.4 7.1 %collective-permute-done.3.refs_2_ = bf16[132,16,128]{2,1,0:T(8,128)(2,1)S(1)} collective-permute-done((bf16[132,16,128]{2,1,0:T(8,128)(2,1)S(1)}, bf16[132,16,128]{2,1,0:T(8,128)(2,1)S(1)}, u32[]{:S(2)}, u32[]{:S(2)}) %collective-permute-start.3) | collective-permute-done | bytes 540704 | tf_op jit(solution)/shard_map/ppermute | solution.py:417
  31.5 4.3 %collective-permute-start.7 = (bf16[132,16,128]{2,1,0:T(8,128)(2,1)S(1)}, bf16[132,16,128]{2,1,0:T(8,128)(2,1)}, u32[]{:S(2)}, u32[]{:S(2)}) collective-permute-start(bf16[132,16,128]{2,1,0:T(8,128)(2,1)S(1)} %collective-permute-done.3.refs_2_), channel_id=1, source_target_pairs={{0,8},{2,10},{8,16},{10,18},{16,24},{18,26},{12,4},{14,6},{20,12},... | collective-permute-start | bytes 1622024 | tf_op jit(solution)/shard_map/ppermute | solution.py:426
  35.8 0.9 join.6.refs_0_
  36.8 0.8 copy-done.16
  37.6 0.9 collective-permute-start.5
  38.5 0.1 select_reduce_fusion
  38.6 0.1 reshape.31
  38.7 0.1 broadcast_in_dim.28
  38.8 0.1 stack.71.place
  38.9 1.0 join.5.refs_0_
  39.9 1.3 collective-permute-start.12
  41.2 6.2 %collective-permute-done.7.refs_5_ = bf16[132,16,128]{2,1,0:T(8,128)(2,1)} collective-permute-done((bf16[132,16,128]{2,1,0:T(8,128)(2,1)S(1)}, bf16[132,16,128]{2,1,0:T(8,128)(2,1)}, u32[]{:S(2)}, u32[]{:S(2)}) %collective-permute-start.7) | collective-permute-done | bytes 540704 | tf_op jit(solution)/shard_map/ppermute | solution.py:426
  47.5 1.0 copy-done.14
  48.6 5.8 %direct_sweeps.2 = (bf16[64,8192]{1,0:T(8,128)(2,1)S(1)}, f32[8,16,128]{2,1,0:T(8,128)S(1)}) custom-call(s32[8]{0:T(128)S(1)} %stack.71.place, bf16[264,16,128]{2,1,0:T(8,128)(2,1)S(1)} %join.7.refs_0_, bf16[132,16,128]{2,1,0:T(8,128)(2,1)S(1)} %copy-done.12, bf16[132,16,128]{2,1,0:T(8,128)(2,1)S(1)} %copy-done.14, ...), custom_call_target="tpu_custom_call" | custom-call | flops 3407872000 | bytes 1024 | tf_op jit(solution)/shard_map/direct_sweeps/pallas_call | solution.py:25
  54.4 3.4 %collective-permute-done.5.refs_1_ = bf16[192,16,128]{2,1,0:T(8,128)(2,1)} collective-permute-done((bf16[192,16,128]{2,1,0:T(8,128)(2,1)}, bf16[192,16,128]{2,1,0:T(8,128)(2,1)}, u32[]{:S(2)}, u32[]{:S(2)}) %collective-permute-start.5) | collective-permute-done | bytes 786464 | tf_op jit(solution)/shard_map/ppermute | solution.py:417
  57.8 0.2 collective-permute-start.8
  58.0 2.7 %collective-permute-start.15 = (bf16[192,16,128]{2,1,0:T(8,128)(2,1)}, bf16[192,16,128]{2,1,0:T(8,128)(2,1)S(1)}, u32[]{:S(2)}, u32[]{:S(2)}) collective-permute-start(bf16[192,16,128]{2,1,0:T(8,128)(2,1)} %collective-permute-done.5.refs_1_), channel_id=1, source_target_pairs={{0,8},{2,10},{8,16},{10,18},{16,24},{18,26},{12,4},{14,6},{20,12},... | collective-permute-start | bytes 2359304 | tf_op jit(solution)/shard_map/ppermute | solution.py:426
  60.8 1.6 %collective-permute-start.10 = (bf16[64,8192]{1,0:T(8,128)(2,1)S(1)}, bf16[64,8192]{1,0:T(8,128)(2,1)S(1)}, u32[]{:S(2)}, u32[]{:S(2)}) collective-permute-start(bf16[64,8192]{1,0:T(8,128)(2,1)S(1)} %get-tuple-element.44.refs_0_.refs_4_.refs_2_), channel_id=1, source_target_pairs={{0,1},{1,0},{2,3},{3,2},{4,5},{5,4},{6,7},{7,6},{8,9},{9,8},{10,11... | collective-permute-start | bytes 3145736 | tf_op jit(solution)/shard_map/ppermute | solution.py:420
  62.4 1.2 copy-done.3
  63.6 6.7 %direct_sweeps.3.refs_1_.refs_5_.refs_3_ = bf16[64,8192]{1,0:T(8,128)(2,1)} custom-call(s32[8]{0:T(128)S(1)} %stack.71.place, bf16[264,16,128]{2,1,0:T(8,128)(2,1)S(1)} %copy-done.3, bf16[132,16,128]{2,1,0:T(8,128)(2,1)S(1)} %copy-done.12, bf16[132,16,128]{2,1,0:T(8,128)(2,1)S(1)} %copy-done.15, bf16[264,16,128]{2,1,0:T(8,128)(2,1)} %collective-permute-done.6.refs_3_, ...), custom_call_target="tpu_custom_call" | custom-call | flops 3407872000 | bytes 1024 | tf_op jit(solution)/shard_map/direct_sweeps/pallas_call | solution.py:25
  70.3 0.9 copy-done.7
  71.2 1.3 collective-permute-start.13
  72.5 4.7 %collective-permute-done.8.refs_1_ = bf16[192,16,128]{2,1,0:T(8,128)(2,1)} collective-permute-done((bf16[192,16,128]{2,1,0:T(8,128)(2,1)}, bf16[192,16,128]{2,1,0:T(8,128)(2,1)}, u32[]{:S(2)}, u32[]{:S(2)}) %collective-permute-start.8) | collective-permute-done | bytes 786464 | tf_op jit(solution)/shard_map/ppermute | solution.py:417
  77.3 0.9 copy-done.9
  78.2 5.2 %collective-permute-start.16 = (bf16[192,16,128]{2,1,0:T(8,128)(2,1)}, bf16[192,16,128]{2,1,0:T(8,128)(2,1)}, u32[]{:S(2)}, u32[]{:S(2)}) collective-permute-start(bf16[192,16,128]{2,1,0:T(8,128)(2,1)} %collective-permute-done.8.refs_1_), channel_id=1, source_target_pairs={{0,8},{2,10},{8,16},{10,18},{16,24},{18,26},{12,4},{14,6},{20,12},... | collective-permute-start | bytes 2359304 | tf_op jit(solution)/shard_map/ppermute | solution.py:426
  83.4 0.8 join.4.refs_0_
  84.2 0.1 fusion
  84.3 1.5 %collective-permute-start.11 = (bf16[64,8192]{1,0:T(8,128)(2,1)}, bf16[64,8192]{1,0:T(8,128)(2,1)S(1)}, u32[]{:S(2)}, u32[]{:S(2)}) collective-permute-start(bf16[64,8192]{1,0:T(8,128)(2,1)} %direct_sweeps.3.refs_1_.refs_5_.refs_3_), channel_id=1, source_target_pairs={{0,1},{1,0},{2,3},{3,2},{4,5},{5,4},{6,7},{7,6},{8,9},{9,8},{10,11... | collective-permute-start | bytes 3145736 | tf_op jit(solution)/shard_map/ppermute | solution.py:420
  85.9 8.4 %adjoint_sweeps.4.refs_0_ = bf16[96,8192]{1,0:T(8,128)(2,1)} custom-call(s32[8]{0:T(128)S(1)} %stack.71.place, bf16[192,16,128]{2,1,0:T(8,128)(2,1)} %join.6.refs_0_, bf16[192,16,128]{2,1,0:T(8,128)(2,1)} %collective-permute-done.5.refs_1_, bf16[192,16,128]{2,1,0:T(8,128)(2,1)S(1)} %copy-done.8, bf16[192,16,128]{2,1,0:T(8,128)(2,1)S(1)} %copy-done.10, ...), custom_call_target="tpu_custom_call" | custom-call | flops 5111808000 | bytes 1024 | tf_op jit(solution)/shard_map/adjoint_sweeps/pallas_call | solution.py:25
  94.3 1.3 collective-permute-start.14
  95.6 0.8 collective-permute-done.9.refs_1_
  96.4 1.6 %collective-permute-done.16.refs_3_ = bf16[192,16,128]{2,1,0:T(8,128)(2,1)} collective-permute-done((bf16[192,16,128]{2,1,0:T(8,128)(2,1)}, bf16[192,16,128]{2,1,0:T(8,128)(2,1)}, u32[]{:S(2)}, u32[]{:S(2)}) %collective-permute-start.16) | collective-permute-done | bytes 786464 | tf_op jit(solution)/shard_map/ppermute | solution.py:426
  98.0 5.2 %collective-permute-start.17 = (bf16[128,16,128]{2,1,0:T(8,128)(2,1)}, bf16[128,16,128]{2,1,0:T(8,128)(2,1)}, u32[]{:S(2)}, u32[]{:S(2)}) collective-permute-start(bf16[128,16,128]{2,1,0:T(8,128)(2,1)} %collective-permute-done.9.refs_1_), channel_id=1, source_target_pairs={{0,8},{2,10},{8,16},{10,18},{16,24},{18,26},{12,4},{14,6},{20,12},... | collective-permute-start | bytes 1572872 | tf_op jit(solution)/shard_map/ppermute | solution.py:426
  103.3 8.9 %adjoint_sweeps.5.refs_1_ = bf16[96,8192]{1,0:T(8,128)(2,1)} custom-call(s32[8]{0:T(128)S(1)} %stack.71.place, bf16[192,16,128]{2,1,0:T(8,128)(2,1)} %join.5.refs_0_, bf16[192,16,128]{2,1,0:T(8,128)(2,1)} %collective-permute-done.8.refs_1_, bf16[192,16,128]{2,1,0:T(8,128)(2,1)} %collective-permute-done.13.refs_2_, ...), custom_call_target="tpu_custom_call" | custom-call | flops 5111808000 | bytes 1024 | tf_op jit(solution)/shard_map/adjoint_sweeps/pallas_call | solution.py:25
  112.2 0.1 dynamic_slice.14
  112.3 0.1 copy.24.singular
  112.4 1.9 %direct_modes_part.1 = (f32[64,1024]{1,0:T(8,128)S(1)}, bf16[64,1024]{1,0:T(8,128)(2,1)S(1)}, bf16[64,1024]{1,0:T(8,128)(2,1)S(1)}, bf16[64,1024]{1,0:T(8,128)(2,1)S(1)}) custom-call(s32[8]{0:T(128)S(1)} %stack.62.info.token, f32[64,1024]{1,0:T(8,128)S(1)} %bitcast.42, f32[64,1]{1,0:T(8,128)S(1)} %copy.24.singular, ...), custom_call_target="tpu_custom_call" | custom-call | flops 524288 | bytes 1024 | tf_op jit(solution)/shard_map/direct_modes_part/pallas_call | solution.py:25
  114.3 5.5 %adjoint_sweeps.3.refs_0_ = bf16[64,8192]{1,0:T(8,128)(2,1)S(1)} custom-call(s32[8]{0:T(128)S(1)} %stack.71.place, bf16[128,16,128]{2,1,0:T(8,128)(2,1)} %join.4.refs_0_, bf16[128,16,128]{2,1,0:T(8,128)(2,1)} %collective-permute-done.9.refs_1_, bf16[128,16,128]{2,1,0:T(8,128)(2,1)} %collective-permute-done.14.refs_2_, ...), custom_call_target="tpu_custom_call" | custom-call | flops 3407872000 | bytes 1024 | tf_op jit(solution)/shard_map/adjoint_sweeps/pallas_call | solution.py:25
  119.8 0.6 collective-permute-start.18
  120.4 0.1 collective-permute-start.24
  120.4 1.9 %collective-permute-start.25 = (bf16[64,1024]{1,0:T(8,128)(2,1)S(1)}, bf16[64,1024]{1,0:T(8,128)(2,1)S(1)}, u32[]{:S(2)}, u32[]{:S(2)}) collective-permute-start(bf16[64,1024]{1,0:T(8,128)(2,1)S(1)} %get-tuple-element.63), channel_id=1, source_target_pairs={{0,4},{2,6},{4,0},{6,2},{8,12},{10,14},{12,8},{14,10},{16,20},{18,... | collective-permute-start | bytes 393224 | tf_op jit(solution)/shard_map/ppermute | solution.py:417
  122.4 5.5 %gram_part.2 = (f32[4,64,384]{2,1,0:T(8,128)S(1)}, f32[64,2048]{1,0:T(8,128)S(1)}) custom-call(s32[8]{0:T(128)S(1)} %stack.62.info.token, f32[64,1024]{1,0:T(8,128)S(1)} %bitcast.40, f32[64,1]{1,0:T(8,128)S(1)} %copy.24.singular, bf16[96,8192]{1,0:T(8,128)(2,1)} %adjoint_sweeps.4.refs_0_, bf16[96,8192]{1,0:T(8,128)(2,1)} %adjoint_sweeps.5.refs_1_, ...), custom_call_target="tpu_custom_call" | custom-call | flops 3145728 | bytes 1024 | tf_op jit(solution)/shard_map/gram_part/pallas_call | solution.py:25
  127.9 2.7 %gram_part.3 = (f32[64,512]{1,0:T(8,128)S(1)}, bf16[64,512]{1,0:T(8,128)(2,1)S(1)}, bf16[64,512]{1,0:T(8,128)(2,1)S(1)}, bf16[64,512]{1,0:T(8,128)(2,1)S(1)}, f3...) custom-call(s32[8]{0:T(128)S(1)} %stack.62.info.token, f32[64,1024]{1,0:T(8,128)S(1)} %bitcast.41, ...), custom_call_target="tpu_custom_call" | custom-call | flops 1048576 | bytes 1024 | tf_op jit(solution)/shard_map/gram_part/pallas_call | solution.py:25
  130.6 1.7 %collective-permute-start.21 = (bf16[64,512]{1,0:T(8,128)(2,1)S(1)}, bf16[64,512]{1,0:T(8,128)(2,1)S(1)}, u32[]{:S(2)}, u32[]{:S(2)}) collective-permute-start(bf16[64,512]{1,0:T(8,128)(2,1)S(1)} %get-tuple-element.59), channel_id=1, source_target_pairs={{0,8},{2,10},{4,12},{6,14},{8,16},{10,18},{12,20},{14,22},{16,24},... | collective-permute-start | bytes 196616 | tf_op jit(solution)/shard_map/ppermute | solution.py:506
  132.2 2.0 %collective-permute-start.22 = (bf16[64,512]{1,0:T(8,128)(2,1)S(1)}, bf16[64,512]{1,0:T(8,128)(2,1)S(1)}, u32[]{:S(2)}, u32[]{:S(2)}) collective-permute-start(bf16[64,512]{1,0:T(8,128)(2,1)S(1)} %get-tuple-element.60), channel_id=1, source_target_pairs={{0,16},{2,18},{4,20},{6,22},{8,24},{10,26},{12,28},{14,30},{16,0},... | collective-permute-start | bytes 196616 | tf_op jit(solution)/shard_map/ppermute | solution.py:506
  134.3 2.3 %collective-permute-start.23 = (bf16[64,512]{1,0:T(8,128)(2,1)S(1)}, bf16[64,512]{1,0:T(8,128)(2,1)S(1)}, u32[]{:S(2)}, u32[]{:S(2)}) collective-permute-start(bf16[64,512]{1,0:T(8,128)(2,1)S(1)} %get-tuple-element.61), channel_id=1, source_target_pairs={{0,24},{2,26},{4,28},{6,30},{8,0},{10,2},{12,4},{14,6},{16,8},{18,... | collective-permute-start | bytes 196616 | tf_op jit(solution)/shard_map/ppermute | solution.py:506
  136.7 0.8 copy.27
  137.4 1.5 %collective-permute-start.27 = (bf16[64,1024]{1,0:T(8,128)(2,1)S(1)}, bf16[64,1024]{1,0:T(8,128)(2,1)S(1)}, u32[]{:S(2)}, u32[]{:S(2)}) collective-permute-start(bf16[64,1024]{1,0:T(8,128)(2,1)S(1)} %bitcast.43), channel_id=1, source_target_pairs={{0,1},{1,0},{2,3},{3,2},{4,5},{5,4},{6,7},{7,6},{8,9},{9,8},{10,11... | collective-permute-start | bytes 393224 | tf_op jit(solution)/shard_map/ppermute | solution.py:420
  138.9 0.7 collective-permute-done.22
  139.6 0.7 multiply_bitcast_fusion
  140.3 2.1 %collective-permute-done.27 = bf16[64,1024]{1,0:T(8,128)(2,1)S(1)} collective-permute-done((bf16[64,1024]{1,0:T(8,128)(2,1)S(1)}, bf16[64,1024]{1,0:T(8,128)(2,1)S(1)}, u32[]{:S(2)}, u32[]{:S(2)}) %collective-permute-start.27) | collective-permute-done | bytes 131104 | tf_op jit(solution)/shard_map/ppermute | solution.py:420
  142.4 0.8 copy.28
  (76 shorter events, 0.7 us)
Async XLA Ops:
  1.0 1.6 %copy-start = (bf16[512,1,16,128]{3,2,1,0:T(8,128)(2,1)S(1)}, bf16[512,1,16,128]{3,2,1,0:T(8,128)(2,1)}, u32[]{:S(2)}) copy-start(bf16[512,1,16,128]{3,2,1,0:T(8,128)(2,1)} %param.9) | copy-start | bytes 6291460
  2.6 0.7 copy-start.6
  3.3 4.0 %copy-start.1 = (bf16[512,1,16,128]{3,2,1,0:T(8,128)(2,1)S(1)}, bf16[512,1,16,128]{3,2,1,0:T(8,128)(2,1)}, u32[]{:S(2)}) copy-start(bf16[512,1,16,128]{3,2,1,0:T(8,128)(2,1)} %param.10) | copy-start | bytes 6291460
  4.2 3.1 %collective-permute-start = (bf16[132,16,128]{2,1,0:T(8,128)(2,1)S(1)}, bf16[132,16,128]{2,1,0:T(8,128)(2,1)S(1)}, u32[]{:S(2)}, u32[]{:S(2)}) collective-permute-start(bf16[132,16,128]{2,1,0:T(8,128)(2,1)S(1)} %get-tuple-element.35), channel_id=1, source_target_pairs={{0,2},{2,0},{4,6},{6,4},{8,10},{10,8},{12,14},{14,12},{16,18},{18,... | collective-permute-start | bytes 1622024 | tf_op jit(solution)/shard_map/ppermute | solution.py:417
  4.7 15.7 %collective-permute-start.2 = (bf16[132,16,128]{2,1,0:T(8,128)(2,1)S(1)}, bf16[132,16,128]{2,1,0:T(8,128)(2,1)S(1)}, u32[]{:S(2)}, u32[]{:S(2)}) collective-permute-start(bf16[132,16,128]{2,1,0:T(8,128)(2,1)S(1)} %get-tuple-element.40), channel_id=1, source_target_pairs={{0,4},{2,6},{4,0},{6,2},{8,12},{10,14},{12,8},{14,10},{16,20},{18,... | collective-permute-start | bytes 1622024 | tf_op jit(solution)/shard_map/ppermute | solution.py:417
  8.7 27.1 %collective-permute-start.1 = (bf16[256,16,128]{2,1,0:T(8,128)(2,1)S(1)}, bf16[256,16,128]{2,1,0:T(8,128)(2,1)S(1)}, u32[]{:S(2)}, u32[]{:S(2)}) collective-permute-start(bf16[256,16,128]{2,1,0:T(8,128)(2,1)S(1)} %get-tuple-element.37), channel_id=1, source_target_pairs={{0,2},{2,0},{4,6},{6,4},{8,10},{10,8},{12,14},{14,12},{16,18},{18,... | collective-permute-start | bytes 3145736 | tf_op jit(solution)/shard_map/ppermute | solution.py:417
  9.0 38.4 %copy-start.2 = (bf16[264,16,128]{2,1,0:T(8,128)(2,1)}, bf16[264,16,128]{2,1,0:T(8,128)(2,1)S(1)}, u32[]{:S(2)}) copy-start(bf16[264,16,128]{2,1,0:T(8,128)(2,1)S(1)} %join.7.refs_0_) | copy-start | bytes 3244036
  9.0 29.4 %copy-start.21 = (s32[512]{0:T(512)S(1)}, s32[512]{0:T(512)}, u32[]{:S(2)}) copy-start(s32[512]{0:T(512)} %param.14) | copy-start | bytes 6148
  9.1 29.4 %copy-start.22 = (s32[512]{0:T(512)S(1)}, s32[512]{0:T(512)}, u32[]{:S(2)}) copy-start(s32[512]{0:T(512)} %param.13) | copy-start | bytes 6148
  9.1 29.4 %copy-start.24 = (f32[16]{0:T(128)S(1)}, f32[16]{0:T(128)}, u32[]{:S(2)}) copy-start(f32[16]{0:T(128)} %param.12) | copy-start | bytes 196
  9.1 30.8 %collective-permute-start.6 = (bf16[264,16,128]{2,1,0:T(8,128)(2,1)S(1)}, bf16[264,16,128]{2,1,0:T(8,128)(2,1)}, u32[]{:S(2)}, u32[]{:S(2)}) collective-permute-start(bf16[264,16,128]{2,1,0:T(8,128)(2,1)S(1)} %join.7.refs_0_), channel_id=1, source_target_pairs={{4,12},{6,14},{12,20},{14,22},{20,28},{22,30},{8,0},{10,2},{16,8},... | collective-permute-start | bytes 3244040 | tf_op jit(solution)/shard_map/ppermute | solution.py:425
  10.5 21.0 %collective-permute-start.3 = (bf16[132,16,128]{2,1,0:T(8,128)(2,1)S(1)}, bf16[132,16,128]{2,1,0:T(8,128)(2,1)S(1)}, u32[]{:S(2)}, u32[]{:S(2)}) collective-permute-start(bf16[132,16,128]{2,1,0:T(8,128)(2,1)S(1)} %get-tuple-element.41), channel_id=1, source_target_pairs={{0,6},{2,4},{4,2},{6,0},{8,14},{10,12},{12,10},{14,8},{16,22},{18,... | collective-permute-start | bytes 1622024 | tf_op jit(solution)/shard_map/ppermute | solution.py:417
  20.4 16.3 %copy-start.11 = (bf16[132,16,128]{2,1,0:T(8,128)(2,1)}, bf16[132,16,128]{2,1,0:T(8,128)(2,1)S(1)}, u32[]{:S(2)}) copy-start(bf16[132,16,128]{2,1,0:T(8,128)(2,1)S(1)} %collective-permute-done.2.refs_1_) | copy-start | bytes 1622020
  20.5 16.4 %collective-permute-start.4 = (bf16[132,16,128]{2,1,0:T(8,128)(2,1)S(1)}, bf16[132,16,128]{2,1,0:T(8,128)(2,1)S(1)}, u32[]{:S(2)}, u32[]{:S(2)}) collective-permute-start(bf16[132,16,128]{2,1,0:T(8,128)(2,1)S(1)} %collective-permute-done.2.refs_1_), channel_id=1, source_target_pairs={{0,8},{2,10},{8,16},{10,18},{16,24},{18,26},{12,4},{14,6},{20,12},... | collective-permute-start | bytes 1622024 | tf_op jit(solution)/shard_map/ppermute | solution.py:426
  31.5 8.4 %copy-start.13 = (bf16[132,16,128]{2,1,0:T(8,128)(2,1)}, bf16[132,16,128]{2,1,0:T(8,128)(2,1)S(1)}, u32[]{:S(2)}) copy-start(bf16[132,16,128]{2,1,0:T(8,128)(2,1)S(1)} %collective-permute-done.3.refs_2_) | copy-start | bytes 1622020
  31.5 15.9 %collective-permute-start.7 = (bf16[132,16,128]{2,1,0:T(8,128)(2,1)S(1)}, bf16[132,16,128]{2,1,0:T(8,128)(2,1)}, u32[]{:S(2)}, u32[]{:S(2)}) collective-permute-start(bf16[132,16,128]{2,1,0:T(8,128)(2,1)S(1)} %collective-permute-done.3.refs_2_), channel_id=1, source_target_pairs={{0,8},{2,10},{8,16},{10,18},{16,24},{18,26},{12,4},{14,6},{20,12},... | collective-permute-start | bytes 1622024 | tf_op jit(solution)/shard_map/ppermute | solution.py:426
  36.8 0.8 copy-start.16
  37.6 20.2 %collective-permute-start.5 = (bf16[192,16,128]{2,1,0:T(8,128)(2,1)}, bf16[192,16,128]{2,1,0:T(8,128)(2,1)}, u32[]{:S(2)}, u32[]{:S(2)}) collective-permute-start(bf16[192,16,128]{2,1,0:T(8,128)(2,1)} %join.6.refs_0_), channel_id=1, source_target_pairs={{0,4},{2,6},{4,0},{6,2},{8,12},{10,14},{12,8},{14,10},{16,20},{18,... | collective-permute-start | bytes 2359304 | tf_op jit(solution)/shard_map/ppermute | solution.py:417
  38.9 8.6 %copy-start.12 = (bf16[132,16,128]{2,1,0:T(8,128)(2,1)S(1)}, bf16[132,16,128]{2,1,0:T(8,128)(2,1)}, u32[]{:S(2)}) copy-start(bf16[132,16,128]{2,1,0:T(8,128)(2,1)} %copy-done.11) | copy-start | bytes 1622020
  38.9 8.6 %copy-start.17 = (bf16[132,16,128]{2,1,0:T(8,128)(2,1)S(1)}, bf16[132,16,128]{2,1,0:T(8,128)(2,1)}, u32[]{:S(2)}) copy-start(bf16[132,16,128]{2,1,0:T(8,128)(2,1)} %copy-done.16) | copy-start | bytes 1622020
  39.9 30.4 %collective-permute-start.12 = (bf16[192,16,128]{2,1,0:T(8,128)(2,1)}, bf16[192,16,128]{2,1,0:T(8,128)(2,1)S(1)}, u32[]{:S(2)}, u32[]{:S(2)}) collective-permute-start(bf16[192,16,128]{2,1,0:T(8,128)(2,1)} %join.6.refs_0_), channel_id=1, source_target_pairs={{4,12},{6,14},{12,20},{14,22},{20,28},{22,30},{8,0},{10,2},{16,8},... | collective-permute-start | bytes 2359304 | tf_op jit(solution)/shard_map/ppermute | solution.py:425
  47.5 1.0 copy-start.14
  48.5 13.8 %copy-start.15 = (bf16[132,16,128]{2,1,0:T(8,128)(2,1)S(1)}, bf16[132,16,128]{2,1,0:T(8,128)(2,1)}, u32[]{:S(2)}) copy-start(bf16[132,16,128]{2,1,0:T(8,128)(2,1)} %copy-done.13) | copy-start | bytes 1622020
  54.4 15.9 %copy-start.18 = (f32[8,16,128]{2,1,0:T(8,128)}, f32[8,16,128]{2,1,0:T(8,128)S(1)}, u32[]{:S(2)}) copy-start(f32[8,16,128]{2,1,0:T(8,128)S(1)} %get-tuple-element.47.refs_8_.refs_6_) | copy-start | bytes 196612
  57.8 19.4 %collective-permute-start.8 = (bf16[192,16,128]{2,1,0:T(8,128)(2,1)}, bf16[192,16,128]{2,1,0:T(8,128)(2,1)}, u32[]{:S(2)}, u32[]{:S(2)}) collective-permute-start(bf16[192,16,128]{2,1,0:T(8,128)(2,1)} %join.5.refs_0_), channel_id=1, source_target_pairs={{0,4},{2,6},{4,0},{6,2},{8,12},{10,14},{12,8},{14,10},{16,20},{18,... | collective-permute-start | bytes 2359304 | tf_op jit(solution)/shard_map/ppermute | solution.py:417
  58.0 19.2 %collective-permute-start.15 = (bf16[192,16,128]{2,1,0:T(8,128)(2,1)}, bf16[192,16,128]{2,1,0:T(8,128)(2,1)S(1)}, u32[]{:S(2)}, u32[]{:S(2)}) collective-permute-start(bf16[192,16,128]{2,1,0:T(8,128)(2,1)} %collective-permute-done.5.refs_1_), channel_id=1, source_target_pairs={{0,8},{2,10},{8,16},{10,18},{16,24},{18,26},{12,4},{14,6},{20,12},... | collective-permute-start | bytes 2359304 | tf_op jit(solution)/shard_map/ppermute | solution.py:426
  60.8 25.0 %collective-permute-start.10 = (bf16[64,8192]{1,0:T(8,128)(2,1)S(1)}, bf16[64,8192]{1,0:T(8,128)(2,1)S(1)}, u32[]{:S(2)}, u32[]{:S(2)}) collective-permute-start(bf16[64,8192]{1,0:T(8,128)(2,1)S(1)} %get-tuple-element.44.refs_0_.refs_4_.refs_2_), channel_id=1, source_target_pairs={{0,1},{1,0},{2,3},{3,2},{4,5},{5,4},{6,7},{7,6},{8,9},{9,8},{10,11... | collective-permute-start | bytes 3145736 | tf_op jit(solution)/shard_map/ppermute | solution.py:420
  62.3 1.2 copy-start.3
  70.3 0.9 copy-start.7
  71.2 23.2 %collective-permute-start.13 = (bf16[192,16,128]{2,1,0:T(8,128)(2,1)}, bf16[192,16,128]{2,1,0:T(8,128)(2,1)}, u32[]{:S(2)}, u32[]{:S(2)}) collective-permute-start(bf16[192,16,128]{2,1,0:T(8,128)(2,1)} %join.5.refs_0_), channel_id=1, source_target_pairs={{4,12},{6,14},{12,20},{14,22},{20,28},{22,30},{8,0},{10,2},{16,8},... | collective-permute-start | bytes 2359304 | tf_op jit(solution)/shard_map/ppermute | solution.py:425
  77.3 0.9 copy-start.9
  78.2 19.9 %collective-permute-start.16 = (bf16[192,16,128]{2,1,0:T(8,128)(2,1)}, bf16[192,16,128]{2,1,0:T(8,128)(2,1)}, u32[]{:S(2)}, u32[]{:S(2)}) collective-permute-start(bf16[192,16,128]{2,1,0:T(8,128)(2,1)} %collective-permute-done.8.refs_1_), channel_id=1, source_target_pairs={{0,8},{2,10},{8,16},{10,18},{16,24},{18,26},{12,4},{14,6},{20,12},... | collective-permute-start | bytes 2359304 | tf_op jit(solution)/shard_map/ppermute | solution.py:426
  83.4 2.5 %copy-start.8 = (bf16[192,16,128]{2,1,0:T(8,128)(2,1)S(1)}, bf16[192,16,128]{2,1,0:T(8,128)(2,1)}, u32[]{:S(2)}) copy-start(bf16[192,16,128]{2,1,0:T(8,128)(2,1)} %copy-done.7) | copy-start | bytes 2359300
  83.4 2.5 %copy-start.10 = (bf16[192,16,128]{2,1,0:T(8,128)(2,1)S(1)}, bf16[192,16,128]{2,1,0:T(8,128)(2,1)}, u32[]{:S(2)}) copy-start(bf16[192,16,128]{2,1,0:T(8,128)(2,1)} %copy-done.9) | copy-start | bytes 2359300
  83.4 2.5 %copy-start.19 = (f32[8,16,128]{2,1,0:T(8,128)S(1)}, f32[8,16,128]{2,1,0:T(8,128)}, u32[]{:S(2)}) copy-start(f32[8,16,128]{2,1,0:T(8,128)} %copy-done.18) | copy-start | bytes 196612
  84.2 12.2 %collective-permute-start.9 = (bf16[128,16,128]{2,1,0:T(8,128)(2,1)}, bf16[128,16,128]{2,1,0:T(8,128)(2,1)}, u32[]{:S(2)}, u32[]{:S(2)}) collective-permute-start(bf16[128,16,128]{2,1,0:T(8,128)(2,1)} %join.4.refs_0_), channel_id=1, source_target_pairs={{0,4},{2,6},{4,0},{6,2},{8,12},{10,14},{12,8},{14,10},{16,20},{18,... | collective-permute-start | bytes 1572872 | tf_op jit(solution)/shard_map/ppermute | solution.py:417
  84.3 28.1 %collective-permute-start.11 = (bf16[64,8192]{1,0:T(8,128)(2,1)}, bf16[64,8192]{1,0:T(8,128)(2,1)S(1)}, u32[]{:S(2)}, u32[]{:S(2)}) collective-permute-start(bf16[64,8192]{1,0:T(8,128)(2,1)} %direct_sweeps.3.refs_1_.refs_5_.refs_3_), channel_id=1, source_target_pairs={{0,1},{1,0},{2,3},{3,2},{4,5},{5,4},{6,7},{7,6},{8,9},{9,8},{10,11... | collective-permute-start | bytes 3145736 | tf_op jit(solution)/shard_map/ppermute | solution.py:420
  94.3 28.0 %collective-permute-start.19 = (bf16[96,8192]{1,0:T(8,128)(2,1)}, bf16[96,8192]{1,0:T(8,128)(2,1)}, u32[]{:S(2)}, u32[]{:S(2)}) collective-permute-start(bf16[96,8192]{1,0:T(8,128)(2,1)} %adjoint_sweeps.4.refs_0_), channel_id=1, source_target_pairs={{0,2},{2,0},{4,6},{6,4},{8,10},{10,8},{12,14},{14,12},{16,18},{18,... | collective-permute-start | bytes 4718600 | tf_op jit(solution)/shard_map/ppermute | solution.py:417
  94.3 19.9 %collective-permute-start.14 = (bf16[128,16,128]{2,1,0:T(8,128)(2,1)}, bf16[128,16,128]{2,1,0:T(8,128)(2,1)}, u32[]{:S(2)}, u32[]{:S(2)}) collective-permute-start(bf16[128,16,128]{2,1,0:T(8,128)(2,1)} %join.4.refs_0_), channel_id=1, source_target_pairs={{4,12},{6,14},{12,20},{14,22},{20,28},{22,30},{8,0},{10,2},{16,8},... | collective-permute-start | bytes 1572872 | tf_op jit(solution)/shard_map/ppermute | solution.py:425
  98.0 16.2 %collective-permute-start.17 = (bf16[128,16,128]{2,1,0:T(8,128)(2,1)}, bf16[128,16,128]{2,1,0:T(8,128)(2,1)}, u32[]{:S(2)}, u32[]{:S(2)}) collective-permute-start(bf16[128,16,128]{2,1,0:T(8,128)(2,1)} %collective-permute-done.9.refs_1_), channel_id=1, source_target_pairs={{0,8},{2,10},{8,16},{10,18},{16,24},{18,26},{12,4},{14,6},{20,12},... | collective-permute-start | bytes 1572872 | tf_op jit(solution)/shard_map/ppermute | solution.py:426
  103.3 9.0 %copy-start.23 = (f32[64]{0:T(128)S(1)}, f32[64]{0:T(128)}, u32[]{:S(2)}) copy-start(f32[64]{0:T(128)} %param.17) | copy-start | bytes 772
  103.3 9.1 %copy-start.5 = (f32[1024,64]{0,1:T(8,128)S(1)}, f32[1024,64]{0,1:T(8,128)}, u32[]{:S(2)}) copy-start(f32[1024,64]{0,1:T(8,128)} %param.16) | copy-start | bytes 786436
  112.2 10.2 %collective-permute-start.20 = (bf16[96,8192]{1,0:T(8,128)(2,1)}, bf16[96,8192]{1,0:T(8,128)(2,1)}, u32[]{:S(2)}, u32[]{:S(2)}) collective-permute-start(bf16[96,8192]{1,0:T(8,128)(2,1)} %adjoint_sweeps.5.refs_1_), channel_id=1, source_target_pairs={{0,2},{2,0},{4,6},{6,4},{8,10},{10,8},{12,14},{14,12},{16,18},{18,... | collective-permute-start | bytes 4718600 | tf_op jit(solution)/shard_map/ppermute | solution.py:417
  112.4 2.0 %copy-start.20 = (f32[8,16,128]{2,1,0:T(8,128)S(1)}, f32[8,16,128]{2,1,0:T(8,128)}, u32[]{:S(2)}) copy-start(f32[8,16,128]{2,1,0:T(8,128)} %copy-done.18) | copy-start | bytes 196612
  114.3 8.0 %copy-start.4 = (f32[1024,64]{0,1:T(8,128)S(1)}, f32[1024,64]{0,1:T(8,128)}, u32[]{:S(2)}) copy-start(f32[1024,64]{0,1:T(8,128)} %param.15) | copy-start | bytes 786436
  119.8 8.1 %collective-permute-start.18 = (bf16[64,8192]{1,0:T(8,128)(2,1)S(1)}, bf16[64,8192]{1,0:T(8,128)(2,1)S(1)}, u32[]{:S(2)}, u32[]{:S(2)}) collective-permute-start(bf16[64,8192]{1,0:T(8,128)(2,1)S(1)} %adjoint_sweeps.3.refs_0_), channel_id=1, source_target_pairs={{0,2},{2,0},{4,6},{6,4},{8,10},{10,8},{12,14},{14,12},{16,18},{18,... | collective-permute-start | bytes 3145736 | tf_op jit(solution)/shard_map/ppermute | solution.py:417
  120.4 13.9 %collective-permute-start.24 = (bf16[64,1024]{1,0:T(8,128)(2,1)S(1)}, bf16[64,1024]{1,0:T(8,128)(2,1)S(1)}, u32[]{:S(2)}, u32[]{:S(2)}) collective-permute-start(bf16[64,1024]{1,0:T(8,128)(2,1)S(1)} %get-tuple-element.62), channel_id=1, source_target_pairs={{0,2},{2,0},{4,6},{6,4},{8,10},{10,8},{12,14},{14,12},{16,18},{18,... | collective-permute-start | bytes 393224 | tf_op jit(solution)/shard_map/ppermute | solution.py:417
  120.4 16.1 %collective-permute-start.25 = (bf16[64,1024]{1,0:T(8,128)(2,1)S(1)}, bf16[64,1024]{1,0:T(8,128)(2,1)S(1)}, u32[]{:S(2)}, u32[]{:S(2)}) collective-permute-start(bf16[64,1024]{1,0:T(8,128)(2,1)S(1)} %get-tuple-element.63), channel_id=1, source_target_pairs={{0,4},{2,6},{4,0},{6,2},{8,12},{10,14},{12,8},{14,10},{16,20},{18,... | collective-permute-start | bytes 393224 | tf_op jit(solution)/shard_map/ppermute | solution.py:417
  122.3 14.2 %collective-permute-start.26 = (bf16[64,1024]{1,0:T(8,128)(2,1)S(1)}, bf16[64,1024]{1,0:T(8,128)(2,1)S(1)}, u32[]{:S(2)}, u32[]{:S(2)}) collective-permute-start(bf16[64,1024]{1,0:T(8,128)(2,1)S(1)} %get-tuple-element.64), channel_id=1, source_target_pairs={{0,6},{2,4},{4,2},{6,0},{8,14},{10,12},{12,10},{14,8},{16,22},{18,... | collective-permute-start | bytes 393224 | tf_op jit(solution)/shard_map/ppermute | solution.py:417
  130.6 8.3 %collective-permute-start.21 = (bf16[64,512]{1,0:T(8,128)(2,1)S(1)}, bf16[64,512]{1,0:T(8,128)(2,1)S(1)}, u32[]{:S(2)}, u32[]{:S(2)}) collective-permute-start(bf16[64,512]{1,0:T(8,128)(2,1)S(1)} %get-tuple-element.59), channel_id=1, source_target_pairs={{0,8},{2,10},{4,12},{6,14},{8,16},{10,18},{12,20},{14,22},{16,24},... | collective-permute-start | bytes 196616 | tf_op jit(solution)/shard_map/ppermute | solution.py:506
  132.2 7.3 %collective-permute-start.22 = (bf16[64,512]{1,0:T(8,128)(2,1)S(1)}, bf16[64,512]{1,0:T(8,128)(2,1)S(1)}, u32[]{:S(2)}, u32[]{:S(2)}) collective-permute-start(bf16[64,512]{1,0:T(8,128)(2,1)S(1)} %get-tuple-element.60), channel_id=1, source_target_pairs={{0,16},{2,18},{4,20},{6,22},{8,24},{10,26},{12,28},{14,30},{16,0},... | collective-permute-start | bytes 196616 | tf_op jit(solution)/shard_map/ppermute | solution.py:506
  134.3 5.3 %collective-permute-start.23 = (bf16[64,512]{1,0:T(8,128)(2,1)S(1)}, bf16[64,512]{1,0:T(8,128)(2,1)S(1)}, u32[]{:S(2)}, u32[]{:S(2)}) collective-permute-start(bf16[64,512]{1,0:T(8,128)(2,1)S(1)} %get-tuple-element.61), channel_id=1, source_target_pairs={{0,24},{2,26},{4,28},{6,30},{8,0},{10,2},{12,4},{14,6},{16,8},{18,... | collective-permute-start | bytes 196616 | tf_op jit(solution)/shard_map/ppermute | solution.py:506
  137.4 5.0 %collective-permute-start.27 = (bf16[64,1024]{1,0:T(8,128)(2,1)S(1)}, bf16[64,1024]{1,0:T(8,128)(2,1)S(1)}, u32[]{:S(2)}, u32[]{:S(2)}) collective-permute-start(bf16[64,1024]{1,0:T(8,128)(2,1)S(1)} %bitcast.43), channel_id=1, source_target_pairs={{0,1},{1,0},{2,3},{3,2},{4,5},{5,4},{6,7},{7,6},{8,9},{9,8},{10,11... | collective-permute-start | bytes 393224 | tf_op jit(solution)/shard_map/ppermute | solution.py:420
